TPU v7x, 128 devices: a whole 4x4x4 slice. The times are simulated.
128 devices in a mesh: dp: 128 (over x, z, y, core).
Axes of the slice: x: 4, y: 4, z: 4, core: 2. Of those that a mesh axis runs over, the one named last changes fastest.
Arguments:
- gradients: bfloat16 [128, 8192, 256], P('dp'), may hold values from -6 to 6
- error_memory: float32 [128, 8192, 256], P('dp'), may hold values from -4 to 4
- block_lists: int32 [128, 8, 1024], P('dp'), may hold values from 0 to 8191, as said below
- master: float32 [8192, 256], P('dp'), may hold values from -0.18 to 0.18
- first_moment: float32 [8192, 256], P('dp'), may hold values from -24 to 24
- second_moment: float32 [8192, 256], P('dp'), may hold values from 1 to 4
Outputs:
- new_errors: float32 [128, 8192, 256], P('dp')
- new_master: float32 [8192, 256], P('dp')
- new_first: float32 [8192, 256], P('dp')
- new_second: float32 [8192, 256], P('dp')
- weights: bfloat16 [8192, 256], replicated
Inputs may be any that keep to these rules, and one draw needn't show every extreme that they name: block_lists[d, 0] names the 1024 distinct blocks that replica d sends; for r >= 1, block_lists[d, r] names 1024 distinct blocks, the same set for all replicas whose indices agree with d above the lowest r bits; block_lists[d, 7] is the same on every replica.
All inputs are finite; a program needn't handle non-finite values.
Results may differ from a plain program's by a relative error of at most 0.0014.
Values may be sent and summed in bfloat16 or wider, within the bound.
A program may use at most 128 MiB of HBM per device.

v0:
```python
import jax
import jax.numpy as jnp
from jax import lax
from jax.sharding import PartitionSpec as P

first_bias = 0.9999734386011124
second_bias = 0.09520785288629036


def partner_2(block, axis, apart):
    count = lax.axis_size(axis)
    route = []
    for low in range(count):
        high = low | 1 << apart
        if high != low and high < count:
            route += [(low, high), (high, low)]
    return lax.ppermute(block, axis, route)


def membership(indices, count):
    return jnp.zeros((count,), jnp.float32).at[indices].set(1.0)


def align(target, source, values):
    hits = (target[:, None] == source[None, :]).astype(jnp.float32)
    return jnp.dot(
        hits, values, precision=lax.Precision.HIGHEST, preferred_element_type=jnp.float32
    )


def body(gradients, error_memory, block_lists, master, first_moment, second_moment):
    compressed = gradients[0].astype(jnp.float32) + error_memory[0]
    chain = block_lists[0]
    levels = chain.shape[0]
    block_count = compressed.shape[0]
    owned_count = master.shape[0]
    sent_mask = membership(chain[0], block_count)
    new_errors = (compressed * (1.0 - sent_mask)[:, None])[None]
    root_list = chain[levels - 1]
    owned_ids = lax.axis_index("dp") * owned_count + jnp.arange(owned_count, dtype=jnp.int32)
    held = jnp.take(compressed, chain[0], axis=0)
    held_list = chain[0]
    for level in range(1, levels):
        parent = chain[level]
        aligned = align(parent, held_list, held)
        partner = partner_2(aligned.astype(jnp.bfloat16), "dp", level - 1).astype(aligned.dtype)
        held = aligned + partner
        held_list = parent
    owned_grad = align(owned_ids, root_list, held)
    new_first = 0.9 * first_moment + 0.1 * owned_grad
    new_second = 0.999 * second_moment + 0.001 * owned_grad * owned_grad
    first_hat = new_first / first_bias
    second_hat = new_second / second_bias
    new_master = master - 0.001 * (first_hat / (jnp.sqrt(second_hat) + 1e-08) + 0.1 * master)
    weights = lax.all_gather(new_master.astype(jnp.bfloat16), "dp", axis=0, tiled=True)
    return (new_errors, new_master, new_first, new_second, weights)


def solution(mesh):
    in_specs = (
        P("dp", None, None),
        P("dp", None, None),
        P("dp", None, None),
        P("dp", None),
        P("dp", None),
        P("dp", None),
    )
    out_specs = (P("dp", None, None), P("dp", None), P("dp", None), P("dp", None), P())
    return jax.shard_map(body, mesh=mesh, in_specs=in_specs, out_specs=out_specs, check_vma=False)
```

profile of v0, /device:TPU:1, one launch (start us, length us, event | category | flops | bytes accessed | tf_op | source)
XLA Modules:
  0.0 205.6 jit_solution(12644822961878629838)
XLA Ops:
  7.2 0.0 all-gather.2.cloned.1.call-start
  7.2 0.8 compare_select_fusion
  8.0 1.1 fusion.57
  9.1 4.3 %scatter_custom_fusion = f32[8192]{0:T(1024)S(1)} fusion(s32[1024]{0:T(1024)S(1)} %bitcast.18, f32[1024]{0:T(1024)S(1)} %broadcast.41, f32[]{:T(128)} %constant.16.clone.1), kind=kCustom, calls=%fused_computation.59 | custom fusion | bytes 32772 | tf_op jit(solution)/shard_map/scatter | solution.py:21
  13.5 9.4 %fusion = (f32[8192,256]{1,0:T(8,128)}, f32[1,8192,256]{2,1,0:T(8,128)}) fusion(f32[1,8192,256]{2,1,0:T(8,128)} %param.7, bf16[1,8192,256]{2,1,0:T(8,128)(2,1)} %param.6, f32[8192]{0:T(1024)S(1)} %broadcast_subtract_fusion), kind=kLoop, calls=%fused_computation.3 | loop fusion | flops 6291456 | bytes 29392896 | tf_op jit(solution)/shard_map/add | solution.py:32
  22.9 6.8 %gather_fusion = f32[1024,256]{1,0:T(8,128)S(1)} fusion(f32[8192,256]{1,0:T(8,128)} %get-tuple-element.9, s32[1024]{0:T(1024)S(1)} %broadcast_clamp_fusion), kind=kCustom, calls=%fused_computation | custom fusion | bytes 2101248 | tf_op jit(solution)/shard_map/jit(_take)/gather | solution.py:41
  29.7 2.2 %fusion.58 = (bf16[1024,256]{1,0:T(8,128)(2,1)S(1)}, f32[1024,256]{1,0:T(8,128)S(1)}) fusion(f32[1024,256]{1,0:T(8,128)S(1)} %gather_fusion, pred[1024]{0:T(1024)(128)(4,1)S(1)} %compare_and_fusion, s32[1024]{0:T(1024)S(1)} %bitcast.16, s32[1024]{0:T(1024)S(1)} %bitcast.29), kind=kOutput, calls=%fused_computation.69 | convolution fusion | flops 3222798336 | bytes 2630656 | tf_op jit(solution)/shard_map/dot_general | solution.py:26
  31.9 1.5 collective-permute-start
  33.4 1.5 collective-permute-done
  35.0 2.1 %fusion.59 = (bf16[1024,256]{1,0:T(8,128)(2,1)S(1)}, f32[1024,256]{1,0:T(8,128)S(1)}) fusion(f32[1024,256]{1,0:T(8,128)S(1)} %get-tuple-element.20, bf16[1024,256]{1,0:T(8,128)(2,1)S(1)} %collective-permute-done, s32[1024]{0:T(1024)S(1)} %bitcast.30, s32[1024]{0:T(1024)S(1)} %bitcast.27), kind=kOutput, calls=%fused_computation.70 | convolution fusion | flops 3223060480 | bytes 3153920 | tf_op jit(solution)/shard_map/dot_general | solution.py:26
  37.1 1.5 collective-permute-start.1
  38.5 11.8 %collective-permute-done.1 = bf16[1024,256]{1,0:T(8,128)(2,1)S(1)} collective-permute-done((bf16[1024,256]{1,0:T(8,128)(2,1)S(1)}, bf16[1024,256]{1,0:T(8,128)(2,1)S(1)}, u32[]{:S(2)}, u32[]{:S(2)}) %collective-permute-start.1) | collective-permute-done | bytes 524320 | tf_op jit(solution)/shard_map/ppermute | solution.py:17
  50.3 2.1 %fusion.60 = (bf16[1024,256]{1,0:T(8,128)(2,1)S(1)}, f32[1024,256]{1,0:T(8,128)S(1)}) fusion(f32[1024,256]{1,0:T(8,128)S(1)} %get-tuple-element.22, bf16[1024,256]{1,0:T(8,128)(2,1)S(1)} %collective-permute-done.1, s32[1024]{0:T(1024)S(1)} %bitcast.28, s32[1024]{0:T(1024)S(1)} %bitcast.25), kind=kOutput, calls=%fused_computation.71 | convolution fusion | flops 3223060480 | bytes 3153920 | tf_op jit(solution)/shard_map/dot_general | solution.py:26
  52.4 3.1 %collective-permute-start.2 = (bf16[1024,256]{1,0:T(8,128)(2,1)S(1)}, bf16[1024,256]{1,0:T(8,128)(2,1)S(1)}, u32[]{:S(2)}, u32[]{:S(2)}) collective-permute-start(bf16[1024,256]{1,0:T(8,128)(2,1)S(1)} %get-tuple-element.23), channel_id=1, source_target_pairs={{0,4},{4,0},{1,5},{5,1},{2,6},{6,2},{3,7},{7,3},{8,12},{12,8},{9,1... | collective-permute-start | bytes 1572872 | tf_op jit(solution)/shard_map/ppermute | solution.py:17
  55.5 10.8 %collective-permute-done.2 = bf16[1024,256]{1,0:T(8,128)(2,1)S(1)} collective-permute-done((bf16[1024,256]{1,0:T(8,128)(2,1)S(1)}, bf16[1024,256]{1,0:T(8,128)(2,1)S(1)}, u32[]{:S(2)}, u32[]{:S(2)}) %collective-permute-start.2) | collective-permute-done | bytes 524320 | tf_op jit(solution)/shard_map/ppermute | solution.py:17
  66.3 2.1 %fusion.61 = (bf16[1024,256]{1,0:T(8,128)(2,1)S(1)}, f32[1024,256]{1,0:T(8,128)S(1)}) fusion(f32[1024,256]{1,0:T(8,128)S(1)} %get-tuple-element.24, bf16[1024,256]{1,0:T(8,128)(2,1)S(1)} %collective-permute-done.2, s32[1024]{0:T(1024)S(1)} %bitcast.26, s32[1024]{0:T(1024)S(1)} %bitcast.23), kind=kOutput, calls=%fused_computation.72 | convolution fusion | flops 3223060480 | bytes 3153920 | tf_op jit(solution)/shard_map/dot_general | solution.py:26
  68.4 1.9 collective-permute-start.3
  70.3 10.1 %collective-permute-done.3 = bf16[1024,256]{1,0:T(8,128)(2,1)S(1)} collective-permute-done((bf16[1024,256]{1,0:T(8,128)(2,1)S(1)}, bf16[1024,256]{1,0:T(8,128)(2,1)S(1)}, u32[]{:S(2)}, u32[]{:S(2)}) %collective-permute-start.3) | collective-permute-done | bytes 524320 | tf_op jit(solution)/shard_map/ppermute | solution.py:17
  80.4 2.1 %fusion.62 = (bf16[1024,256]{1,0:T(8,128)(2,1)S(1)}, f32[1024,256]{1,0:T(8,128)S(1)}) fusion(f32[1024,256]{1,0:T(8,128)S(1)} %get-tuple-element.26, bf16[1024,256]{1,0:T(8,128)(2,1)S(1)} %collective-permute-done.3, s32[1024]{0:T(1024)S(1)} %bitcast.24, s32[1024]{0:T(1024)S(1)} %bitcast.21), kind=kOutput, calls=%fused_computation.73 | convolution fusion | flops 3223060480 | bytes 3153920 | tf_op jit(solution)/shard_map/dot_general | solution.py:26
  82.5 0.0 copy-start.1
  82.6 3.3 %collective-permute-start.4 = (bf16[1024,256]{1,0:T(8,128)(2,1)S(1)}, bf16[1024,256]{1,0:T(8,128)(2,1)S(1)}, u32[]{:S(2)}, u32[]{:S(2)}) collective-permute-start(bf16[1024,256]{1,0:T(8,128)(2,1)S(1)} %get-tuple-element.27), channel_id=1, source_target_pairs={{0,16},{16,0},{1,17},{17,1},{2,18},{18,2},{3,19},{19,3},{4,20},{20... | collective-permute-start | bytes 1572872 | tf_op jit(solution)/shard_map/ppermute | solution.py:17
  85.8 9.2 %collective-permute-done.4 = bf16[1024,256]{1,0:T(8,128)(2,1)S(1)} collective-permute-done((bf16[1024,256]{1,0:T(8,128)(2,1)S(1)}, bf16[1024,256]{1,0:T(8,128)(2,1)S(1)}, u32[]{:S(2)}, u32[]{:S(2)}) %collective-permute-start.4) | collective-permute-done | bytes 524320 | tf_op jit(solution)/shard_map/ppermute | solution.py:17
  95.0 2.1 %fusion.63 = (bf16[1024,256]{1,0:T(8,128)(2,1)S(1)}, f32[1024,256]{1,0:T(8,128)S(1)}) fusion(f32[1024,256]{1,0:T(8,128)S(1)} %get-tuple-element.28, bf16[1024,256]{1,0:T(8,128)(2,1)S(1)} %collective-permute-done.4, s32[1024]{0:T(1024)S(1)} %bitcast.22, s32[1024]{0:T(1024)S(1)} %bitcast.19), kind=kOutput, calls=%fused_computation.74 | convolution fusion | flops 3223060480 | bytes 3153920 | tf_op jit(solution)/shard_map/dot_general | solution.py:26
  97.2 1.2 collective-permute-start.5
  98.4 8.6 %collective-permute-done.5 = bf16[1024,256]{1,0:T(8,128)(2,1)S(1)} collective-permute-done((bf16[1024,256]{1,0:T(8,128)(2,1)S(1)}, bf16[1024,256]{1,0:T(8,128)(2,1)S(1)}, u32[]{:S(2)}, u32[]{:S(2)}) %collective-permute-start.5) | collective-permute-done | bytes 524320 | tf_op jit(solution)/shard_map/ppermute | solution.py:17
  107.0 2.1 %fusion.64 = (bf16[1024,256]{1,0:T(8,128)(2,1)S(1)}, f32[1024,256]{1,0:T(8,128)S(1)}) fusion(f32[1024,256]{1,0:T(8,128)S(1)} %get-tuple-element.30, bf16[1024,256]{1,0:T(8,128)(2,1)S(1)} %collective-permute-done.5, s32[1024]{0:T(1024)S(1)} %bitcast.20, s32[1024]{0:T(1024)S(1)} %bitcast.13), kind=kOutput, calls=%fused_computation.75 | convolution fusion | flops 3223060480 | bytes 3153920 | tf_op jit(solution)/shard_map/dot_general | solution.py:26
  109.1 2.8 %collective-permute-start.6 = (bf16[1024,256]{1,0:T(8,128)(2,1)S(1)}, bf16[1024,256]{1,0:T(8,128)(2,1)S(1)}, u32[]{:S(2)}, u32[]{:S(2)}) collective-permute-start(bf16[1024,256]{1,0:T(8,128)(2,1)S(1)} %get-tuple-element.31), channel_id=1, source_target_pairs={{0,64},{64,0},{1,65},{65,1},{2,66},{66,2},{3,67},{67,3},{4,68},{68... | collective-permute-start | bytes 1572872 | tf_op jit(solution)/shard_map/ppermute | solution.py:17
  111.9 7.6 %collective-permute-done.6 = bf16[1024,256]{1,0:T(8,128)(2,1)S(1)} collective-permute-done((bf16[1024,256]{1,0:T(8,128)(2,1)S(1)}, bf16[1024,256]{1,0:T(8,128)(2,1)S(1)}, u32[]{:S(2)}, u32[]{:S(2)}) %collective-permute-start.6) | collective-permute-done | bytes 524320 | tf_op jit(solution)/shard_map/ppermute | solution.py:17
  119.5 1.3 fusion.55
  120.8 0.0 all-gather.2.cloned.1.call-update
  120.8 73.5 %all-gather.2.cloned.1.call-done = bf16[8192,256]{1,0:T(8,128)(2,1)} async-done(((bf16[64,256]{1,0:T(8,128)(2,1)}), bf16[8192,256]{1,0:T(8,128)(2,1)}) %all-gather.2.cloned.1.call-update) | async-done | bytes 4194320 | tf_op jit(solution)/shard_map/all_gather | solution.py:55
  194.3 4.5 %copy.12 = bf16[8192,256]{1,0:T(8,128)(2,1)} copy(bf16[8192,256]{1,0:T(8,128)(2,1)} %all-gather.2.cloned.1.call-done) | data formatting | bytes 8388608
  (10 shorter events, 0.0 us)
Async XLA Ops:
  7.2 187.2 %all-gather.2.cloned.1.call-start = ((), (), s32[]{:S(2)}) async-start(), calls=%async_computation | async-start | bytes 4227072 | tf_op jit(solution)/shard_map/all_gather | solution.py:55
  31.9 3.0 %collective-permute-start = (bf16[1024,256]{1,0:T(8,128)(2,1)S(1)}, bf16[1024,256]{1,0:T(8,128)(2,1)S(1)}, u32[]{:S(2)}, u32[]{:S(2)}) collective-permute-start(bf16[1024,256]{1,0:T(8,128)(2,1)S(1)} %get-tuple-element.19), channel_id=1, source_target_pairs={{0,1},{1,0},{2,3},{3,2},{4,5},{5,4},{6,7},{7,6},{8,9},{9,8},{10,11... | collective-permute-start | bytes 1572872 | tf_op jit(solution)/shard_map/ppermute | solution.py:17
  37.1 13.2 %collective-permute-start.1 = (bf16[1024,256]{1,0:T(8,128)(2,1)S(1)}, bf16[1024,256]{1,0:T(8,128)(2,1)S(1)}, u32[]{:S(2)}, u32[]{:S(2)}) collective-permute-start(bf16[1024,256]{1,0:T(8,128)(2,1)S(1)} %get-tuple-element.21), channel_id=1, source_target_pairs={{0,2},{2,0},{1,3},{3,1},{4,6},{6,4},{5,7},{7,5},{8,10},{10,8},{9,1... | collective-permute-start | bytes 1572872 | tf_op jit(solution)/shard_map/ppermute | solution.py:17
  52.4 13.9 %collective-permute-start.2 = (bf16[1024,256]{1,0:T(8,128)(2,1)S(1)}, bf16[1024,256]{1,0:T(8,128)(2,1)S(1)}, u32[]{:S(2)}, u32[]{:S(2)}) collective-permute-start(bf16[1024,256]{1,0:T(8,128)(2,1)S(1)} %get-tuple-element.23), channel_id=1, source_target_pairs={{0,4},{4,0},{1,5},{5,1},{2,6},{6,2},{3,7},{7,3},{8,12},{12,8},{9,1... | collective-permute-start | bytes 1572872 | tf_op jit(solution)/shard_map/ppermute | solution.py:17
  68.4 12.0 %collective-permute-start.3 = (bf16[1024,256]{1,0:T(8,128)(2,1)S(1)}, bf16[1024,256]{1,0:T(8,128)(2,1)S(1)}, u32[]{:S(2)}, u32[]{:S(2)}) collective-permute-start(bf16[1024,256]{1,0:T(8,128)(2,1)S(1)} %get-tuple-element.25), channel_id=1, source_target_pairs={{0,8},{8,0},{1,9},{9,1},{2,10},{10,2},{3,11},{11,3},{4,12},{12,4},... | collective-permute-start | bytes 1572872 | tf_op jit(solution)/shard_map/ppermute | solution.py:17
  82.5 37.0 %copy-start = (f32[64,256]{1,0:T(8,128)S(1)}, f32[64,256]{1,0:T(8,128)}, u32[]{:S(2)}) copy-start(f32[64,256]{1,0:T(8,128)} %param.9) | copy-start | bytes 196612
  82.5 37.0 %copy-start.1 = (f32[64,256]{1,0:T(8,128)S(1)}, f32[64,256]{1,0:T(8,128)}, u32[]{:S(2)}) copy-start(f32[64,256]{1,0:T(8,128)} %param.10) | copy-start | bytes 196612
  82.5 36.9 %copy-start.2 = (f32[64,256]{1,0:T(8,128)S(1)}, f32[64,256]{1,0:T(8,128)}, u32[]{:S(2)}) copy-start(f32[64,256]{1,0:T(8,128)} %param.11) | copy-start | bytes 196612
  82.6 12.5 %collective-permute-start.4 = (bf16[1024,256]{1,0:T(8,128)(2,1)S(1)}, bf16[1024,256]{1,0:T(8,128)(2,1)S(1)}, u32[]{:S(2)}, u32[]{:S(2)}) collective-permute-start(bf16[1024,256]{1,0:T(8,128)(2,1)S(1)} %get-tuple-element.27), channel_id=1, source_target_pairs={{0,16},{16,0},{1,17},{17,1},{2,18},{18,2},{3,19},{19,3},{4,20},{20... | collective-permute-start | bytes 1572872 | tf_op jit(solution)/shard_map/ppermute | solution.py:17
  97.2 9.8 %collective-permute-start.5 = (bf16[1024,256]{1,0:T(8,128)(2,1)S(1)}, bf16[1024,256]{1,0:T(8,128)(2,1)S(1)}, u32[]{:S(2)}, u32[]{:S(2)}) collective-permute-start(bf16[1024,256]{1,0:T(8,128)(2,1)S(1)} %get-tuple-element.29), channel_id=1, source_target_pairs={{0,32},{32,0},{1,33},{33,1},{2,34},{34,2},{3,35},{35,3},{4,36},{36... | collective-permute-start | bytes 1572872 | tf_op jit(solution)/shard_map/ppermute | solution.py:17
  109.1 10.4 %collective-permute-start.6 = (bf16[1024,256]{1,0:T(8,128)(2,1)S(1)}, bf16[1024,256]{1,0:T(8,128)(2,1)S(1)}, u32[]{:S(2)}, u32[]{:S(2)}) collective-permute-start(bf16[1024,256]{1,0:T(8,128)(2,1)S(1)} %get-tuple-element.31), channel_id=1, source_target_pairs={{0,64},{64,0},{1,65},{65,1},{2,66},{66,2},{3,67},{67,3},{4,68},{68... | collective-permute-start | bytes 1572872 | tf_op jit(solution)/shard_map/ppermute | solution.py:17
Sparse Core Ops, SparseCore 0:
  121.0 73.3 all-gather.1
where the time goes:
time: 206 us
  waiting for transfers between devices  133 us (65%)
  local copies, waits for them, and re-layouts  16.8 us (8%)
  matrix products  16.2 us (8%)
  starting transfers between devices  15.3 us (7%)
  between operations  14.2 us (7%)
  other arithmetic  10.2 us (5%)
    all_gather x1, waiting for transfers between devices, body(): lax.all_gather(new_master.astype(jnp.bfloat16), 'dp', axis=0, tiled=True)  73.5 us
    ppermute x7, waiting for transfers between devices, partner_2(): return lax.ppermute(block, axis, route)  59.5 us
    dot_general x8, matrix products, align(): jnp.dot(hits, values, precision=lax.Precision.HIGHEST, preferred_element_...  16.2 us
    ppermute x7, starting transfers between devices, partner_2(): return lax.ppermute(block, axis, route)  15.3 us
    add x1, other arithmetic, body(): compressed = gradients[0].astype(jnp.float32) + error_memory[0]  9.42 us
    gather x1, local copies, waits for them, and re-layouts, body(): held = jnp.take(compressed, chain[0], axis=0)  6.84 us
    unnamed x7, local copies, waits for them, and re-layouts  4.49 us
    scatter x1, local copies, waits for them, and re-layouts, membership(): return jnp.zeros((count,), jnp.float32).at[indices].set(1.0)  4.35 us
  transfers between devices with their start and end apart: 8, of which 8 were waited for; matrix products, arithmetic and copies ran while one was open for 0% of the time, Pallas kernels for 0%

commit v1 on v0

v1 whole, which is shorter than its diff:
```python
import functools

import jax
import jax.numpy as jnp
from jax import lax
from jax.experimental import pallas as pl
from jax.experimental.pallas import tpu as pltpu
from jax.sharding import PartitionSpec as P

FIRST_BIAS = 0.9999734386011124
SECOND_BIAS = 0.09520785288629036
MESH = pl.DeviceIdType.MESH
F32 = jnp.float32
BF16 = jnp.bfloat16
MIB = 1 << 20

GROUP = 128
CHUNK = 512


def iota(shape, dim):
    return lax.broadcasted_iota(jnp.int32, shape, dim)


def onehot(hits):
    return jnp.where(hits, 1.0, 0.0).astype(BF16)


def adamw(master, first, second, summed):
    new_first = 0.9 * first + 0.1 * summed
    new_second = 0.999 * second + 0.001 * summed * summed
    first_hat = new_first / FIRST_BIAS
    second_hat = new_second / SECOND_BIAS
    new_master = master - 0.001 * (
        first_hat / (jnp.sqrt(second_hat) + 1e-08) + 0.1 * master
    )
    return new_master, new_first, new_second


def pack_kernel(
    grad_hbm, err_hbm, lists, out_hbm, packed, expand,
    grad, err, acc, sent, kept, starts_v, rooted, column, starts,
    grad_sem, err_sem, out_sem, starts_sem,
):
    rows = grad.shape[0]
    groups = rows // GROUP
    keep_n = lists.shape[1]
    chunks = rows // CHUNK

    def loads(i):
        span = pl.ds(i * CHUNK, CHUNK)
        return (
            pltpu.make_async_copy(grad_hbm.at[0, span], grad.at[span], grad_sem.at[i]),
            pltpu.make_async_copy(err_hbm.at[0, span], err.at[span], err_sem.at[i]),
        )

    def store(i):
        span = pl.ds(i * CHUNK, CHUNK)
        return pltpu.make_async_copy(err.at[span], out_hbm.at[0, span], out_sem.at[i])

    for i in range(chunks):
        for copy in loads(i):
            copy.start()

    acc[...] = jnp.zeros_like(acc)

    def member(r):
        ids = lists[r : r + 1, :]
        high = onehot(iota((groups, keep_n), 0) == ids // GROUP)
        low = onehot(iota((GROUP, keep_n), 0) == ids % GROUP)
        return lax.dot_general(
            high, low, (((1,), (1,)), ((), ())), preferred_element_type=F32
        )

    levels = lists.shape[0]
    first = member(0)
    sent[...] = first
    keep = first
    for r in range(1, levels - 1):
        keep = keep * member(r)
    root = member(levels - 1)
    keep = keep * root

    root_b = root.astype(BF16)
    before = onehot(iota((GROUP, GROUP), 0) < iota((GROUP, GROUP), 1))
    inside = jnp.dot(root_b, before, preferred_element_type=F32)
    total = jnp.dot(root_b, jnp.ones((GROUP, GROUP), BF16), preferred_element_type=F32)
    above = onehot(iota((groups, groups), 1) < iota((groups, groups), 0))
    start = jnp.dot(above, total.astype(BF16), preferred_element_type=F32)
    rank = (start + inside).astype(jnp.int32)
    starts_v[...] = start.astype(jnp.int32)
    to_smem = pltpu.make_async_copy(starts_v, starts, starts_sem)
    to_smem.start()
    kept[...] = jnp.where(keep > 0.5, rank, -1)
    rooted[...] = jnp.where(root > 0.5, rank, -1)

    me = lax.axis_index("dp")
    own = rooted[pl.ds(me // 2, 1), :].astype(F32)
    column[...] = jnp.transpose(jnp.broadcast_to(own, (GROUP, GROUP)))
    half = column[pl.ds((me % 2) * 64, 64), :]
    for k in range(keep_n // GROUP):
        lanes = (iota((64, GROUP), 1) + k * GROUP).astype(F32)
        expand[:, k * GROUP : (k + 1) * GROUP] = onehot(half == lanes)
    to_smem.wait()

    diagonal = iota((GROUP, GROUP), 0) == iota((GROUP, GROUP), 1)
    window = GROUP + 8

    def step(i, _):
        for copy in loads(i):
            copy.wait()
        for j in range(CHUNK // GROUP):
            g = i * (CHUNK // GROUP) + j
            span = pl.ds(pl.multiple_of(g * GROUP, GROUP), GROUP)
            value = grad[span, :].astype(F32) + err[span, :]
            stays = 1.0 - sent[pl.ds(g, 1), :]
            spread = jnp.dot(
                jnp.where(diagonal, stays, 0.0).astype(BF16),
                jnp.ones((GROUP, value.shape[1]), BF16),
                preferred_element_type=F32,
            )
            err[span, :] = value * spread
            base = pl.multiple_of((starts[g, 0] // 8) * 8, 8)
            place = kept[pl.ds(g, 1), :] - base
            hits = onehot(iota((window, GROUP), 0) == place)
            acc[pl.ds(base, window), :] += jnp.dot(
                hits, value.astype(BF16), preferred_element_type=F32
            )
        store(i).start()
        return 0

    lax.fori_loop(0, chunks, step, 0)
    for c in range(2):
        part = acc[0:keep_n, c * 128 : (c + 1) * 128].astype(BF16)
        packed[c] = part.reshape(packed.shape[1:])
    lax.fori_loop(0, chunks, lambda i, _: (store(i).wait(), 0)[1], 0)


def merge_kernel(
    packed, expand, master, first, second, weights, summed,
    from_core, part, sum1, part1, sum2, part2, got1, got2, got3, sums,
    core_send, core_recv, rs_send, rs_recv, ag_send, ag_recv,
    half_send, half_recv, w_send, w_recv, f_send, f_recv,
):
    me = lax.axis_index("dp")
    c = me % 2
    y = (me // 2) % 4
    z = (me // 8) % 4
    x = me // 32
    sibling = me + 1 - 2 * c

    def along(coord, stride, k):
        return me + ((coord + k) % 4 - coord) * stride

    def copy(src, dst, send, recv, peer):
        return pltpu.make_async_remote_copy(
            src_ref=src, dst_ref=dst, send_sem=send, recv_sem=recv,
            device_id=(peer,), device_id_type=MESH,
        )

    barrier = pltpu.get_barrier_semaphore()
    peers = [sibling]
    for coord, stride in ((x, 32), (z, 8), (y, 2)):
        peers += [along(coord, stride, k) for k in (1, 2, 3)]
    for peer in peers:
        pl.semaphore_signal(barrier, inc=1, device_id=(peer,), device_id_type=MESH)
    pl.semaphore_wait(barrier, len(peers))

    pending = []

    d = 1 - c
    a1, s1 = d * x + c * z, d * 32 + c * 8
    a2, s2 = d * z + c * y, d * 8 + c * 2
    a3, s3 = d * y + c * x, d * 2 + c * 32

    swap = copy(packed.at[d], from_core, core_send, core_recv, sibling)
    swap.start()
    swap.wait_recv()
    pending.append(swap)
    part[...] = (packed[c].astype(F32) + from_core[...].astype(F32)).astype(BF16)

    def reduce(phase, source, coord, stride, got, own):
        sends = []
        for k in (1, 2, 3):
            go = copy(
                source.at[(coord + k) % 4], got.at[k - 1],
                rs_send.at[phase, k - 1], rs_recv.at[phase, k - 1],
                along(coord, stride, k),
            )
            go.start()
            sends.append(go)
        pending.extend(sends)
        total = own
        for k in (1, 2, 3):
            sends[k - 1].wait_recv()
            total = total + got[k - 1].astype(F32)
        return total

    sum1[...] = reduce(
        0, part, a1, s1, got1, packed[c, a1].astype(F32) + from_core[a1].astype(F32)
    )
    part1[...] = sum1[...].astype(BF16)
    sum2[...] = reduce(1, part1, a2, s2, got2, sum1[a2])
    part2[...] = sum2[...].astype(BF16)
    sums[c, a1, a2, a3] = reduce(2, part2, a3, s3, got3, sum2[a3]).astype(BF16)

    def gather(phase, block, coord, stride):
        sends = []
        for k in (1, 2, 3):
            go = copy(
                block, block, ag_send.at[phase, k - 1], ag_recv.at[phase, k - 1],
                along(coord, stride, k),
            )
            go.start()
            sends.append(go)
        pending.extend(sends)
        return sends

    for go in gather(0, sums.at[c, a1, a2, a3], a3, s3):
        go.wait_recv()
    for go in gather(1, sums.at[c, a1, a2], a2, s2):
        go.wait_recv()
    last = gather(2, sums.at[c, a1], a1, s1)
    halves = []
    for k in range(4):
        if k:
            last[k - 1].wait_recv()
        block = sums.at[c, (a1 - k + 4) % 4]
        go = copy(block, block, half_send.at[k], half_recv.at[k], sibling)
        go.start()
        halves.append(go)
    for go in halves:
        go.wait_recv()
    pending.extend(halves)

    for h in range(2):
        lanes = slice(h * 128, (h + 1) * 128)
        total = jnp.dot(
            expand[...], sums[h].reshape(-1, 128), preferred_element_type=F32
        )
        summed[:, lanes] = total
        new_master, _, _ = adamw(
            master[:, lanes], first[:, lanes], second[:, lanes], total
        )
        weights[x, z, y, c, h] = new_master.astype(BF16)

    def blocks(ref, taken, half, rows):
        index = tuple(
            pl.ds(0, 4) if axis in taken else coord
            for axis, coord in (("x", x), ("z", z), ("y", y))
        )
        return ref.at[(*index, c, *half, rows)]

    where = {"x": (x, 32), "z": (z, 8), "y": (y, 2)}
    streams = (
        ("xzy", (0,), pl.ds(0, 48)),
        ("zyx", (1,), pl.ds(0, 48)),
        ("yxz", (pl.ds(0, 2),), pl.ds(48, 16)),
    )

    def forward(block, sem):
        go = copy(block, block, f_send.at[sem], f_recv.at[sem], sibling)
        go.start()
        pending.append(go)
        return go

    forwards = []
    mine = weights.at[x, z, y, c]
    waiting = [[] for _ in streams]
    for phase in range(3):
        for s, (order, half, rows) in enumerate(streams):
            for go, _ in waiting[s]:
                go.wait_recv()
            taken = order[:phase]
            coord, stride = where[order[phase]]
            block = blocks(weights, taken, half, rows)
            arrived = waiting[s]
            waiting[s] = []
            for k in (1, 2, 3):
                n = (s * 3 + phase) * 3 + k - 1
                go = copy(block, block, w_send.at[n], w_recv.at[n], along(coord, stride, k))
                go.start()
                pending.append(go)
                origin = tuple(
                    pl.ds(0, 4) if axis in taken
                    else ((at - k + 4) % 4 if axis == order[phase] else at)
                    for axis, at in (("x", x), ("z", z), ("y", y))
                )
                waiting[s].append((go, (weights.at[(*origin, c, *half, rows)], n)))
            for _, (came, n) in arrived:
                forwards.append(forward(came, n))
        if phase == 0:
            forwards.append(forward(mine, 27))
    for k in range(3):
        for s in range(3):
            go, (came, n) = waiting[s][k]
            go.wait_recv()
            forwards.append(forward(came, n))
    for go in forwards:
        go.wait_recv()
    for go in pending:
        go.wait_send()


def finish_kernel(
    weights, summed, master, first, second,
    out_hbm, new_master, new_first, new_second, sems,
):
    copies = []
    for h in range(2):
        go = pltpu.make_async_copy(
            weights.at[:, h], out_hbm.at[:, :, pl.ds(h * 128, 128)], sems.at[h]
        )
        go.start()
        copies.append(go)
    new_master[...], new_first[...], new_second[...] = adamw(
        master[...], first[...], second[...], summed[...]
    )
    for go in copies:
        go.wait()


def body(gradients, error_memory, block_lists, master, first_moment, second_moment):
    _, rows, width = gradients.shape
    owned = master.shape[0]
    devices = lax.axis_size("dp")
    levels, keep_n = block_lists.shape[1:]
    groups = rows // GROUP
    chunks = rows // CHUNK
    vmem = pl.BlockSpec(memory_space=pltpu.VMEM)
    anywhere = pl.BlockSpec(memory_space=pl.ANY)
    dma = pltpu.SemaphoreType.DMA

    new_errors, packed, expand = pl.pallas_call(
        pack_kernel,
        out_shape=(
            jax.ShapeDtypeStruct((1, rows, width), F32),
            jax.ShapeDtypeStruct((2, 4, 4, 4, 16, 128), BF16),
            jax.ShapeDtypeStruct((owned, keep_n), BF16),
        ),
        in_specs=[anywhere, anywhere, vmem],
        out_specs=(anywhere, vmem, vmem),
        scratch_shapes=[
            pltpu.VMEM((rows, width), BF16),
            pltpu.VMEM((rows, width), F32),
            pltpu.VMEM((keep_n + GROUP + 8, width), F32),
            pltpu.VMEM((groups, GROUP), F32),
            pltpu.VMEM((groups, GROUP), jnp.int32),
            pltpu.VMEM((groups, GROUP), jnp.int32),
            pltpu.VMEM((groups, GROUP), jnp.int32),
            pltpu.VMEM((GROUP, GROUP), F32),
            pltpu.SMEM((groups, GROUP), jnp.int32),
            dma((chunks,)),
            dma((chunks,)),
            dma((chunks,)),
            dma,
        ],
        compiler_params=pltpu.CompilerParams(vmem_limit_bytes=32 * MIB),
        name="pack",
    )(gradients, error_memory, block_lists[0])

    weights, summed = pl.pallas_call(
        merge_kernel,
        out_shape=(
            pltpu.VMEM((4, 4, 4, 2, 2, owned, 128), BF16),
            jax.ShapeDtypeStruct((owned, width), F32),
        ),
        in_specs=[vmem] * 5,
        out_specs=(vmem, vmem),
        scratch_shapes=[
            pltpu.VMEM((4, 4, 4, 16, 128), BF16),
            pltpu.VMEM((4, 4, 4, 16, 128), BF16),
            pltpu.VMEM((4, 4, 16, 128), F32),
            pltpu.VMEM((4, 4, 16, 128), BF16),
            pltpu.VMEM((4, 16, 128), F32),
            pltpu.VMEM((4, 16, 128), BF16),
            pltpu.VMEM((3, 4, 4, 16, 128), BF16),
            pltpu.VMEM((3, 4, 16, 128), BF16),
            pltpu.VMEM((3, 16, 128), BF16),
            pltpu.VMEM((2, 4, 4, 4, 16, 128), BF16),
            dma, dma,
            dma((3, 3)), dma((3, 3)),
            dma((3, 3)), dma((3, 3)),
            dma((4,)), dma((4,)),
            dma((27,)), dma((27,)),
            dma((28,)), dma((28,)),
        ],
        compiler_params=pltpu.CompilerParams(
            collective_id=0, has_side_effects=True, vmem_limit_bytes=24 * MIB
        ),
        name="merge",
    )(packed, expand, master, first_moment, second_moment)

    weights = weights.reshape(devices, 2, owned, 128)
    out, new_master, new_first, new_second = pl.pallas_call(
        finish_kernel,
        out_shape=(
            jax.ShapeDtypeStruct((devices, owned, width), BF16),
            jax.ShapeDtypeStruct((owned, width), F32),
            jax.ShapeDtypeStruct((owned, width), F32),
            jax.ShapeDtypeStruct((owned, width), F32),
        ),
        in_specs=[vmem] * 5,
        out_specs=(anywhere, vmem, vmem, vmem),
        scratch_shapes=[dma((2,))],
        compiler_params=pltpu.CompilerParams(vmem_limit_bytes=24 * MIB),
        name="finish",
    )(weights, summed, master, first_moment, second_moment)
    return new_errors, new_master, new_first, new_second, out.reshape(rows, width)


def solution(mesh):
    in_specs = (
        P("dp", None, None),
        P("dp", None, None),
        P("dp", None, None),
        P("dp", None),
        P("dp", None),
        P("dp", None),
    )
    out_specs = (P("dp", None, None), P("dp", None), P("dp", None), P("dp", None), P())
    return jax.shard_map(
        body, mesh=mesh, in_specs=in_specs, out_specs=out_specs, check_vma=False
    )
```

time: 206 us -> 77.1 us (0.37)
  waiting for transfers between devices: 133 us -> 0 us
  Pallas kernels: 0 us -> 69.9 us
  matrix products: 16.2 us -> 0 us
  starting transfers between devices: 15.3 us -> 0 us
  between operations: 14.2 us -> 0.68 us
  local copies, waits for them, and re-layouts: 16.8 us -> 6.33 us
  other arithmetic: 10.2 us -> 0 us
    all_gather x1 -> x0, waiting for transfers between devices: 73.5 us -> none  [body(): lax.all_gather(new_master.astype(jnp.bfloat16), 'dp', axis=0, tiled=True)]
    pallas_call x0 -> x3, Pallas kernels: none -> 69.9 us  [the longest x1 56.3 us: body(): pl.pallas_call(merge_kernel, out_shape=(pltpu.VMEM((4, 4, 4, 2, 2, owned,...]
    ppermute x7 -> x0, waiting for transfers between devices: 59.5 us -> none  [partner_2(): return lax.ppermute(block, axis, route)]
    dot_general x8 -> x0, matrix products: 16.2 us -> none  [align(): jnp.dot(hits, values, precision=lax.Precision.HIGHEST, preferred_element_...]
    ppermute x7 -> x0, starting transfers between devices: 15.3 us -> none  [partner_2(): return lax.ppermute(block, axis, route)]
    add x2 -> x0, other arithmetic: 9.42 us -> none  [the longest x1 9.42 us: body(): compressed = gradients[0].astype(jnp.float32) + error_memory[0]]
    gather x1 -> x0, local copies, waits for them, and re-layouts: 6.84 us -> none  [body(): held = jnp.take(compressed, chain[0], axis=0)]
    scatter x1 -> x0, local copies, waits for them, and re-layouts: 4.35 us -> none  [membership(): return jnp.zeros((count,), jnp.float32).at[indices].set(1.0)]
  transfers between devices with their start and end apart: 8 -> 0, of which waited for: 8 -> 0; matrix products, arithmetic and copies ran while one was open for 0% -> 0% of each run, Pallas kernels for 0% -> 0%
where the time goes in v1:
time: 77.1 us; the launch traced here: 76.9 us
  Pallas kernels  69.9 us (91%)
  local copies, waits for them, and re-layouts  6.33 us (8%)
    pallas_call x1, Pallas kernels, body(): pl.pallas_call(merge_kernel, out_shape=(pltpu.VMEM((4, 4, 4, 2, 2, owned,...  56.3 us
    pallas_call x1, Pallas kernels, body(): pl.pallas_call(pack_kernel, out_shape=(jax.ShapeDtypeStruct((1, rows, wid...  10.9 us
    unnamed x12, local copies, waits for them, and re-layouts  6.33 us
    pallas_call x1, Pallas kernels, body(): pl.pallas_call(finish_kernel, out_shape=(jax.ShapeDtypeStruct((devices, o...  2.7 us

profile of v1, /device:TPU:1, one launch (start us, length us, event | category | flops | bytes accessed | tf_op | source)
XLA Modules:
  0.0 76.9 jit_solution(10794938666735232794)
XLA Ops:
  0.6 0.0 copy-start
  0.6 3.4 %copy-done = f32[1,8192,256]{2,1,0:T(8,128)S(1)} copy-done((f32[1,8192,256]{2,1,0:T(8,128)S(1)}, f32[1,8192,256]{2,1,0:T(8,128)}, u32[]{:S(2)}) %copy-start) | copy-done | bytes 8388632
  4.0 0.0 copy-start.1
  4.0 2.2 %copy-done.1 = bf16[1,8192,256]{2,1,0:T(8,128)(2,1)S(1)} copy-done((bf16[1,8192,256]{2,1,0:T(8,128)(2,1)S(1)}, bf16[1,8192,256]{2,1,0:T(8,128)(2,1)}, u32[]{:S(2)}) %copy-start.1) | copy-done | bytes 4194328
  6.2 0.0 copy-start.5
  6.2 0.8 copy-done.5
  7.0 0.0 copy-start.2
  7.0 0.0 copy-start.3
  7.0 0.0 copy-start.4
  7.0 10.9 %pack.1 = (f32[1,8192,256]{2,1,0:T(8,128)}, bf16[2,4,4,4,16,128]{5,4,3,2,1,0:T(8,128)(2,1)S(1)}, bf16[64,1024]{1,0:T(8,128)(2,1)S(1)}) custom-call(bf16[1,8192,256]{2,1,0:T(8,128)(2,1)S(1)} %copy-done.1, f32[1,8192,256]{2,1,0:T(8,128)S(1)} %copy-done, s32[8,1024]{1,0:T(8,128)S(1)} %bitcast.4), custom_call_target="tpu_custom_call" | custom-call | tf_op jit(solution)/shard_map/pack/pallas_call | solution.py:334
  17.9 0.0 copy-done.2
  17.9 0.0 copy-done.3
  17.9 0.0 copy-done.4
  17.9 56.3 %merge.1 = (bf16[4,4,4,2,2,64,128]{6,5,4,3,2,1,0:T(8,128)(2,1)S(1)}, f32[64,256]{1,0:T(8,128)S(1)}) custom-call(bf16[2,4,4,4,16,128]{5,4,3,2,1,0:T(8,128)(2,1)S(1)} %get-tuple-element.15.packed, bf16[64,1024]{1,0:T(8,128)(2,1)S(1)} %get-tuple-element.16.expand, f32[64,256]{1,0:T(8,128)S(1)} %copy-done.2, f32[64,256]{1,0:T(8,128)S(1)} %copy-done.3, ...), custom_call_target="tpu_custom_call" | custom-call | tf_op jit(solution)/shard_map/merge/pallas_call | solution.py:362
  74.2 2.7 %finish.1 = (bf16[128,64,256]{2,1,0:T(8,128)(2,1)}, f32[64,256]{1,0:T(8,128)}, f32[64,256]{1,0:T(8,128)}, f32[64,256]{1,0:T(8,128)}) custom-call(bf16[128,2,64,128]{3,2,1,0:T(8,128)(2,1)S(1)} %bitcast.3, f32[64,256]{1,0:T(8,128)S(1)} %get-tuple-element.18.summed, f32[64,256]{1,0:T(8,128)S(1)} %copy-done.2, f32[64,256]{1,0:T(8,128)S(1)} %copy-done.3, ...), custom_call_target="tpu_custom_call" | custom-call | tf_op jit(solution)/shard_map/finish/pallas_call | solution.py:395
Async XLA Ops:
  0.6 3.4 %copy-start = (f32[1,8192,256]{2,1,0:T(8,128)S(1)}, f32[1,8192,256]{2,1,0:T(8,128)}, u32[]{:S(2)}) copy-start(f32[1,8192,256]{2,1,0:T(8,128)} %err_hbm.1) | copy-start | bytes 25165828
  4.0 2.2 %copy-start.1 = (bf16[1,8192,256]{2,1,0:T(8,128)(2,1)S(1)}, bf16[1,8192,256]{2,1,0:T(8,128)(2,1)}, u32[]{:S(2)}) copy-start(bf16[1,8192,256]{2,1,0:T(8,128)(2,1)} %grad_hbm.1) | copy-start | bytes 12582916
  6.2 0.8 copy-start.5
  7.0 10.9 %copy-start.2 = (f32[64,256]{1,0:T(8,128)S(1)}, f32[64,256]{1,0:T(8,128)}, u32[]{:S(2)}) copy-start(f32[64,256]{1,0:T(8,128)} %master.3) | copy-start | bytes 196612
  7.0 10.9 %copy-start.3 = (f32[64,256]{1,0:T(8,128)S(1)}, f32[64,256]{1,0:T(8,128)}, u32[]{:S(2)}) copy-start(f32[64,256]{1,0:T(8,128)} %first.3) | copy-start | bytes 196612
  7.0 10.9 %copy-start.4 = (f32[64,256]{1,0:T(8,128)S(1)}, f32[64,256]{1,0:T(8,128)}, u32[]{:S(2)}) copy-start(f32[64,256]{1,0:T(8,128)} %second.3) | copy-start | bytes 196612

commit v2 on v1

--- a/solution.py
+++ b/solution.py
@@ -138,7 +138,7 @@
 
 def merge_kernel(
     packed, expand, master, first, second, weights, summed,
-    from_core, part, sum1, part1, sum2, part2, got1, got2, got3, sums,
+    from_core, part, got, sums,
     core_send, core_recv, rs_send, rs_recv, ag_send, ag_recv,
     half_send, half_recv, w_send, w_recv, f_send, f_recv,
 ):
@@ -158,80 +158,56 @@
             device_id=(peer,), device_id_type=MESH,
         )
 
+    chip = me // 2
+    chips = packed.shape[1]
+
+    def far(k):
+        other = (chip + k) % chips
+        return other, 2 * other + c
+
     barrier = pltpu.get_barrier_semaphore()
-    peers = [sibling]
-    for coord, stride in ((x, 32), (z, 8), (y, 2)):
-        peers += [along(coord, stride, k) for k in (1, 2, 3)]
-    for peer in peers:
-        pl.semaphore_signal(barrier, inc=1, device_id=(peer,), device_id_type=MESH)
-    pl.semaphore_wait(barrier, len(peers))
+
+    def greet(k, _):
+        pl.semaphore_signal(
+            barrier, inc=1, device_id=(far(k)[1],), device_id_type=MESH
+        )
+        return 0
+
+    pl.semaphore_signal(barrier, inc=1, device_id=(sibling,), device_id_type=MESH)
+    lax.fori_loop(1, chips, greet, 0)
+    pl.semaphore_wait(barrier, chips)
 
     pending = []
-
-    d = 1 - c
-    a1, s1 = d * x + c * z, d * 32 + c * 8
-    a2, s2 = d * z + c * y, d * 8 + c * 2
-    a3, s3 = d * y + c * x, d * 2 + c * 32
-
-    swap = copy(packed.at[d], from_core, core_send, core_recv, sibling)
+    swap = copy(packed.at[1 - c], from_core, core_send, core_recv, sibling)
     swap.start()
     swap.wait_recv()
-    pending.append(swap)
     part[...] = (packed[c].astype(F32) + from_core[...].astype(F32)).astype(BF16)
 
-    def reduce(phase, source, coord, stride, got, own):
-        sends = []
-        for k in (1, 2, 3):
-            go = copy(
-                source.at[(coord + k) % 4], got.at[k - 1],
-                rs_send.at[phase, k - 1], rs_recv.at[phase, k - 1],
-                along(coord, stride, k),
-            )
-            go.start()
-            sends.append(go)
-        pending.extend(sends)
-        total = own
-        for k in (1, 2, 3):
-            sends[k - 1].wait_recv()
-            total = total + got[k - 1].astype(F32)
-        return total
-
-    sum1[...] = reduce(
-        0, part, a1, s1, got1, packed[c, a1].astype(F32) + from_core[a1].astype(F32)
-    )
-    part1[...] = sum1[...].astype(BF16)
-    sum2[...] = reduce(1, part1, a2, s2, got2, sum1[a2])
-    part2[...] = sum2[...].astype(BF16)
-    sums[c, a1, a2, a3] = reduce(2, part2, a3, s3, got3, sum2[a3]).astype(BF16)
-
-    def gather(phase, block, coord, stride):
-        sends = []
-        for k in (1, 2, 3):
-            go = copy(
-                block, block, ag_send.at[phase, k - 1], ag_recv.at[phase, k - 1],
-                along(coord, stride, k),
-            )
-            go.start()
-            sends.append(go)
-        pending.extend(sends)
-        return sends
-
-    for go in gather(0, sums.at[c, a1, a2, a3], a3, s3):
-        go.wait_recv()
-    for go in gather(1, sums.at[c, a1, a2], a2, s2):
-        go.wait_recv()
-    last = gather(2, sums.at[c, a1], a1, s1)
-    halves = []
-    for k in range(4):
-        if k:
-            last[k - 1].wait_recv()
-        block = sums.at[c, (a1 - k + 4) % 4]
-        go = copy(block, block, half_send.at[k], half_recv.at[k], sibling)
-        go.start()
-        halves.append(go)
-    for go in halves:
-        go.wait_recv()
-    pending.extend(halves)
+    def scatter(k):
+        other, peer = far(k)
+        return copy(part.at[other], got.at[k - 1], rs_send.at[k], rs_recv.at[k], peer)
+
+    def gather(k):
+        unit = sums.at[c, chip]
+        return copy(unit, unit, ag_send.at[k], ag_recv.at[k], far(k)[1])
+
+    def each(act):
+        lax.fori_loop(1, chips, lambda k, _: (act(k), 0)[1], 0)
+
+    each(lambda k: scatter(k).start())
+    own = packed[c, chip].astype(F32) + from_core[chip].astype(F32)
+    each(lambda k: scatter(k).wait_recv())
+    sums[c, chip] = (own + jnp.sum(got[...].astype(F32), axis=0)).astype(BF16)
+    each(lambda k: gather(k).start())
+    each(lambda k: gather(k).wait_recv())
+    block = sums.at[c]
+    halves = copy(block, block, half_send, half_recv, sibling)
+    halves.start()
+    each(lambda k: scatter(k).wait_send())
+    each(lambda k: gather(k).wait_send())
+    swap.wait_send()
+    halves.wait_recv()
+    pending.append(halves)
 
     for h in range(2):
         lanes = slice(h * 128, (h + 1) * 128)
@@ -329,16 +305,17 @@
     chunks = rows // CHUNK
     vmem = pl.BlockSpec(memory_space=pltpu.VMEM)
     anywhere = pl.BlockSpec(memory_space=pl.ANY)
+    hbm = pl.BlockSpec(memory_space=pltpu.HBM)
     dma = pltpu.SemaphoreType.DMA
 
     new_errors, packed, expand = pl.pallas_call(
         pack_kernel,
         out_shape=(
             jax.ShapeDtypeStruct((1, rows, width), F32),
-            jax.ShapeDtypeStruct((2, 4, 4, 4, 16, 128), BF16),
+            jax.ShapeDtypeStruct((2, 64, 16, 128), BF16),
             jax.ShapeDtypeStruct((owned, keep_n), BF16),
         ),
-        in_specs=[anywhere, anywhere, vmem],
+        in_specs=[hbm, hbm, vmem],
         out_specs=(anywhere, vmem, vmem),
         scratch_shapes=[
             pltpu.VMEM((rows, width), BF16),
@@ -368,20 +345,14 @@
         in_specs=[vmem] * 5,
         out_specs=(vmem, vmem),
         scratch_shapes=[
-            pltpu.VMEM((4, 4, 4, 16, 128), BF16),
-            pltpu.VMEM((4, 4, 4, 16, 128), BF16),
-            pltpu.VMEM((4, 4, 16, 128), F32),
-            pltpu.VMEM((4, 4, 16, 128), BF16),
-            pltpu.VMEM((4, 16, 128), F32),
-            pltpu.VMEM((4, 16, 128), BF16),
-            pltpu.VMEM((3, 4, 4, 16, 128), BF16),
-            pltpu.VMEM((3, 4, 16, 128), BF16),
-            pltpu.VMEM((3, 16, 128), BF16),
-            pltpu.VMEM((2, 4, 4, 4, 16, 128), BF16),
+            pltpu.VMEM((64, 16, 128), BF16),
+            pltpu.VMEM((64, 16, 128), BF16),
+            pltpu.VMEM((63, 16, 128), BF16),
+            pltpu.VMEM((2, 64, 16, 128), BF16),
             dma, dma,
-            dma((3, 3)), dma((3, 3)),
-            dma((3, 3)), dma((3, 3)),
-            dma((4,)), dma((4,)),
+            dma((64,)), dma((64,)),
+            dma((64,)), dma((64,)),
+            dma, dma,
             dma((27,)), dma((27,)),
             dma((28,)), dma((28,)),
         ],

time: 77.1 us -> 74.4 us (0.965)
  Pallas kernels: 69.9 us -> 67.1 us
    pallas_call x1, Pallas kernels: 56.3 us -> 53.5 us  [body(): pl.pallas_call(merge_kernel, out_shape=(pltpu.VMEM((4, 4, 4, 2, 2, owned,...]
where the time goes in v2:
time: 74.4 us; the launch traced here: 74.2 us
  Pallas kernels  67.1 us (90%)
  local copies, waits for them, and re-layouts  6.33 us (9%)
    pallas_call x1, Pallas kernels, body(): pl.pallas_call(merge_kernel, out_shape=(pltpu.VMEM((4, 4, 4, 2, 2, owned,...  53.5 us
    pallas_call x1, Pallas kernels, body(): pl.pallas_call(pack_kernel, out_shape=(jax.ShapeDtypeStruct((1, rows, wid...  10.9 us
    unnamed x12, local copies, waits for them, and re-layouts  6.33 us
    pallas_call x1, Pallas kernels, body(): pl.pallas_call(finish_kernel, out_shape=(jax.ShapeDtypeStruct((devices, o...  2.7 us

profile of v2, /device:TPU:1, one launch (start us, length us, event | category | flops | bytes accessed | tf_op | source)
XLA Modules:
  0.0 74.2 jit_solution(16149939354944120723)
XLA Ops:
  0.6 0.0 copy-start
  0.6 3.4 %copy-done = f32[1,8192,256]{2,1,0:T(8,128)S(1)} copy-done((f32[1,8192,256]{2,1,0:T(8,128)S(1)}, f32[1,8192,256]{2,1,0:T(8,128)}, u32[]{:S(2)}) %copy-start) | copy-done | bytes 8388632
  4.0 0.0 copy-start.1
  4.0 2.2 %copy-done.1 = bf16[1,8192,256]{2,1,0:T(8,128)(2,1)S(1)} copy-done((bf16[1,8192,256]{2,1,0:T(8,128)(2,1)S(1)}, bf16[1,8192,256]{2,1,0:T(8,128)(2,1)}, u32[]{:S(2)}) %copy-start.1) | copy-done | bytes 4194328
  6.2 0.0 copy-start.5
  6.2 0.8 %copy-done.5 = s32[1,8,1024]{2,1,0:T(8,128)S(1)} copy-done((s32[1,8,1024]{2,1,0:T(8,128)S(1)}, s32[1,8,1024]{2,1,0:T(8,128)}, u32[]{:S(2)}) %copy-start.5) | copy-done | bytes 32792
  7.0 0.0 copy-start.2
  7.0 0.0 copy-start.3
  7.0 0.0 copy-start.4
  7.0 10.9 %pack.1 = (f32[1,8192,256]{2,1,0:T(8,128)}, bf16[2,64,16,128]{3,2,1,0:T(8,128)(2,1)S(1)}, bf16[64,1024]{1,0:T(8,128)(2,1)S(1)}) custom-call(bf16[1,8192,256]{2,1,0:T(8,128)(2,1)S(1)} %copy-done.1, f32[1,8192,256]{2,1,0:T(8,128)S(1)} %copy-done, s32[8,1024]{1,0:T(8,128)S(1)} %bitcast.4), custom_call_target="tpu_custom_call" | custom-call | tf_op jit(solution)/shard_map/pack/pallas_call | solution.py:311
  17.9 0.0 copy-done.2
  17.9 0.0 copy-done.3
  17.9 0.0 copy-done.4
  17.9 53.5 %merge.1 = (bf16[4,4,4,2,2,64,128]{6,5,4,3,2,1,0:T(8,128)(2,1)S(1)}, f32[64,256]{1,0:T(8,128)S(1)}) custom-call(bf16[2,64,16,128]{3,2,1,0:T(8,128)(2,1)S(1)} %get-tuple-element.15.packed, bf16[64,1024]{1,0:T(8,128)(2,1)S(1)} %get-tuple-element.16.expand, f32[64,256]{1,0:T(8,128)S(1)} %copy-done.2, f32[64,256]{1,0:T(8,128)S(1)} %copy-done.3, ...), custom_call_target="tpu_custom_call" | custom-call | tf_op jit(solution)/shard_map/merge/pallas_call | solution.py:339
  71.5 2.7 %finish.1 = (bf16[128,64,256]{2,1,0:T(8,128)(2,1)}, f32[64,256]{1,0:T(8,128)}, f32[64,256]{1,0:T(8,128)}, f32[64,256]{1,0:T(8,128)}) custom-call(bf16[128,2,64,128]{3,2,1,0:T(8,128)(2,1)S(1)} %bitcast.3, f32[64,256]{1,0:T(8,128)S(1)} %get-tuple-element.18.summed, f32[64,256]{1,0:T(8,128)S(1)} %copy-done.2, f32[64,256]{1,0:T(8,128)S(1)} %copy-done.3, ...), custom_call_target="tpu_custom_call" | custom-call | tf_op jit(solution)/shard_map/finish/pallas_call | solution.py:366
Async XLA Ops:
  0.6 3.4 %copy-start = (f32[1,8192,256]{2,1,0:T(8,128)S(1)}, f32[1,8192,256]{2,1,0:T(8,128)}, u32[]{:S(2)}) copy-start(f32[1,8192,256]{2,1,0:T(8,128)} %err_hbm.1) | copy-start | bytes 25165828
  4.0 2.2 %copy-start.1 = (bf16[1,8192,256]{2,1,0:T(8,128)(2,1)S(1)}, bf16[1,8192,256]{2,1,0:T(8,128)(2,1)}, u32[]{:S(2)}) copy-start(bf16[1,8192,256]{2,1,0:T(8,128)(2,1)} %grad_hbm.1) | copy-start | bytes 12582916
  6.2 0.8 %copy-start.5 = (s32[1,8,1024]{2,1,0:T(8,128)S(1)}, s32[1,8,1024]{2,1,0:T(8,128)}, u32[]{:S(2)}) copy-start(s32[1,8,1024]{2,1,0:T(8,128)} %param.8) | copy-start | bytes 98308
  7.0 10.9 %copy-start.2 = (f32[64,256]{1,0:T(8,128)S(1)}, f32[64,256]{1,0:T(8,128)}, u32[]{:S(2)}) copy-start(f32[64,256]{1,0:T(8,128)} %master.3) | copy-start | bytes 196612
  7.0 10.9 %copy-start.3 = (f32[64,256]{1,0:T(8,128)S(1)}, f32[64,256]{1,0:T(8,128)}, u32[]{:S(2)}) copy-start(f32[64,256]{1,0:T(8,128)} %first.3) | copy-start | bytes 196612
  7.0 10.9 %copy-start.4 = (f32[64,256]{1,0:T(8,128)S(1)}, f32[64,256]{1,0:T(8,128)}, u32[]{:S(2)}) copy-start(f32[64,256]{1,0:T(8,128)} %second.3) | copy-start | bytes 196612

commit v3 on v0

v3 whole, which is shorter than its diff:
```python
import jax
import jax.numpy as jnp
from jax import lax
from jax.experimental import pallas as pl
from jax.experimental.pallas import tpu as pltpu
from jax.sharding import PartitionSpec as P

FIRST_BIAS = 0.9999734386011124
SECOND_BIAS = 0.09520785288629036
MESH = pl.DeviceIdType.MESH
F32 = jnp.float32
BF16 = jnp.bfloat16
MIB = 1 << 20

GROUP = 128
CHUNK = 512
UNIT = 16
SPAN = 256

ORDERS = ("xzy", "zyx", "yxz")


def iota(shape, dim):
    return lax.broadcasted_iota(jnp.int32, shape, dim)


def onehot(hits):
    return jnp.where(hits, 1.0, 0.0).astype(BF16)


def adamw(master, first, second, summed):
    new_first = 0.9 * first + 0.1 * summed
    new_second = 0.999 * second + 0.001 * summed * summed
    first_hat = new_first / FIRST_BIAS
    second_hat = new_second / SECOND_BIAS
    new_master = master - 0.001 * (
        first_hat / (jnp.sqrt(second_hat) + 1e-08) + 0.1 * master
    )
    return new_master, new_first, new_second


def merge_kernel(
    grad_hbm, err_hbm, lists_hbm, master_hbm, first_hbm, second_hbm,
    err, weights, result, expand, rooted, starts,
    grad, lists, raw, state_rows, acc, sent, kept, column, value_b,
    packed, from_core, part, got,
    state, state1, state2, state3, sgot1, sgot2, sgot3,
    grad_sem, err_sem, list_sem, raw_sem,
    core_send, core_recv, raw_send, raw_recv,
    rs_send, rs_recv, ag_send, ag_recv, half_send, half_recv,
    s_send, s_recv, w_send, w_recv, f_send, f_recv,
):
    rows = grad.shape[0]
    groups = rows // GROUP
    chunks = rows // CHUNK
    levels, keep_n = lists.shape
    me = lax.axis_index("dp")
    c = me % 2
    y = (me // 2) % 4
    z = (me // 8) % 4
    x = me // 32
    chip = me // 2
    chips = groups
    sibling = me + 1 - 2 * c
    at = {"x": x, "z": z, "y": y}
    strides = {"x": 32, "z": 8, "y": 2}

    def far(k):
        other = (chip + k) % chips
        return other, 2 * other + c

    def along(axis, k):
        return me + ((at[axis] + k) % 4 - at[axis]) * strides[axis]

    def copy(src, dst, send, recv, peer):
        return pltpu.make_async_remote_copy(
            src_ref=src, dst_ref=dst, send_sem=send, recv_sem=recv,
            device_id=(peer,), device_id_type=MESH,
        )

    def each(act, first=1):
        lax.fori_loop(first, chips, lambda k, _: (act(k), 0)[1], 0)

    list_load = pltpu.make_async_copy(lists_hbm.at[0], lists, list_sem)
    list_load.start()
    raw_loads = []
    for a, source in enumerate((master_hbm, first_hbm, second_hbm)):
        for h in range(2):
            go = pltpu.make_async_copy(
                source.at[:, pl.ds(h * 128, 128)], raw.at[h, a], raw_sem.at[h, a]
            )
            go.start()
            raw_loads.append(go)

    def loads(i):
        span = pl.ds(pl.multiple_of(i * CHUNK, CHUNK), CHUNK)
        return (
            pltpu.make_async_copy(grad_hbm.at[0, span], grad.at[span], grad_sem.at[i]),
            pltpu.make_async_copy(err_hbm.at[0, span], err.at[0, span], err_sem.at[i]),
        )

    def load(i, _):
        for go in loads(i):
            go.start()
        return 0

    lax.fori_loop(0, chunks, load, 0)

    barrier = pltpu.get_barrier_semaphore()
    pl.semaphore_signal(barrier, inc=1, device_id=(sibling,), device_id_type=MESH)
    each(
        lambda k: pl.semaphore_signal(
            barrier, inc=1, device_id=(far(k)[1],), device_id_type=MESH
        )
    )

    list_load.wait()

    def member(r):
        ids = lists[r : r + 1, :]
        high = onehot(iota((groups, keep_n), 0) == ids // GROUP)
        low = onehot(iota((GROUP, keep_n), 0) == ids % GROUP)
        return lax.dot_general(
            high, low, (((1,), (1,)), ((), ())), preferred_element_type=F32
        )

    root = member(levels - 1)
    root_b = root.astype(BF16)
    before = onehot(iota((GROUP, GROUP), 0) < iota((GROUP, GROUP), 1))
    inside = jnp.dot(root_b, before, preferred_element_type=F32)
    total = jnp.dot(root_b, jnp.ones((GROUP, GROUP), BF16), preferred_element_type=F32)
    above = onehot(iota((groups, groups), 1) < iota((groups, groups), 0))
    start = jnp.dot(above, total.astype(BF16), preferred_element_type=F32)
    rank = start + inside
    starts[...] = start.astype(jnp.int32)
    rooted[...] = jnp.where(root > 0.5, rank, -1.0)

    keep = member(0)
    sent[...] = keep
    for r in range(1, levels - 1):
        keep = keep * member(r)
    kept[...] = jnp.where(keep * root > 0.5, rank, -1.0)

    chip_ranks = rooted[pl.ds(chip, 1), :]
    column[...] = jnp.transpose(jnp.broadcast_to(chip_ranks, (GROUP, GROUP)))
    half = column[pl.ds(pl.multiple_of(c * 64, 64), 64), :]
    for k in range(keep_n // GROUP):
        lanes = (iota((64, GROUP), 1) + k * GROUP).astype(F32)
        expand[:, k * GROUP : (k + 1) * GROUP] = onehot(half == lanes)

    for go in raw_loads:
        go.wait()
    for h in range(2):
        new_master, _, _ = adamw(raw[h, 0], raw[h, 1], raw[h, 2], 0.0)
        weights[x, z, y, c, h] = jnp.where(half < 0.0, new_master, 0.0).astype(BF16)
    own_rows = pl.ds(pl.multiple_of(c * 64, 64), 64)
    state_rows[:, own_rows, :] = raw[c]

    pl.semaphore_wait(barrier, chips)

    raw_swap = copy(
        raw.at[1 - c], state_rows.at[:, own_rows], raw_send, raw_recv, sibling
    )
    raw_swap.start()

    pending = [raw_swap]

    parts = (
        ((0,), pl.ds(0, 48)),
        ((1,), pl.ds(0, 48)),
        ((pl.ds(0, 2),), pl.ds(48, 16)),
    )

    def region(s, taken, place):
        cols, span = parts[s]
        index = tuple(pl.ds(0, 4) if axis in taken else place[axis] for axis in "xzy")
        return weights.at[(*index, c, *cols, span)]

    def spread(phase):
        out = []
        for s, order in enumerate(ORDERS):
            axis = order[phase]
            block = region(s, order[:phase], at)
            for k in (1, 2, 3):
                n = (s * 3 + phase) * 3 + k - 1
                go = copy(block, block, w_send.at[n], w_recv.at[n], along(axis, k))
                go.start()
                pending.append(go)
                origin = {**at, axis: (at[axis] - k + 4) % 4}
                out.append((go, region(s, order[:phase], origin), n))
        return out

    forwards = []

    def forward(block, n):
        go = copy(block, block, f_send.at[n], f_recv.at[n], sibling)
        go.start()
        pending.append(go)
        forwards.append(go)

    def arrive(sends):
        for go, _, _ in sends:
            go.wait_recv()

    wave = spread(0)
    forward(weights.at[x, z, y, c], 27)

    acc[...] = jnp.zeros_like(acc)
    diagonal = iota((GROUP, GROUP), 0) == iota((GROUP, GROUP), 1)
    inner = iota((SPAN // 16, 16, GROUP), 0) * 16 + iota((SPAN // 16, 16, GROUP), 1)
    inner = inner.astype(F32).astype(BF16)
    one = jnp.ones((SPAN // 16, 16, GROUP), BF16)
    zero = jnp.zeros((SPAN // 16, 16, GROUP), BF16)

    def pack(i, _):
        for go in loads(i):
            go.wait()
        each_row = []
        for j in range(CHUNK // GROUP):
            g = i * (CHUNK // GROUP) + j
            span = pl.ds(pl.multiple_of(g * GROUP, GROUP), GROUP)
            value = grad[span, :].astype(F32) + err[0, span, :]
            stays = 1.0 - sent[pl.ds(g, 1), :]
            mask = jnp.dot(
                jnp.where(diagonal, stays, 0.0).astype(BF16),
                jnp.ones((GROUP, value.shape[1]), BF16),
                preferred_element_type=F32,
            )
            err[0, span, :] = value * mask
            value_b[j * GROUP : (j + 1) * GROUP, :] = value.astype(BF16)
            each_row.append(kept[pl.ds(g, 1), :])
        for q in range(keep_n // SPAN):
            hits = []
            for row in each_row:
                near = jnp.clip(row - q * SPAN, -1.0, SPAN)
                near = jnp.broadcast_to(near, (16, GROUP)).astype(BF16)
                hit = jnp.where(inner == near[None], one, zero)
                hits.append(hit.reshape(SPAN, GROUP))
            acc[q * SPAN : (q + 1) * SPAN, :] += jnp.dot(
                jnp.concatenate(hits, axis=1), value_b[...], preferred_element_type=F32
            )
        return 0

    lax.fori_loop(0, chunks // 4, pack, 0)

    raw_swap.wait_recv()
    split = []
    for a in range(3):
        whole = state_rows[a]
        high = whole.astype(BF16)
        rest = whole - high.astype(F32)
        middle = rest.astype(BF16)
        low = (rest - middle.astype(F32)).astype(BF16)
        split += [high, middle, low]
    split = jnp.concatenate(split, axis=1)

    def place(i, _):
        hits = onehot(chip_ranks == (iota((128, GROUP), 0) + i * 128).astype(F32))
        moved = jnp.dot(hits, split, preferred_element_type=F32)
        for a, order in enumerate(ORDERS):
            high, middle, low = (
                moved[:, (3 * a + p) * 128 : (3 * a + p + 1) * 128] for p in range(3)
            )
            exact = ((high + middle) + low).reshape(8, UNIT, 128)
            for u in range(8):
                spot = {"x": i // 2, "z": (i % 2) * 2 + u // 4, "y": u % 4}
                state[a, spot[order[0]], spot[order[1]], spot[order[2]]] = exact[u]
        return 0

    lax.fori_loop(0, keep_n // 128, place, 0)

    def state_phase(phase, source, target):
        out = []
        for a, order in enumerate(ORDERS):
            axis = order[phase]
            for k in (1, 2, 3):
                go = copy(
                    source.at[a, (at[axis] + k) % 4], target.at[a, k - 1],
                    s_send.at[phase, a, k - 1], s_recv.at[phase, a, k - 1],
                    along(axis, k),
                )
                go.start()
                pending.append(go)
                out.append(go)
        return out

    def state_sum(phase, sends, source, target, result_ref):
        for go in sends:
            go.wait_recv()
        for a, order in enumerate(ORDERS):
            value = source[a, at[order[phase]]]
            for k in range(3):
                value = value + target[a, k]
            result_ref[a] = value

    sends1 = state_phase(0, state, sgot1)

    arrive(wave)
    next_wave = spread(1)
    for _, block, n in wave:
        forward(block, n)
    wave = next_wave

    lax.fori_loop(chunks // 4, chunks, pack, 0)

    for h in range(2):
        packed[h] = (
            acc[:, h * 128 : (h + 1) * 128].astype(BF16).reshape(packed.shape[1:])
        )
    swap = copy(packed.at[1 - c], from_core, core_send, core_recv, sibling)
    swap.start()
    pending.append(swap)

    state_sum(0, sends1, state, sgot1, state1)
    sends2 = state_phase(1, state1, sgot2)

    swap.wait_recv()
    part[...] = (packed[c].astype(F32) + from_core[...].astype(F32)).astype(BF16)

    def scatter(k):
        other, peer = far(k)
        return copy(part.at[other], got.at[k - 1], rs_send.at[k], rs_recv.at[k], peer)

    each(lambda k: scatter(k).start())
    own = packed[c, chip].astype(F32) + from_core[chip].astype(F32)

    arrive(wave)
    next_wave = spread(2)
    for _, block, n in wave:
        forward(block, n)
    wave = next_wave

    state_sum(1, sends2, state1, sgot2, state2)
    sends3 = state_phase(2, state2, sgot3)
    state_sum(2, sends3, state2, sgot3, state3)

    each(lambda k: scatter(k).wait_recv())
    summed = (own + jnp.sum(got[...].astype(F32), axis=0)).astype(BF16)
    new_master, _, _ = adamw(state3[0], state3[1], state3[2], summed.astype(F32))
    result[c, chip, 0] = summed
    result[c, chip, 1] = new_master.astype(BF16)

    def gather(k):
        unit = result.at[c, chip]
        return copy(unit, unit, ag_send.at[k], ag_recv.at[k], far(k)[1])

    def pass_on(k):
        unit = result.at[c, (chip - k + chips) % chips]
        return copy(unit, unit, half_send.at[k], half_recv.at[k], sibling)

    each(lambda k: gather(k).start())
    pass_on(0).start()

    for go, block, n in wave:
        go.wait_recv()
        forward(block, n)

    def relay(k):
        gather(k).wait_recv()
        pass_on(k).start()

    each(relay)
    each(lambda k: scatter(k).wait_send())
    each(lambda k: gather(k).wait_send())
    for go in pending:
        go.wait_send()
    for go in forwards:
        go.wait_recv()
    each(lambda k: pass_on(k).wait_send(), 0)
    each(lambda k: pass_on(k).wait_recv(), 0)


def finish_kernel(
    err, weights, result, expand, rooted, starts_v, master, first, second,
    err_hbm, out_hbm, new_master, new_first, new_second,
    out, starts, err_sem, out_sem, starts_sem,
):
    groups = rooted.shape[0]
    to_smem = pltpu.make_async_copy(starts_v, starts, starts_sem)
    to_smem.start()
    rows = err.shape[1]
    pieces = err_sem.shape[0]
    copies = []
    for i in range(pieces):
        span = pl.ds(i * (rows // pieces), rows // pieces)
        go = pltpu.make_async_copy(err.at[0, span], err_hbm.at[0, span], err_sem.at[i])
        go.start()
        copies.append(go)

    total = jnp.concatenate(
        [
            jnp.dot(
                expand[...], result[h, :, 0].reshape(-1, 128),
                preferred_element_type=F32,
            )
            for h in range(2)
        ],
        axis=1,
    )
    new_master[...], new_first[...], new_second[...] = adamw(
        master[...], first[...], second[...], total
    )

    to_smem.wait()
    units = result.shape[1]
    window = GROUP // UNIT + 1
    batch = groups // out_sem.shape[0]

    def store(i):
        span = pl.ds(i * batch, batch)
        return pltpu.make_async_copy(out.at[span], out_hbm.at[span], out_sem.at[i])

    def fill(i, _):
        for j in range(batch):
            g = i * batch + j
            unit = jnp.minimum(starts[g, 0] // UNIT, units - window)
            near = rooted[pl.ds(g, 1), :] - (unit * UNIT).astype(F32)
            hits = onehot(iota((window * UNIT, GROUP), 0).astype(F32) == near)
            for h in range(2):
                held = result[h, pl.ds(unit, window), 1].reshape(window * UNIT, 128)
                moved = lax.dot_general(
                    hits, held, (((0,), (0,)), ((), ())), preferred_element_type=F32
                )
                for c in range(2):
                    mine = weights[g, c, h].astype(F32) + moved[c * 64 : c * 64 + 64]
                    out[g, c * 64 : c * 64 + 64, h * 128 : h * 128 + 128] = mine.astype(
                        BF16
                    )
        store(i).start()
        return 0

    steps = out_sem.shape[0]
    lax.fori_loop(0, steps, fill, 0)
    for go in copies:
        go.wait()
    lax.fori_loop(0, steps, lambda i, _: (store(i).wait(), 0)[1], 0)


def body(gradients, error_memory, block_lists, master, first_moment, second_moment):
    _, rows, width = gradients.shape
    owned = master.shape[0]
    levels, keep_n = block_lists.shape[1:]
    groups = rows // GROUP
    chunks = rows // CHUNK
    vmem = pl.BlockSpec(memory_space=pltpu.VMEM)
    anywhere = pl.BlockSpec(memory_space=pl.ANY)
    dma = pltpu.SemaphoreType.DMA

    err, weights, result, expand, rooted, starts = pl.pallas_call(
        merge_kernel,
        out_shape=(
            pltpu.VMEM((1, rows, width), F32),
            pltpu.VMEM((4, 4, 4, 2, 2, owned, 128), BF16),
            pltpu.VMEM((2, groups, 2, UNIT, 128), BF16),
            pltpu.VMEM((owned, keep_n), BF16),
            pltpu.VMEM((groups, GROUP), F32),
            pltpu.VMEM((groups, GROUP), jnp.int32),
        ),
        in_specs=[anywhere] * 6,
        out_specs=(vmem,) * 6,
        scratch_shapes=[
            pltpu.VMEM((rows, width), BF16),
            pltpu.VMEM((levels, keep_n), jnp.int32),
            pltpu.VMEM((2, 3, owned, 128), F32),
            pltpu.VMEM((3, GROUP, 128), F32),
            pltpu.VMEM((keep_n, width), F32),
            pltpu.VMEM((groups, GROUP), F32),
            pltpu.VMEM((groups, GROUP), F32),
            pltpu.VMEM((GROUP, GROUP), F32),
            pltpu.VMEM((CHUNK, width), BF16),
            pltpu.VMEM((2, groups, UNIT, 128), BF16),
            pltpu.VMEM((groups, UNIT, 128), BF16),
            pltpu.VMEM((groups, UNIT, 128), BF16),
            pltpu.VMEM((groups - 1, UNIT, 128), BF16),
            pltpu.VMEM((3, 4, 4, 4, UNIT, 128), F32),
            pltpu.VMEM((3, 4, 4, UNIT, 128), F32),
            pltpu.VMEM((3, 4, UNIT, 128), F32),
            pltpu.VMEM((3, UNIT, 128), F32),
            pltpu.VMEM((3, 3, 4, 4, UNIT, 128), F32),
            pltpu.VMEM((3, 3, 4, UNIT, 128), F32),
            pltpu.VMEM((3, 3, UNIT, 128), F32),
            dma((chunks,)), dma((chunks,)), dma, dma((2, 3)),
            dma, dma, dma, dma,
            dma((groups,)), dma((groups,)),
            dma((groups,)), dma((groups,)),
            dma((groups,)), dma((groups,)),
            dma((3, 3, 3)), dma((3, 3, 3)),
            dma((27,)), dma((27,)),
            dma((28,)), dma((28,)),
        ],
        compiler_params=pltpu.CompilerParams(
            collective_id=0, has_side_effects=True, vmem_limit_bytes=46 * MIB
        ),
        name="merge",
    )(gradients, error_memory, block_lists, master, first_moment, second_moment)

    new_errors, out, new_master, new_first, new_second = pl.pallas_call(
        finish_kernel,
        out_shape=(
            jax.ShapeDtypeStruct((1, rows, width), F32),
            jax.ShapeDtypeStruct((groups, GROUP, width), BF16),
            jax.ShapeDtypeStruct((owned, width), F32),
            jax.ShapeDtypeStruct((owned, width), F32),
            jax.ShapeDtypeStruct((owned, width), F32),
        ),
        in_specs=[vmem] * 9,
        out_specs=(anywhere, anywhere, vmem, vmem, vmem),
        scratch_shapes=[
            pltpu.VMEM((groups, GROUP, width), BF16),
            pltpu.SMEM((groups, GROUP), jnp.int32),
            dma((4,)), dma((8,)), dma,
        ],
        compiler_params=pltpu.CompilerParams(vmem_limit_bytes=32 * MIB),
        name="finish",
    )(
        err, weights.reshape(groups, 2, 2, owned, 128), result, expand, rooted, starts,
        master, first_moment, second_moment,
    )
    return new_errors, new_master, new_first, new_second, out.reshape(rows, width)


def solution(mesh):
    in_specs = (
        P("dp", None, None),
        P("dp", None, None),
        P("dp", None, None),
        P("dp", None),
        P("dp", None),
        P("dp", None),
    )
    out_specs = (P("dp", None, None), P("dp", None), P("dp", None), P("dp", None), P())
    return jax.shard_map(
        body, mesh=mesh, in_specs=in_specs, out_specs=out_specs, check_vma=False
    )
```

time: 206 us -> 63.6 us (0.31)
  waiting for transfers between devices: 133 us -> 0 us
  Pallas kernels: 0 us -> 62.8 us
  local copies, waits for them, and re-layouts: 16.8 us -> 0.01 us
  matrix products: 16.2 us -> 0 us
  starting transfers between devices: 15.3 us -> 0 us
  between operations: 14.2 us -> 0.69 us
  other arithmetic: 10.2 us -> 0 us
    all_gather x1 -> x0, waiting for transfers between devices: 73.5 us -> none  [body(): lax.all_gather(new_master.astype(jnp.bfloat16), 'dp', axis=0, tiled=True)]
    pallas_call x0 -> x2, Pallas kernels: none -> 62.8 us  [the longest x1 56 us: body(): pl.pallas_call(merge_kernel, out_shape=(pltpu.VMEM((1, rows, width), F32)...]
    ppermute x7 -> x0, waiting for transfers between devices: 59.5 us -> none  [partner_2(): return lax.ppermute(block, axis, route)]
    dot_general x8 -> x0, matrix products: 16.2 us -> none  [align(): jnp.dot(hits, values, precision=lax.Precision.HIGHEST, preferred_element_...]
    ppermute x7 -> x0, starting transfers between devices: 15.3 us -> none  [partner_2(): return lax.ppermute(block, axis, route)]
    add x2 -> x0, other arithmetic: 9.42 us -> none  [the longest x1 9.42 us: body(): compressed = gradients[0].astype(jnp.float32) + error_memory[0]]
    gather x1 -> x0, local copies, waits for them, and re-layouts: 6.84 us -> none  [body(): held = jnp.take(compressed, chain[0], axis=0)]
    unnamed x7 -> x6, local copies, waits for them, and re-layouts: 4.49 us -> 0.01 us
  transfers between devices with their start and end apart: 8 -> 0, of which waited for: 8 -> 0; matrix products, arithmetic and copies ran while one was open for 0% -> 0% of each run, Pallas kernels for 0% -> 0%
where the time goes in v3:
time: 63.6 us; the launch traced here: 63.5 us
  Pallas kernels  62.8 us (99%)
  between operations  0.69 us (1%)
    pallas_call x1, Pallas kernels, body(): pl.pallas_call(merge_kernel, out_shape=(pltpu.VMEM((1, rows, width), F32)...  56 us
    pallas_call x1, Pallas kernels, body(): pl.pallas_call(finish_kernel, out_shape=(jax.ShapeDtypeStruct((1, rows, w...  6.73 us

profile of v3, /device:TPU:1, one launch (start us, length us, event | category | flops | bytes accessed | tf_op | source)
XLA Modules:
  0.0 63.5 jit_solution(7645603008855619147)
XLA Ops:
  0.6 0.0 copy-start.2
  0.6 0.0 copy-start.1
  0.7 0.0 copy-start
  0.7 56.0 %merge.1 = (f32[1,8192,256]{2,1,0:T(8,128)S(1)}, bf16[4,4,4,2,2,64,128]{6,5,4,3,2,1,0:T(8,128)(2,1)S(1)}, bf16[2,64,2,16,128]{4,3,2,1,0:T(8,128)(2,1)S(1)}, bf16...) custom-call(bf16[1,8192,256]{2,1,0:T(8,128)(2,1)} %grad_hbm.1, f32[1,8192,256]{2,1,0:T(8,128)} %err_hbm.1, ...), custom_call_target="tpu_custom_call" | custom-call | tf_op jit(solution)/shard_map/merge/pallas_call | solution.py:449
  56.7 0.0 copy-done.2
  56.7 0.0 copy-done.1
  56.7 0.0 copy-done
  56.7 6.7 %finish.1 = (f32[1,8192,256]{2,1,0:T(8,128)}, bf16[64,128,256]{2,1,0:T(8,128)(2,1)}, f32[64,256]{1,0:T(8,128)}, f32[64,256]{1,0:T(8,128)}, f32[64,256]{1,0:T(8,128)}) custom-call(f32[1,8192,256]{2,1,0:T(8,128)S(1)} %get-tuple-element.16.err, bf16[64,2,2,64,128]{4,3,2,1,0:T(8,128)(2,1)S(1)} %bitcast.2, ...), custom_call_target="tpu_custom_call" | custom-call | tf_op jit(solution)/shard_map/finish/pallas_call | solution.py:497
Async XLA Ops:
  0.6 56.1 %copy-start.2 = (f32[64,256]{1,0:T(8,128)S(1)}, f32[64,256]{1,0:T(8,128)}, u32[]{:S(2)}) copy-start(f32[64,256]{1,0:T(8,128)} %second.1) | copy-start | bytes 196612
  0.6 56.1 %copy-start.1 = (f32[64,256]{1,0:T(8,128)S(1)}, f32[64,256]{1,0:T(8,128)}, u32[]{:S(2)}) copy-start(f32[64,256]{1,0:T(8,128)} %first.1) | copy-start | bytes 196612
  0.7 56.1 %copy-start = (f32[64,256]{1,0:T(8,128)S(1)}, f32[64,256]{1,0:T(8,128)}, u32[]{:S(2)}) copy-start(f32[64,256]{1,0:T(8,128)} %master.1) | copy-start | bytes 196612

commit v4 on v3

--- a/solution.py
+++ b/solution.py
@@ -13,7 +13,7 @@
 MIB = 1 << 20
 
 GROUP = 128
-CHUNK = 512
+CHUNK = 1024
 UNIT = 16
 SPAN = 256
 
@@ -78,19 +78,25 @@
             device_id=(peer,), device_id_type=MESH,
         )
 
-    def each(act, first=1):
-        lax.fori_loop(first, chips, lambda k, _: (act(k), 0)[1], 0)
+    def each(act):
+        def nine(i, _):
+            for j in range(9):
+                act(i * 9 + j + 1)
+            return 0
+
+        lax.fori_loop(0, (chips - 1) // 9, nine, 0)
+
+    def bytes_of(ref, send, recv):
+        return copy(ref, ref, send, recv, sibling)
 
     list_load = pltpu.make_async_copy(lists_hbm.at[0], lists, list_sem)
     list_load.start()
-    raw_loads = []
     for a, source in enumerate((master_hbm, first_hbm, second_hbm)):
         for h in range(2):
             go = pltpu.make_async_copy(
-                source.at[:, pl.ds(h * 128, 128)], raw.at[h, a], raw_sem.at[h, a]
+                source.at[:, pl.ds(h * 128, 128)], raw.at[h, a], raw_sem
             )
             go.start()
-            raw_loads.append(go)
 
     def loads(i):
         span = pl.ds(pl.multiple_of(i * CHUNK, CHUNK), CHUNK)
@@ -148,8 +154,7 @@
         lanes = (iota((64, GROUP), 1) + k * GROUP).astype(F32)
         expand[:, k * GROUP : (k + 1) * GROUP] = onehot(half == lanes)
 
-    for go in raw_loads:
-        go.wait()
+    pltpu.make_async_copy(raw, raw, raw_sem).wait()
     for h in range(2):
         new_master, _, _ = adamw(raw[h, 0], raw[h, 1], raw[h, 2], 0.0)
         weights[x, z, y, c, h] = jnp.where(half < 0.0, new_master, 0.0).astype(BF16)
@@ -163,8 +168,6 @@
     )
     raw_swap.start()
 
-    pending = [raw_swap]
-
     parts = (
         ((0,), pl.ds(0, 48)),
         ((1,), pl.ds(0, 48)),
@@ -176,34 +179,37 @@
         index = tuple(pl.ds(0, 4) if axis in taken else place[axis] for axis in "xzy")
         return weights.at[(*index, c, *cols, span)]
 
+    def triple(s, phase, sends, recvs):
+        order = ORDERS[s]
+        block = region(s, order[:phase], {**at, order[phase]: pl.ds(0, 3)})
+        n = s * 3 + phase
+        return bytes_of(block, sends.at[n], recvs.at[n])
+
     def spread(phase):
-        out = []
         for s, order in enumerate(ORDERS):
             axis = order[phase]
             block = region(s, order[:phase], at)
+            n = s * 3 + phase
             for k in (1, 2, 3):
-                n = (s * 3 + phase) * 3 + k - 1
-                go = copy(block, block, w_send.at[n], w_recv.at[n], along(axis, k))
-                go.start()
-                pending.append(go)
-                origin = {**at, axis: (at[axis] - k + 4) % 4}
-                out.append((go, region(s, order[:phase], origin), n))
-        return out
-
-    forwards = []
-
-    def forward(block, n):
-        go = copy(block, block, f_send.at[n], f_recv.at[n], sibling)
-        go.start()
-        pending.append(go)
-        forwards.append(go)
-
-    def arrive(sends):
-        for go, _, _ in sends:
-            go.wait_recv()
-
-    wave = spread(0)
-    forward(weights.at[x, z, y, c], 27)
+                copy(
+                    block, block, w_send.at[n], w_recv.at[n], along(axis, k)
+                ).start()
+
+    def arrive(phase, s):
+        triple(s, phase, w_send, w_recv).wait_recv()
+
+    def forward(phase, s):
+        order = ORDERS[s]
+        axis = order[phase]
+        n = s * 3 + phase
+        for k in (1, 2, 3):
+            block = region(s, order[:phase], {**at, axis: (at[axis] + k) % 4})
+            copy(block, block, f_send.at[n], f_recv.at[n], sibling).start()
+
+    spread(0)
+    mine = weights.at[x, z, y, c]
+    own_forward = copy(mine, mine, f_send.at[9], f_recv.at[9], sibling)
+    own_forward.start()
 
     acc[...] = jnp.zeros_like(acc)
     diagonal = iota((GROUP, GROUP), 0) == iota((GROUP, GROUP), 1)
@@ -270,36 +276,36 @@
     lax.fori_loop(0, keep_n // 128, place, 0)
 
     def state_phase(phase, source, target):
-        out = []
         for a, order in enumerate(ORDERS):
             axis = order[phase]
             for k in (1, 2, 3):
                 go = copy(
                     source.at[a, (at[axis] + k) % 4], target.at[a, k - 1],
-                    s_send.at[phase, a, k - 1], s_recv.at[phase, a, k - 1],
+                    s_send.at[phase * 3 + a], s_recv.at[phase * 3 + a],
                     along(axis, k),
                 )
                 go.start()
-                pending.append(go)
-                out.append(go)
-        return out
-
-    def state_sum(phase, sends, source, target, result_ref):
-        for go in sends:
-            go.wait_recv()
+
+    def state_bytes(phase, target, a):
+        n = phase * 3 + a
+        return bytes_of(target.at[a], s_send.at[n], s_recv.at[n])
+
+    def state_sum(phase, source, target, result_ref):
+        for a in range(3):
+            state_bytes(phase, target, a).wait_recv()
         for a, order in enumerate(ORDERS):
             value = source[a, at[order[phase]]]
             for k in range(3):
                 value = value + target[a, k]
             result_ref[a] = value
 
-    sends1 = state_phase(0, state, sgot1)
-
-    arrive(wave)
-    next_wave = spread(1)
-    for _, block, n in wave:
-        forward(block, n)
-    wave = next_wave
+    state_phase(0, state, sgot1)
+
+    for s in range(3):
+        arrive(0, s)
+    spread(1)
+    for s in range(3):
+        forward(0, s)
 
     lax.fori_loop(chunks // 4, chunks, pack, 0)
 
@@ -309,65 +315,75 @@
         )
     swap = copy(packed.at[1 - c], from_core, core_send, core_recv, sibling)
     swap.start()
-    pending.append(swap)
-
-    state_sum(0, sends1, state, sgot1, state1)
-    sends2 = state_phase(1, state1, sgot2)
+
+    state_sum(0, state, sgot1, state1)
+    state_phase(1, state1, sgot2)
 
     swap.wait_recv()
     part[...] = (packed[c].astype(F32) + from_core[...].astype(F32)).astype(BF16)
 
     def scatter(k):
         other, peer = far(k)
-        return copy(part.at[other], got.at[k - 1], rs_send.at[k], rs_recv.at[k], peer)
+        return copy(part.at[other], got.at[k - 1], rs_send, rs_recv, peer)
 
     each(lambda k: scatter(k).start())
     own = packed[c, chip].astype(F32) + from_core[chip].astype(F32)
 
-    arrive(wave)
-    next_wave = spread(2)
-    for _, block, n in wave:
-        forward(block, n)
-    wave = next_wave
-
-    state_sum(1, sends2, state1, sgot2, state2)
-    sends3 = state_phase(2, state2, sgot3)
-    state_sum(2, sends3, state2, sgot3, state3)
-
-    each(lambda k: scatter(k).wait_recv())
+    for s in range(3):
+        arrive(1, s)
+    spread(2)
+    for s in range(3):
+        forward(1, s)
+
+    state_sum(1, state1, sgot2, state2)
+    state_phase(2, state2, sgot3)
+    state_sum(2, state2, sgot3, state3)
+
+    scattered = bytes_of(got, rs_send, rs_recv)
+    scattered.wait_recv()
     summed = (own + jnp.sum(got[...].astype(F32), axis=0)).astype(BF16)
     new_master, _, _ = adamw(state3[0], state3[1], state3[2], summed.astype(F32))
     result[c, chip, 0] = summed
     result[c, chip, 1] = new_master.astype(BF16)
 
+    plane = chips // 4
+
     def gather(k):
         unit = result.at[c, chip]
-        return copy(unit, unit, ag_send.at[k], ag_recv.at[k], far(k)[1])
-
-    def pass_on(k):
-        unit = result.at[c, (chip - k + chips) % chips]
-        return copy(unit, unit, half_send.at[k], half_recv.at[k], sibling)
+        return copy(unit, unit, ag_send, ag_recv.at[x], far(k)[1])
+
+    def pass_on(q):
+        block = result.at[c, pl.ds(q * plane, plane)]
+        return copy(block, block, half_send, half_recv, sibling)
 
     each(lambda k: gather(k).start())
-    pass_on(0).start()
-
-    for go, block, n in wave:
-        go.wait_recv()
-        forward(block, n)
-
-    def relay(k):
-        gather(k).wait_recv()
-        pass_on(k).start()
-
-    each(relay)
-    each(lambda k: scatter(k).wait_send())
-    each(lambda k: gather(k).wait_send())
-    for go in pending:
-        go.wait_send()
-    for go in forwards:
-        go.wait_recv()
-    each(lambda k: pass_on(k).wait_send(), 0)
-    each(lambda k: pass_on(k).wait_recv(), 0)
+
+    for s in range(3):
+        arrive(2, s)
+        forward(2, s)
+
+    for k in (3, 2, 1):
+        q = (x + k) % 4
+        block = result.at[c, pl.ds(q * plane, plane)]
+        bytes_of(block, ag_send, ag_recv.at[q]).wait_recv()
+        pass_on(q).start()
+    bytes_of(result.at[c, pl.ds(0, plane - 1)], ag_send, ag_recv.at[x]).wait_recv()
+    pass_on(x).start()
+
+    scattered.wait_send()
+    bytes_of(result.at[c, pl.ds(0, chips - 1)], ag_send, ag_recv.at[x]).wait_send()
+    raw_swap.wait_send()
+    swap.wait_send()
+    own_forward.wait()
+    for a in range(3):
+        state_bytes(0, sgot1, a).wait_send()
+        state_bytes(1, sgot2, a).wait_send()
+        state_bytes(2, sgot3, a).wait_send()
+    for phase in range(3):
+        for s in range(3):
+            triple(s, phase, w_send, w_recv).wait_send()
+            triple(s, phase, f_send, f_recv).wait()
+    bytes_of(result.at[c], half_send, half_recv).wait()
 
 
 def finish_kernel(
@@ -479,14 +495,12 @@
             pltpu.VMEM((3, 3, 4, 4, UNIT, 128), F32),
             pltpu.VMEM((3, 3, 4, UNIT, 128), F32),
             pltpu.VMEM((3, 3, UNIT, 128), F32),
-            dma((chunks,)), dma((chunks,)), dma, dma((2, 3)),
+            dma((chunks,)), dma((chunks,)), dma, dma,
             dma, dma, dma, dma,
-            dma((groups,)), dma((groups,)),
-            dma((groups,)), dma((groups,)),
-            dma((groups,)), dma((groups,)),
-            dma((3, 3, 3)), dma((3, 3, 3)),
-            dma((27,)), dma((27,)),
-            dma((28,)), dma((28,)),
+            dma, dma, dma, dma((4,)), dma, dma,
+            dma((9,)), dma((9,)),
+            dma((9,)), dma((9,)),
+            dma((10,)), dma((10,)),
         ],
         compiler_params=pltpu.CompilerParams(
             collective_id=0, has_side_effects=True, vmem_limit_bytes=46 * MIB

time: 63.6 us -> 56.6 us (0.89)
  Pallas kernels: 62.8 us -> 55.8 us
    pallas_call x1, Pallas kernels: 56 us -> 49 us  [body(): pl.pallas_call(merge_kernel, out_shape=(pltpu.VMEM((1, rows, width), F32)...]
where the time goes in v4:
time: 56.6 us; the launch traced here: 56.5 us
  Pallas kernels  55.8 us (99%)
  between operations  0.69 us (1%)
    pallas_call x1, Pallas kernels, body(): pl.pallas_call(merge_kernel, out_shape=(pltpu.VMEM((1, rows, width), F32)...  49 us
    pallas_call x1, Pallas kernels, body(): pl.pallas_call(finish_kernel, out_shape=(jax.ShapeDtypeStruct((1, rows, w...  6.75 us

profile of v4, /device:TPU:1, one launch (start us, length us, event | category | flops | bytes accessed | tf_op | source)
XLA Modules:
  0.0 56.5 jit_solution(10001506393080354618)
XLA Ops:
  0.6 0.0 copy-start.2
  0.6 0.0 copy-start.1
  0.7 0.0 copy-start
  0.7 49.0 %merge.1 = (f32[1,8192,256]{2,1,0:T(8,128)S(1)}, bf16[4,4,4,2,2,64,128]{6,5,4,3,2,1,0:T(8,128)(2,1)S(1)}, bf16[2,64,2,16,128]{4,3,2,1,0:T(8,128)(2,1)S(1)}, bf16...) custom-call(bf16[1,8192,256]{2,1,0:T(8,128)(2,1)} %grad_hbm.1, f32[1,8192,256]{2,1,0:T(8,128)} %err_hbm.1, ...), custom_call_target="tpu_custom_call" | custom-call | tf_op jit(solution)/shard_map/merge/pallas_call | solution.py:465
  49.7 0.0 copy-done.2
  49.7 0.0 copy-done.1
  49.7 0.0 copy-done
  49.7 6.7 %finish.1 = (f32[1,8192,256]{2,1,0:T(8,128)}, bf16[64,128,256]{2,1,0:T(8,128)(2,1)}, f32[64,256]{1,0:T(8,128)}, f32[64,256]{1,0:T(8,128)}, f32[64,256]{1,0:T(8,128)}) custom-call(f32[1,8192,256]{2,1,0:T(8,128)S(1)} %get-tuple-element.16.err, bf16[64,2,2,64,128]{4,3,2,1,0:T(8,128)(2,1)S(1)} %bitcast.2, ...), custom_call_target="tpu_custom_call" | custom-call | tf_op jit(solution)/shard_map/finish/pallas_call | solution.py:511
Async XLA Ops:
  0.6 49.0 %copy-start.2 = (f32[64,256]{1,0:T(8,128)S(1)}, f32[64,256]{1,0:T(8,128)}, u32[]{:S(2)}) copy-start(f32[64,256]{1,0:T(8,128)} %second.1) | copy-start | bytes 196612
  0.6 49.0 %copy-start.1 = (f32[64,256]{1,0:T(8,128)S(1)}, f32[64,256]{1,0:T(8,128)}, u32[]{:S(2)}) copy-start(f32[64,256]{1,0:T(8,128)} %first.1) | copy-start | bytes 196612
  0.7 49.0 %copy-start = (f32[64,256]{1,0:T(8,128)S(1)}, f32[64,256]{1,0:T(8,128)}, u32[]{:S(2)}) copy-start(f32[64,256]{1,0:T(8,128)} %master.1) | copy-start | bytes 196612

commit v5 on v4

--- a/solution.py
+++ b/solution.py
@@ -48,7 +48,7 @@
     grad_sem, err_sem, list_sem, raw_sem,
     core_send, core_recv, raw_send, raw_recv,
     rs_send, rs_recv, ag_send, ag_recv, half_send, half_recv,
-    s_send, s_recv, w_send, w_recv, f_send, f_recv,
+    s_send, s_recv, w_send, w_recv, f_send, f_recv, round_z, round_x,
 ):
     rows = grad.shape[0]
     groups = rows // GROUP
@@ -89,6 +89,16 @@
     def bytes_of(ref, send, recv):
         return copy(ref, ref, send, recv, sibling)
 
+    def greet(semaphore, peers):
+        for peer in peers:
+            pl.semaphore_signal(
+                semaphore, inc=1, device_id=(peer,), device_id_type=MESH
+            )
+
+    line = {axis: [along(axis, k) for k in (1, 2, 3)] for axis in "xzy"}
+    barrier = pltpu.get_barrier_semaphore()
+    greet(barrier, [sibling, *line["y"], *line["z"], *line["x"]])
+
     list_load = pltpu.make_async_copy(lists_hbm.at[0], lists, list_sem)
     list_load.start()
     for a, source in enumerate((master_hbm, first_hbm, second_hbm)):
@@ -111,14 +121,6 @@
         return 0
 
     lax.fori_loop(0, chunks, load, 0)
-
-    barrier = pltpu.get_barrier_semaphore()
-    pl.semaphore_signal(barrier, inc=1, device_id=(sibling,), device_id_type=MESH)
-    each(
-        lambda k: pl.semaphore_signal(
-            barrier, inc=1, device_id=(far(k)[1],), device_id_type=MESH
-        )
-    )
 
     list_load.wait()
 
@@ -161,7 +163,8 @@
     own_rows = pl.ds(pl.multiple_of(c * 64, 64), 64)
     state_rows[:, own_rows, :] = raw[c]
 
-    pl.semaphore_wait(barrier, chips)
+    pl.semaphore_wait(barrier, 10)
+    greet(round_z, line["z"])
 
     raw_swap = copy(
         raw.at[1 - c], state_rows.at[:, own_rows], raw_send, raw_recv, sibling
@@ -226,13 +229,6 @@
             g = i * (CHUNK // GROUP) + j
             span = pl.ds(pl.multiple_of(g * GROUP, GROUP), GROUP)
             value = grad[span, :].astype(F32) + err[0, span, :]
-            stays = 1.0 - sent[pl.ds(g, 1), :]
-            mask = jnp.dot(
-                jnp.where(diagonal, stays, 0.0).astype(BF16),
-                jnp.ones((GROUP, value.shape[1]), BF16),
-                preferred_element_type=F32,
-            )
-            err[0, span, :] = value * mask
             value_b[j * GROUP : (j + 1) * GROUP, :] = value.astype(BF16)
             each_row.append(kept[pl.ds(g, 1), :])
         for q in range(keep_n // SPAN):
@@ -247,7 +243,23 @@
             )
         return 0
 
+    def settle(i, _):
+        for j in range(CHUNK // GROUP):
+            g = i * (CHUNK // GROUP) + j
+            span = pl.ds(pl.multiple_of(g * GROUP, GROUP), GROUP)
+            stays = 1.0 - sent[pl.ds(g, 1), :]
+            mask = jnp.dot(
+                jnp.where(diagonal, stays, 0.0).astype(BF16),
+                jnp.ones((GROUP, err.shape[2]), BF16),
+                preferred_element_type=F32,
+            )
+            err[0, span, :] = (grad[span, :].astype(F32) + err[0, span, :]) * mask
+        return 0
+
     lax.fori_loop(0, chunks // 4, pack, 0)
+
+    pl.semaphore_wait(round_z, 3)
+    greet(round_x, line["x"])
 
     raw_swap.wait_recv()
     split = []
@@ -301,13 +313,15 @@
 
     state_phase(0, state, sgot1)
 
+    lax.fori_loop(chunks // 4, chunks // 2, pack, 0)
+
     for s in range(3):
         arrive(0, s)
     spread(1)
     for s in range(3):
         forward(0, s)
 
-    lax.fori_loop(chunks // 4, chunks, pack, 0)
+    lax.fori_loop(chunks // 2, chunks, pack, 0)
 
     for h in range(2):
         packed[h] = (
@@ -319,6 +333,8 @@
     state_sum(0, state, sgot1, state1)
     state_phase(1, state1, sgot2)
 
+    pl.semaphore_wait(round_x, 3)
+
     swap.wait_recv()
     part[...] = (packed[c].astype(F32) + from_core[...].astype(F32)).astype(BF16)
 
@@ -339,6 +355,7 @@
     state_phase(2, state2, sgot3)
     state_sum(2, state2, sgot3, state3)
 
+    lax.fori_loop(0, chunks // 2, settle, 0)
     scattered = bytes_of(got, rs_send, rs_recv)
     scattered.wait_recv()
     summed = (own + jnp.sum(got[...].astype(F32), axis=0)).astype(BF16)
@@ -357,6 +374,7 @@
         return copy(block, block, half_send, half_recv, sibling)
 
     each(lambda k: gather(k).start())
+    lax.fori_loop(chunks // 2, chunks, settle, 0)
 
     for s in range(3):
         arrive(2, s)
@@ -501,6 +519,7 @@
             dma((9,)), dma((9,)),
             dma((9,)), dma((9,)),
             dma((10,)), dma((10,)),
+            pltpu.SemaphoreType.REGULAR, pltpu.SemaphoreType.REGULAR,
         ],
         compiler_params=pltpu.CompilerParams(
             collective_id=0, has_side_effects=True, vmem_limit_bytes=46 * MIB

time: 56.6 us -> 54.8 us (0.968)
  Pallas kernels: 55.8 us -> 54 us
    pallas_call x1, Pallas kernels: 49 us -> 47.3 us  [body(): pl.pallas_call(merge_kernel, out_shape=(pltpu.VMEM((1, rows, width), F32)...]
where the time goes in v5:
time: 54.8 us; the launch traced here: 54.7 us
  Pallas kernels  54 us (99%)
  between operations  0.69 us (1%)
    pallas_call x1, Pallas kernels, body(): pl.pallas_call(merge_kernel, out_shape=(pltpu.VMEM((1, rows, width), F32)...  47.3 us
    pallas_call x1, Pallas kernels, body(): pl.pallas_call(finish_kernel, out_shape=(jax.ShapeDtypeStruct((1, rows, w...  6.76 us

profile of v5, /device:TPU:1, one launch (start us, length us, event | category | flops | bytes accessed | tf_op | source)
XLA Modules:
  0.0 54.7 jit_solution(4227783196480317100)
XLA Ops:
  0.6 0.0 copy-start.2
  0.6 0.0 copy-start.1
  0.7 0.0 copy-start
  0.7 47.3 %merge.1 = (f32[1,8192,256]{2,1,0:T(8,128)S(1)}, bf16[4,4,4,2,2,64,128]{6,5,4,3,2,1,0:T(8,128)(2,1)S(1)}, bf16[2,64,2,16,128]{4,3,2,1,0:T(8,128)(2,1)S(1)}, bf16...) custom-call(bf16[1,8192,256]{2,1,0:T(8,128)(2,1)} %grad_hbm.1, f32[1,8192,256]{2,1,0:T(8,128)} %err_hbm.1, ...), custom_call_target="tpu_custom_call" | custom-call | tf_op jit(solution)/shard_map/merge/pallas_call | solution.py:483
  47.9 0.0 copy-done.2
  48.0 0.0 copy-done.1
  48.0 0.0 copy-done
  48.0 6.8 %finish.1 = (f32[1,8192,256]{2,1,0:T(8,128)}, bf16[64,128,256]{2,1,0:T(8,128)(2,1)}, f32[64,256]{1,0:T(8,128)}, f32[64,256]{1,0:T(8,128)}, f32[64,256]{1,0:T(8,128)}) custom-call(f32[1,8192,256]{2,1,0:T(8,128)S(1)} %get-tuple-element.16.err, bf16[64,2,2,64,128]{4,3,2,1,0:T(8,128)(2,1)S(1)} %bitcast.2, ...), custom_call_target="tpu_custom_call" | custom-call | tf_op jit(solution)/shard_map/finish/pallas_call | solution.py:530
Async XLA Ops:
  0.6 47.3 %copy-start.2 = (f32[64,256]{1,0:T(8,128)S(1)}, f32[64,256]{1,0:T(8,128)}, u32[]{:S(2)}) copy-start(f32[64,256]{1,0:T(8,128)} %second.1) | copy-start | bytes 196612
  0.6 47.3 %copy-start.1 = (f32[64,256]{1,0:T(8,128)S(1)}, f32[64,256]{1,0:T(8,128)}, u32[]{:S(2)}) copy-start(f32[64,256]{1,0:T(8,128)} %first.1) | copy-start | bytes 196612
  0.7 47.3 %copy-start = (f32[64,256]{1,0:T(8,128)S(1)}, f32[64,256]{1,0:T(8,128)}, u32[]{:S(2)}) copy-start(f32[64,256]{1,0:T(8,128)} %master.1) | copy-start | bytes 196612

commit v6 on v5

--- a/solution.py
+++ b/solution.py
@@ -18,6 +18,7 @@
 SPAN = 256
 
 ORDERS = ("xzy", "zyx", "yxz")
+STATE_ORDERS = ("zyx", "xzy", "yxz")
 
 
 def iota(shape, dim):
@@ -44,7 +45,8 @@
     err, weights, result, expand, rooted, starts,
     grad, lists, raw, state_rows, acc, sent, kept, column, value_b,
     packed, from_core, part, got,
-    state, state1, state2, state3, sgot1, sgot2, sgot3,
+    master0, master1, master2, master3, mgot1, mgot2, mgot3,
+    moment0, moment1, moment2, moment3, vgot1, vgot2, vgot3,
     grad_sem, err_sem, list_sem, raw_sem,
     core_send, core_recv, raw_send, raw_recv,
     rs_send, rs_recv, ag_send, ag_recv, half_send, half_recv,
@@ -89,6 +91,17 @@
     def bytes_of(ref, send, recv):
         return copy(ref, ref, send, recv, sibling)
 
+    def three(master_ref, moments_ref):
+        return master_ref, moments_ref.at[0], moments_ref.at[1]
+
+    state = three(master0, moment0)
+    state1 = three(master1, moment1)
+    state2 = three(master2, moment2)
+    state3 = three(master3, moment3)
+    sgot1 = three(mgot1, vgot1)
+    sgot2 = three(mgot2, vgot2)
+    sgot3 = three(mgot3, vgot3)
+
     def greet(semaphore, peers):
         for peer in peers:
             pl.semaphore_signal(
@@ -121,6 +134,64 @@
         return 0
 
     lax.fori_loop(0, chunks, load, 0)
+
+    pltpu.make_async_copy(raw, raw, raw_sem).wait()
+    for h in range(2):
+        new_master, _, _ = adamw(raw[h, 0], raw[h, 1], raw[h, 2], 0.0)
+        weights[x, z, y, c, h] = new_master.astype(BF16)
+    own_rows = pl.ds(pl.multiple_of(c * 64, 64), 64)
+    state_rows[:, own_rows, :] = raw[c]
+
+    pl.semaphore_wait(barrier, 10)
+    greet(round_z, line["z"])
+
+    raw_swap = copy(
+        raw.at[1 - c], state_rows.at[:, own_rows], raw_send, raw_recv, sibling
+    )
+    raw_swap.start()
+
+    parts = (
+        ((0,), pl.ds(0, 48)),
+        ((1,), pl.ds(0, 48)),
+        ((pl.ds(0, 2),), pl.ds(48, 16)),
+    )
+
+    def region(s, taken, place):
+        cols, span = parts[s]
+        index = tuple(pl.ds(0, 4) if axis in taken else place[axis] for axis in "xzy")
+        return weights.at[(*index, c, *cols, span)]
+
+    def triple(s, phase, sends, recvs):
+        order = ORDERS[s]
+        block = region(s, order[:phase], {**at, order[phase]: pl.ds(0, 3)})
+        n = s * 3 + phase
+        return bytes_of(block, sends.at[n], recvs.at[n])
+
+    def spread(phase):
+        for s, order in enumerate(ORDERS):
+            axis = order[phase]
+            block = region(s, order[:phase], at)
+            n = s * 3 + phase
+            for k in (1, 2, 3):
+                copy(
+                    block, block, w_send.at[n], w_recv.at[n], along(axis, k)
+                ).start()
+
+    def arrive(phase, s):
+        triple(s, phase, w_send, w_recv).wait_recv()
+
+    def forward(phase, s):
+        order = ORDERS[s]
+        axis = order[phase]
+        n = s * 3 + phase
+        for k in (1, 2, 3):
+            block = region(s, order[:phase], {**at, axis: (at[axis] + k) % 4})
+            copy(block, block, f_send.at[n], f_recv.at[n], sibling).start()
+
+    spread(0)
+    mine = weights.at[x, z, y, c]
+    own_forward = copy(mine, mine, f_send.at[9], f_recv.at[9], sibling)
+    own_forward.start()
 
     list_load.wait()
 
@@ -150,69 +221,6 @@
     kept[...] = jnp.where(keep * root > 0.5, rank, -1.0)
 
     chip_ranks = rooted[pl.ds(chip, 1), :]
-    column[...] = jnp.transpose(jnp.broadcast_to(chip_ranks, (GROUP, GROUP)))
-    half = column[pl.ds(pl.multiple_of(c * 64, 64), 64), :]
-    for k in range(keep_n // GROUP):
-        lanes = (iota((64, GROUP), 1) + k * GROUP).astype(F32)
-        expand[:, k * GROUP : (k + 1) * GROUP] = onehot(half == lanes)
-
-    pltpu.make_async_copy(raw, raw, raw_sem).wait()
-    for h in range(2):
-        new_master, _, _ = adamw(raw[h, 0], raw[h, 1], raw[h, 2], 0.0)
-        weights[x, z, y, c, h] = jnp.where(half < 0.0, new_master, 0.0).astype(BF16)
-    own_rows = pl.ds(pl.multiple_of(c * 64, 64), 64)
-    state_rows[:, own_rows, :] = raw[c]
-
-    pl.semaphore_wait(barrier, 10)
-    greet(round_z, line["z"])
-
-    raw_swap = copy(
-        raw.at[1 - c], state_rows.at[:, own_rows], raw_send, raw_recv, sibling
-    )
-    raw_swap.start()
-
-    parts = (
-        ((0,), pl.ds(0, 48)),
-        ((1,), pl.ds(0, 48)),
-        ((pl.ds(0, 2),), pl.ds(48, 16)),
-    )
-
-    def region(s, taken, place):
-        cols, span = parts[s]
-        index = tuple(pl.ds(0, 4) if axis in taken else place[axis] for axis in "xzy")
-        return weights.at[(*index, c, *cols, span)]
-
-    def triple(s, phase, sends, recvs):
-        order = ORDERS[s]
-        block = region(s, order[:phase], {**at, order[phase]: pl.ds(0, 3)})
-        n = s * 3 + phase
-        return bytes_of(block, sends.at[n], recvs.at[n])
-
-    def spread(phase):
-        for s, order in enumerate(ORDERS):
-            axis = order[phase]
-            block = region(s, order[:phase], at)
-            n = s * 3 + phase
-            for k in (1, 2, 3):
-                copy(
-                    block, block, w_send.at[n], w_recv.at[n], along(axis, k)
-                ).start()
-
-    def arrive(phase, s):
-        triple(s, phase, w_send, w_recv).wait_recv()
-
-    def forward(phase, s):
-        order = ORDERS[s]
-        axis = order[phase]
-        n = s * 3 + phase
-        for k in (1, 2, 3):
-            block = region(s, order[:phase], {**at, axis: (at[axis] + k) % 4})
-            copy(block, block, f_send.at[n], f_recv.at[n], sibling).start()
-
-    spread(0)
-    mine = weights.at[x, z, y, c]
-    own_forward = copy(mine, mine, f_send.at[9], f_recv.at[9], sibling)
-    own_forward.start()
 
     acc[...] = jnp.zeros_like(acc)
     diagonal = iota((GROUP, GROUP), 0) == iota((GROUP, GROUP), 1)
@@ -262,54 +270,56 @@
     greet(round_x, line["x"])
 
     raw_swap.wait_recv()
-    split = []
-    for a in range(3):
-        whole = state_rows[a]
-        high = whole.astype(BF16)
-        rest = whole - high.astype(F32)
-        middle = rest.astype(BF16)
-        low = (rest - middle.astype(F32)).astype(BF16)
-        split += [high, middle, low]
-    split = jnp.concatenate(split, axis=1)
+    whole = state_rows[0]
+    high = whole.astype(BF16)
+    rest = whole - high.astype(F32)
+    middle = rest.astype(BF16)
+    low = (rest - middle.astype(F32)).astype(BF16)
+    moments = [state_rows[a].astype(BF16) for a in (1, 2)]
+    split = jnp.concatenate([high, middle, low, *moments], axis=1)
 
     def place(i, _):
         hits = onehot(chip_ranks == (iota((128, GROUP), 0) + i * 128).astype(F32))
         moved = jnp.dot(hits, split, preferred_element_type=F32)
-        for a, order in enumerate(ORDERS):
-            high, middle, low = (
-                moved[:, (3 * a + p) * 128 : (3 * a + p + 1) * 128] for p in range(3)
-            )
-            exact = ((high + middle) + low).reshape(8, UNIT, 128)
+        high, middle, low, *pair = (
+            moved[:, p * 128 : (p + 1) * 128] for p in range(5)
+        )
+        values = ((high + middle) + low, *(value.astype(BF16) for value in pair))
+        for a, order in enumerate(STATE_ORDERS):
+            value = values[a].reshape(8, UNIT, 128)
             for u in range(8):
                 spot = {"x": i // 2, "z": (i % 2) * 2 + u // 4, "y": u % 4}
-                state[a, spot[order[0]], spot[order[1]], spot[order[2]]] = exact[u]
+                index = tuple(spot[axis] for axis in order)
+                if a == 0:
+                    master0[index] = value[u]
+                else:
+                    moment0[(a - 1, *index)] = value[u]
         return 0
 
     lax.fori_loop(0, keep_n // 128, place, 0)
 
     def state_phase(phase, source, target):
-        for a, order in enumerate(ORDERS):
+        for a, order in enumerate(STATE_ORDERS):
             axis = order[phase]
+            n = phase * 3 + a
             for k in (1, 2, 3):
-                go = copy(
-                    source.at[a, (at[axis] + k) % 4], target.at[a, k - 1],
-                    s_send.at[phase * 3 + a], s_recv.at[phase * 3 + a],
-                    along(axis, k),
-                )
-                go.start()
+                copy(
+                    source[a].at[(at[axis] + k) % 4], target[a].at[k - 1],
+                    s_send.at[n], s_recv.at[n], along(axis, k),
+                ).start()
 
     def state_bytes(phase, target, a):
         n = phase * 3 + a
-        return bytes_of(target.at[a], s_send.at[n], s_recv.at[n])
-
-    def state_sum(phase, source, target, result_ref):
+        return bytes_of(target[a], s_send.at[n], s_recv.at[n])
+
+    def state_sum(phase, source, target, total):
         for a in range(3):
             state_bytes(phase, target, a).wait_recv()
-        for a, order in enumerate(ORDERS):
-            value = source[a, at[order[phase]]]
+        for a, order in enumerate(STATE_ORDERS):
+            value = source[a][at[order[phase]]].astype(F32)
             for k in range(3):
-                value = value + target[a, k]
-            result_ref[a] = value
+                value = value + target[a][k].astype(F32)
+            total[a][...] = value.astype(total[a].dtype)
 
     state_phase(0, state, sgot1)
 
@@ -355,11 +365,17 @@
     state_phase(2, state2, sgot3)
     state_sum(2, state2, sgot3, state3)
 
+    column[...] = jnp.transpose(jnp.broadcast_to(chip_ranks, (GROUP, GROUP)))
+    half = column[own_rows, :]
+    for k in range(keep_n // GROUP):
+        lanes = (iota((64, GROUP), 1) + k * GROUP).astype(F32)
+        expand[:, k * GROUP : (k + 1) * GROUP] = onehot(half == lanes)
+
     lax.fori_loop(0, chunks // 2, settle, 0)
     scattered = bytes_of(got, rs_send, rs_recv)
     scattered.wait_recv()
     summed = (own + jnp.sum(got[...].astype(F32), axis=0)).astype(BF16)
-    new_master, _, _ = adamw(state3[0], state3[1], state3[2], summed.astype(F32))
+    new_master, _, _ = adamw(*(ref[...].astype(F32) for ref in state3), summed.astype(F32))
     result[c, chip, 0] = summed
     result[c, chip, 1] = new_master.astype(BF16)
 
@@ -375,10 +391,6 @@
 
     each(lambda k: gather(k).start())
     lax.fori_loop(chunks // 2, chunks, settle, 0)
-
-    for s in range(3):
-        arrive(2, s)
-        forward(2, s)
 
     for k in (3, 2, 1):
         q = (x + k) % 4
@@ -387,6 +399,10 @@
         pass_on(q).start()
     bytes_of(result.at[c, pl.ds(0, plane - 1)], ag_send, ag_recv.at[x]).wait_recv()
     pass_on(x).start()
+
+    for s in range(3):
+        arrive(2, s)
+        forward(2, s)
 
     scattered.wait_send()
     bytes_of(result.at[c, pl.ds(0, chips - 1)], ag_send, ag_recv.at[x]).wait_send()
@@ -450,16 +466,23 @@
             unit = jnp.minimum(starts[g, 0] // UNIT, units - window)
             near = rooted[pl.ds(g, 1), :] - (unit * UNIT).astype(F32)
             hits = onehot(iota((window * UNIT, GROUP), 0).astype(F32) == near)
-            for h in range(2):
-                held = result[h, pl.ds(unit, window), 1].reshape(window * UNIT, 128)
-                moved = lax.dot_general(
-                    hits, held, (((0,), (0,)), ((), ())), preferred_element_type=F32
-                )
-                for c in range(2):
-                    mine = weights[g, c, h].astype(F32) + moved[c * 64 : c * 64 + 64]
-                    out[g, c * 64 : c * 64 + 64, h * 128 : h * 128 + 128] = mine.astype(
-                        BF16
-                    )
+            held = [
+                result[h, pl.ds(unit, window), 1].reshape(window * UNIT, 128)
+                for h in range(2)
+            ]
+            held = jnp.concatenate([*held, jnp.ones_like(held[0])], axis=1)
+            moved = lax.dot_general(
+                hits, held, (((0,), (0,)), ((), ())), preferred_element_type=F32
+            )
+            for c in range(2):
+                span = slice(c * 64, c * 64 + 64)
+                reached = moved[span, 256:] > 0.5
+                for h in range(2):
+                    lanes = slice(h * 128, h * 128 + 128)
+                    before = weights[g, c, h].astype(F32)
+                    out[g, span, lanes] = jnp.where(
+                        reached, moved[span, lanes], before
+                    ).astype(BF16)
         store(i).start()
         return 0
 
@@ -506,13 +529,13 @@
             pltpu.VMEM((groups, UNIT, 128), BF16),
             pltpu.VMEM((groups, UNIT, 128), BF16),
             pltpu.VMEM((groups - 1, UNIT, 128), BF16),
-            pltpu.VMEM((3, 4, 4, 4, UNIT, 128), F32),
-            pltpu.VMEM((3, 4, 4, UNIT, 128), F32),
-            pltpu.VMEM((3, 4, UNIT, 128), F32),
-            pltpu.VMEM((3, UNIT, 128), F32),
-            pltpu.VMEM((3, 3, 4, 4, UNIT, 128), F32),
-            pltpu.VMEM((3, 3, 4, UNIT, 128), F32),
-            pltpu.VMEM((3, 3, UNIT, 128), F32),
+            *(
+                pltpu.VMEM((*lead, *shape, UNIT, 128), kind)
+                for lead, kind in (((), F32), ((2,), BF16))
+                for shape in (
+                    (4, 4, 4), (4, 4), (4,), (), (3, 4, 4), (3, 4), (3,)
+                )
+            ),
             dma((chunks,)), dma((chunks,)), dma, dma,
             dma, dma, dma, dma,
             dma, dma, dma, dma((4,)), dma, dma,

time: 54.8 us -> 56.9 us (1.038)
  Pallas kernels: 54 us -> 56.1 us
    pallas_call x1, Pallas kernels: 47.3 us -> 49.3 us  [body(): pl.pallas_call(merge_kernel, out_shape=(pltpu.VMEM((1, rows, width), F32)...]
where the time goes in v6:
time: 56.9 us; the launch traced here: 56.8 us
  Pallas kernels  56.1 us (99%)
  between operations  0.69 us (1%)
    pallas_call x1, Pallas kernels, body(): pl.pallas_call(merge_kernel, out_shape=(pltpu.VMEM((1, rows, width), F32)...  49.3 us
    pallas_call x1, Pallas kernels, body(): pl.pallas_call(finish_kernel, out_shape=(jax.ShapeDtypeStruct((1, rows, w...  6.79 us

profile of v6, /device:TPU:1, one launch (start us, length us, event | category | flops | bytes accessed | tf_op | source)
XLA Modules:
  0.0 56.8 jit_solution(3051285434336655128)
XLA Ops:
  0.6 0.0 copy-start.2
  0.6 0.0 copy-start.1
  0.7 0.0 copy-start
  0.7 49.3 %merge.1 = (f32[1,8192,256]{2,1,0:T(8,128)S(1)}, bf16[4,4,4,2,2,64,128]{6,5,4,3,2,1,0:T(8,128)(2,1)S(1)}, bf16[2,64,2,16,128]{4,3,2,1,0:T(8,128)(2,1)S(1)}, bf16...) custom-call(bf16[1,8192,256]{2,1,0:T(8,128)(2,1)} %grad_hbm.1, f32[1,8192,256]{2,1,0:T(8,128)} %err_hbm.1, ...), custom_call_target="tpu_custom_call" | custom-call | tf_op jit(solution)/shard_map/merge/pallas_call | solution.py:506
  49.9 0.0 copy-done.2
  49.9 0.0 copy-done.1
  50.0 0.0 copy-done
  50.0 6.8 %finish.1 = (f32[1,8192,256]{2,1,0:T(8,128)}, bf16[64,128,256]{2,1,0:T(8,128)(2,1)}, f32[64,256]{1,0:T(8,128)}, f32[64,256]{1,0:T(8,128)}, f32[64,256]{1,0:T(8,128)}) custom-call(f32[1,8192,256]{2,1,0:T(8,128)S(1)} %get-tuple-element.16.err, bf16[64,2,2,64,128]{4,3,2,1,0:T(8,128)(2,1)S(1)} %bitcast.2, ...), custom_call_target="tpu_custom_call" | custom-call | tf_op jit(solution)/shard_map/finish/pallas_call | solution.py:553
Async XLA Ops:
  0.6 49.3 %copy-start.2 = (f32[64,256]{1,0:T(8,128)S(1)}, f32[64,256]{1,0:T(8,128)}, u32[]{:S(2)}) copy-start(f32[64,256]{1,0:T(8,128)} %second.1) | copy-start | bytes 196612
  0.6 49.3 %copy-start.1 = (f32[64,256]{1,0:T(8,128)S(1)}, f32[64,256]{1,0:T(8,128)}, u32[]{:S(2)}) copy-start(f32[64,256]{1,0:T(8,128)} %first.1) | copy-start | bytes 196612
  0.7 49.3 %copy-start = (f32[64,256]{1,0:T(8,128)S(1)}, f32[64,256]{1,0:T(8,128)}, u32[]{:S(2)}) copy-start(f32[64,256]{1,0:T(8,128)} %master.1) | copy-start | bytes 196612

commit v7 on v6

--- a/solution.py
+++ b/solution.py
@@ -43,12 +43,12 @@
 def merge_kernel(
     grad_hbm, err_hbm, lists_hbm, master_hbm, first_hbm, second_hbm,
     err, weights, result, expand, rooted, starts,
-    grad, lists, raw, state_rows, acc, sent, kept, column, value_b,
+    grad, lists, raw, raw_b, acc, sent, kept, column, value_b,
     packed, from_core, part, got,
-    master0, master1, master2, master3, mgot1, mgot2, mgot3,
-    moment0, moment1, moment2, moment3, vgot1, vgot2, vgot3,
+    master0, master1, master2, master3, mgot2, mgot3,
+    moment0, moment1, moment2, moment3, vgot2, vgot3,
     grad_sem, err_sem, list_sem, raw_sem,
-    core_send, core_recv, raw_send, raw_recv,
+    core_send, core_recv, raw_send, raw_recv, rawb_send, rawb_recv,
     rs_send, rs_recv, ag_send, ag_recv, half_send, half_recv,
     s_send, s_recv, w_send, w_recv, f_send, f_recv, round_z, round_x,
 ):
@@ -98,7 +98,6 @@
     state1 = three(master1, moment1)
     state2 = three(master2, moment2)
     state3 = three(master3, moment3)
-    sgot1 = three(mgot1, vgot1)
     sgot2 = three(mgot2, vgot2)
     sgot3 = three(mgot3, vgot3)
 
@@ -140,15 +139,30 @@
         new_master, _, _ = adamw(raw[h, 0], raw[h, 1], raw[h, 2], 0.0)
         weights[x, z, y, c, h] = new_master.astype(BF16)
     own_rows = pl.ds(pl.multiple_of(c * 64, 64), 64)
-    state_rows[:, own_rows, :] = raw[c]
+    raw_b[...] = raw[:, 1:].astype(BF16)
+    mine_at = [at[order[0]] for order in STATE_ORDERS]
+    master0[mine_at[0], own_rows, :] = raw[c, 0]
+    for a in (1, 2):
+        moment0[a - 1, mine_at[a], own_rows, :] = raw_b[c, a - 1]
 
     pl.semaphore_wait(barrier, 10)
     greet(round_z, line["z"])
 
-    raw_swap = copy(
-        raw.at[1 - c], state_rows.at[:, own_rows], raw_send, raw_recv, sibling
-    )
-    raw_swap.start()
+    raw_swaps = [
+        copy(
+            raw.at[1 - c, 0], state[0].at[mine_at[0], own_rows],
+            raw_send, raw_recv, sibling,
+        )
+    ]
+    for a in (1, 2):
+        raw_swaps.append(
+            copy(
+                raw_b.at[1 - c, a - 1], state[a].at[mine_at[a], own_rows],
+                rawb_send.at[a - 1], rawb_recv.at[a - 1], sibling,
+            )
+        )
+    for go in raw_swaps:
+        go.start()
 
     parts = (
         ((0,), pl.ds(0, 48)),
@@ -213,6 +227,15 @@
     rank = start + inside
     starts[...] = start.astype(jnp.int32)
     rooted[...] = jnp.where(root > 0.5, rank, -1.0)
+
+    for go in raw_swaps:
+        go.wait_recv()
+    for a, order in enumerate(STATE_ORDERS):
+        block = state[a].at[mine_at[a]]
+        for k in (1, 2, 3):
+            copy(
+                block, block, s_send.at[a], s_recv.at[a], along(order[0], k)
+            ).start()
 
     keep = member(0)
     sent[...] = keep
@@ -269,34 +292,35 @@
     pl.semaphore_wait(round_z, 3)
     greet(round_x, line["x"])
 
-    raw_swap.wait_recv()
-    whole = state_rows[0]
-    high = whole.astype(BF16)
-    rest = whole - high.astype(F32)
-    middle = rest.astype(BF16)
-    low = (rest - middle.astype(F32)).astype(BF16)
-    moments = [state_rows[a].astype(BF16) for a in (1, 2)]
-    split = jnp.concatenate([high, middle, low, *moments], axis=1)
-
-    def place(i, _):
-        hits = onehot(chip_ranks == (iota((128, GROUP), 0) + i * 128).astype(F32))
+    def place(a):
+        order = STATE_ORDERS[a]
+        bytes_of(state[a].at[pl.ds(0, 3)], s_send.at[a], s_recv.at[a]).wait_recv()
+        units = {"x": 16, "z": 4, "y": 1}
+        spot = iota((16 * UNIT, GROUP), 0)
+        target = (
+            (spot // 64) * (units[order[1]] * UNIT)
+            + (spot // 16) % 4 * (units[order[2]] * UNIT)
+            + spot % 16
+            + at[order[0]] * (units[order[0]] * UNIT)
+        ).astype(F32)
+        hits = []
+        for k in range(4):
+            source = chip + (k - at[order[0]]) * units[order[0]]
+            hits.append(onehot(rooted[pl.ds(source, 1), :] == target))
+        hits = jnp.concatenate(hits, axis=1)
+        whole = state[a][...].reshape(4 * GROUP, 128)
+        if a:
+            split = whole
+        else:
+            high = whole.astype(BF16)
+            rest = whole - high.astype(F32)
+            middle = rest.astype(BF16)
+            low = (rest - middle.astype(F32)).astype(BF16)
+            split = jnp.concatenate([high, middle, low], axis=1)
         moved = jnp.dot(hits, split, preferred_element_type=F32)
-        high, middle, low, *pair = (
-            moved[:, p * 128 : (p + 1) * 128] for p in range(5)
-        )
-        values = ((high + middle) + low, *(value.astype(BF16) for value in pair))
-        for a, order in enumerate(STATE_ORDERS):
-            value = values[a].reshape(8, UNIT, 128)
-            for u in range(8):
-                spot = {"x": i // 2, "z": (i % 2) * 2 + u // 4, "y": u % 4}
-                index = tuple(spot[axis] for axis in order)
-                if a == 0:
-                    master0[index] = value[u]
-                else:
-                    moment0[(a - 1, *index)] = value[u]
-        return 0
-
-    lax.fori_loop(0, keep_n // 128, place, 0)
+        if not a:
+            moved = (moved[:, :128] + moved[:, 128:256]) + moved[:, 256:]
+        state1[a][...] = moved.astype(state1[a].dtype).reshape(state1[a].shape)
 
     def state_phase(phase, source, target):
         for a, order in enumerate(STATE_ORDERS):
@@ -321,8 +345,6 @@
                 value = value + target[a][k].astype(F32)
             total[a][...] = value.astype(total[a].dtype)
 
-    state_phase(0, state, sgot1)
-
     lax.fori_loop(chunks // 4, chunks // 2, pack, 0)
 
     for s in range(3):
@@ -330,6 +352,10 @@
     spread(1)
     for s in range(3):
         forward(0, s)
+
+    for a in range(3):
+        place(a)
+    state_phase(1, state1, sgot2)
 
     lax.fori_loop(chunks // 2, chunks, pack, 0)
 
@@ -340,9 +366,6 @@
     swap = copy(packed.at[1 - c], from_core, core_send, core_recv, sibling)
     swap.start()
 
-    state_sum(0, state, sgot1, state1)
-    state_phase(1, state1, sgot2)
-
     pl.semaphore_wait(round_x, 3)
 
     swap.wait_recv()
@@ -363,7 +386,6 @@
 
     state_sum(1, state1, sgot2, state2)
     state_phase(2, state2, sgot3)
-    state_sum(2, state2, sgot3, state3)
 
     column[...] = jnp.transpose(jnp.broadcast_to(chip_ranks, (GROUP, GROUP)))
     half = column[own_rows, :]
@@ -372,6 +394,7 @@
         expand[:, k * GROUP : (k + 1) * GROUP] = onehot(half == lanes)
 
     lax.fori_loop(0, chunks // 2, settle, 0)
+    state_sum(2, state2, sgot3, state3)
     scattered = bytes_of(got, rs_send, rs_recv)
     scattered.wait_recv()
     summed = (own + jnp.sum(got[...].astype(F32), axis=0)).astype(BF16)
@@ -406,11 +429,12 @@
 
     scattered.wait_send()
     bytes_of(result.at[c, pl.ds(0, chips - 1)], ag_send, ag_recv.at[x]).wait_send()
-    raw_swap.wait_send()
+    for go in raw_swaps:
+        go.wait_send()
     swap.wait_send()
     own_forward.wait()
     for a in range(3):
-        state_bytes(0, sgot1, a).wait_send()
+        bytes_of(state[a].at[pl.ds(0, 3)], s_send.at[a], s_recv.at[a]).wait_send()
         state_bytes(1, sgot2, a).wait_send()
         state_bytes(2, sgot3, a).wait_send()
     for phase in range(3):
@@ -519,7 +543,7 @@
             pltpu.VMEM((rows, width), BF16),
             pltpu.VMEM((levels, keep_n), jnp.int32),
             pltpu.VMEM((2, 3, owned, 128), F32),
-            pltpu.VMEM((3, GROUP, 128), F32),
+            pltpu.VMEM((2, 2, owned, 128), BF16),
             pltpu.VMEM((keep_n, width), F32),
             pltpu.VMEM((groups, GROUP), F32),
             pltpu.VMEM((groups, GROUP), F32),
@@ -530,14 +554,15 @@
             pltpu.VMEM((groups, UNIT, 128), BF16),
             pltpu.VMEM((groups - 1, UNIT, 128), BF16),
             *(
-                pltpu.VMEM((*lead, *shape, UNIT, 128), kind)
+                pltpu.VMEM((*lead, *shape, 128), kind)
                 for lead, kind in (((), F32), ((2,), BF16))
                 for shape in (
-                    (4, 4, 4), (4, 4), (4,), (), (3, 4, 4), (3, 4), (3,)
+                    (4, GROUP), (4, 4, UNIT), (4, UNIT), (UNIT,),
+                    (3, 4, UNIT), (3, UNIT),
                 )
             ),
             dma((chunks,)), dma((chunks,)), dma, dma,
-            dma, dma, dma, dma,
+            dma, dma, dma, dma, dma((2,)), dma((2,)),
             dma, dma, dma, dma((4,)), dma, dma,
             dma((9,)), dma((9,)),
             dma((9,)), dma((9,)),

time: 56.9 us -> 55.2 us (0.970)
  Pallas kernels: 56.1 us -> 54.4 us
    pallas_call x1, Pallas kernels: 49.3 us -> 47.7 us  [body(): pl.pallas_call(merge_kernel, out_shape=(pltpu.VMEM((1, rows, width), F32)...]
where the time goes in v7:
time: 55.2 us; the launch traced here: 55.1 us
  Pallas kernels  54.4 us (99%)
  between operations  0.69 us (1%)
    pallas_call x1, Pallas kernels, body(): pl.pallas_call(merge_kernel, out_shape=(pltpu.VMEM((1, rows, width), F32)...  47.7 us
    pallas_call x1, Pallas kernels, body(): pl.pallas_call(finish_kernel, out_shape=(jax.ShapeDtypeStruct((1, rows, w...  6.78 us

profile of v7, /device:TPU:1, one launch (start us, length us, event | category | flops | bytes accessed | tf_op | source)
XLA Modules:
  0.0 55.1 jit_solution(12554702903030239055)
XLA Ops:
  0.6 0.0 copy-start.2
  0.6 0.0 copy-start.1
  0.7 0.0 copy-start
  0.7 47.7 %merge.1 = (f32[1,8192,256]{2,1,0:T(8,128)S(1)}, bf16[4,4,4,2,2,64,128]{6,5,4,3,2,1,0:T(8,128)(2,1)S(1)}, bf16[2,64,2,16,128]{4,3,2,1,0:T(8,128)(2,1)S(1)}, bf16...) custom-call(bf16[1,8192,256]{2,1,0:T(8,128)(2,1)} %grad_hbm.1, f32[1,8192,256]{2,1,0:T(8,128)} %err_hbm.1, ...), custom_call_target="tpu_custom_call" | custom-call | tf_op jit(solution)/shard_map/merge/pallas_call | solution.py:530
  48.3 0.0 copy-done.2
  48.3 0.0 copy-done.1
  48.3 0.0 copy-done
  48.4 6.8 %finish.1 = (f32[1,8192,256]{2,1,0:T(8,128)}, bf16[64,128,256]{2,1,0:T(8,128)(2,1)}, f32[64,256]{1,0:T(8,128)}, f32[64,256]{1,0:T(8,128)}, f32[64,256]{1,0:T(8,128)}) custom-call(f32[1,8192,256]{2,1,0:T(8,128)S(1)} %get-tuple-element.16.err, bf16[64,2,2,64,128]{4,3,2,1,0:T(8,128)(2,1)S(1)} %bitcast.2, ...), custom_call_target="tpu_custom_call" | custom-call | tf_op jit(solution)/shard_map/finish/pallas_call | solution.py:578
Async XLA Ops:
  0.6 47.7 %copy-start.2 = (f32[64,256]{1,0:T(8,128)S(1)}, f32[64,256]{1,0:T(8,128)}, u32[]{:S(2)}) copy-start(f32[64,256]{1,0:T(8,128)} %second.1) | copy-start | bytes 196612
  0.6 47.7 %copy-start.1 = (f32[64,256]{1,0:T(8,128)S(1)}, f32[64,256]{1,0:T(8,128)}, u32[]{:S(2)}) copy-start(f32[64,256]{1,0:T(8,128)} %first.1) | copy-start | bytes 196612
  0.7 47.7 %copy-start = (f32[64,256]{1,0:T(8,128)S(1)}, f32[64,256]{1,0:T(8,128)}, u32[]{:S(2)}) copy-start(f32[64,256]{1,0:T(8,128)} %master.1) | copy-start | bytes 196612

commit v8 on v7

--- a/solution.py
+++ b/solution.py
@@ -169,42 +169,47 @@
         ((1,), pl.ds(0, 48)),
         ((pl.ds(0, 2),), pl.ds(48, 16)),
     )
-
-    def region(s, taken, place):
-        cols, span = parts[s]
+    pieces = (
+        (((0,), pl.ds(0, 16)), ((0,), pl.ds(16, 32))),
+        (((1,), pl.ds(0, 16)), ((1,), pl.ds(16, 32))),
+        (((0,), pl.ds(48, 16)), ((1,), pl.ds(48, 16))),
+    )
+
+    def region(s, stage, place):
+        cols, span = parts[s] if stage < 2 else pieces[s][stage - 2]
+        taken = ORDERS[s][: min(stage, 2)]
         index = tuple(pl.ds(0, 4) if axis in taken else place[axis] for axis in "xzy")
         return weights.at[(*index, c, *cols, span)]
 
-    def triple(s, phase, sends, recvs):
-        order = ORDERS[s]
-        block = region(s, order[:phase], {**at, order[phase]: pl.ds(0, 3)})
-        n = s * 3 + phase
+    def triple(s, stage, sends, recvs):
+        axis = ORDERS[s][min(stage, 2)]
+        n = s * 4 + stage
+        block = region(s, stage, {**at, axis: pl.ds(0, 3)})
         return bytes_of(block, sends.at[n], recvs.at[n])
 
-    def spread(phase):
+    def spread(stage):
         for s, order in enumerate(ORDERS):
-            axis = order[phase]
-            block = region(s, order[:phase], at)
-            n = s * 3 + phase
+            block = region(s, stage, at)
+            n = s * 4 + stage
             for k in (1, 2, 3):
                 copy(
-                    block, block, w_send.at[n], w_recv.at[n], along(axis, k)
+                    block, block, w_send.at[n], w_recv.at[n],
+                    along(order[min(stage, 2)], k),
                 ).start()
 
-    def arrive(phase, s):
-        triple(s, phase, w_send, w_recv).wait_recv()
-
-    def forward(phase, s):
-        order = ORDERS[s]
-        axis = order[phase]
-        n = s * 3 + phase
+    def arrive(stage, s):
+        triple(s, stage, w_send, w_recv).wait_recv()
+
+    def forward(stage, s):
+        axis = ORDERS[s][min(stage, 2)]
+        n = s * 4 + stage
         for k in (1, 2, 3):
-            block = region(s, order[:phase], {**at, axis: (at[axis] + k) % 4})
+            block = region(s, stage, {**at, axis: (at[axis] + k) % 4})
             copy(block, block, f_send.at[n], f_recv.at[n], sibling).start()
 
     spread(0)
     mine = weights.at[x, z, y, c]
-    own_forward = copy(mine, mine, f_send.at[9], f_recv.at[9], sibling)
+    own_forward = copy(mine, mine, f_send.at[12], f_recv.at[12], sibling)
     own_forward.start()
 
     list_load.wait()
@@ -378,14 +383,14 @@
     each(lambda k: scatter(k).start())
     own = packed[c, chip].astype(F32) + from_core[chip].astype(F32)
 
+    state_sum(1, state1, sgot2, state2)
+    state_phase(2, state2, sgot3)
+
     for s in range(3):
         arrive(1, s)
     spread(2)
     for s in range(3):
         forward(1, s)
-
-    state_sum(1, state1, sgot2, state2)
-    state_phase(2, state2, sgot3)
 
     column[...] = jnp.transpose(jnp.broadcast_to(chip_ranks, (GROUP, GROUP)))
     half = column[own_rows, :]
@@ -413,6 +418,10 @@
         return copy(block, block, half_send, half_recv, sibling)
 
     each(lambda k: gather(k).start())
+    spread(3)
+    for s in range(3):
+        arrive(2, s)
+        forward(2, s)
     lax.fori_loop(chunks // 2, chunks, settle, 0)
 
     for k in (3, 2, 1):
@@ -424,8 +433,8 @@
     pass_on(x).start()
 
     for s in range(3):
-        arrive(2, s)
-        forward(2, s)
+        arrive(3, s)
+        forward(3, s)
 
     scattered.wait_send()
     bytes_of(result.at[c, pl.ds(0, chips - 1)], ag_send, ag_recv.at[x]).wait_send()
@@ -437,10 +446,10 @@
         bytes_of(state[a].at[pl.ds(0, 3)], s_send.at[a], s_recv.at[a]).wait_send()
         state_bytes(1, sgot2, a).wait_send()
         state_bytes(2, sgot3, a).wait_send()
-    for phase in range(3):
+    for stage in range(4):
         for s in range(3):
-            triple(s, phase, w_send, w_recv).wait_send()
-            triple(s, phase, f_send, f_recv).wait()
+            triple(s, stage, w_send, w_recv).wait_send()
+            triple(s, stage, f_send, f_recv).wait()
     bytes_of(result.at[c], half_send, half_recv).wait()
 
 
@@ -565,8 +574,8 @@
             dma, dma, dma, dma, dma((2,)), dma((2,)),
             dma, dma, dma, dma((4,)), dma, dma,
             dma((9,)), dma((9,)),
-            dma((9,)), dma((9,)),
-            dma((10,)), dma((10,)),
+            dma((12,)), dma((12,)),
+            dma((13,)), dma((13,)),
             pltpu.SemaphoreType.REGULAR, pltpu.SemaphoreType.REGULAR,
         ],
         compiler_params=pltpu.CompilerParams(

time: 55.2 us -> 51 us (0.924)
  Pallas kernels: 54.4 us -> 50.2 us
    pallas_call x1, Pallas kernels: 47.7 us -> 43.4 us  [body(): pl.pallas_call(merge_kernel, out_shape=(pltpu.VMEM((1, rows, width), F32)...]
where the time goes in v8:
time: 51 us; the launch traced here: 50.9 us
  Pallas kernels  50.2 us (98%)
  between operations  0.69 us (1%)
    pallas_call x1, Pallas kernels, body(): pl.pallas_call(merge_kernel, out_shape=(pltpu.VMEM((1, rows, width), F32)...  43.4 us
    pallas_call x1, Pallas kernels, body(): pl.pallas_call(finish_kernel, out_shape=(jax.ShapeDtypeStruct((1, rows, w...  6.8 us

profile of v8, /device:TPU:1, one launch (start us, length us, event | category | flops | bytes accessed | tf_op | source)
XLA Modules:
  0.0 50.9 jit_solution(4159483762449756884)
XLA Ops:
  0.6 0.0 copy-start.2
  0.6 0.0 copy-start.1
  0.7 0.0 copy-start
  0.7 43.4 %merge.1 = (f32[1,8192,256]{2,1,0:T(8,128)S(1)}, bf16[4,4,4,2,2,64,128]{6,5,4,3,2,1,0:T(8,128)(2,1)S(1)}, bf16[2,64,2,16,128]{4,3,2,1,0:T(8,128)(2,1)S(1)}, bf16...) custom-call(bf16[1,8192,256]{2,1,0:T(8,128)(2,1)} %grad_hbm.1, f32[1,8192,256]{2,1,0:T(8,128)} %err_hbm.1, ...), custom_call_target="tpu_custom_call" | custom-call | tf_op jit(solution)/shard_map/merge/pallas_call | solution.py:539
  44.1 0.0 copy-done.2
  44.1 0.0 copy-done.1
  44.1 0.0 copy-done
  44.1 6.8 %finish.1 = (f32[1,8192,256]{2,1,0:T(8,128)}, bf16[64,128,256]{2,1,0:T(8,128)(2,1)}, f32[64,256]{1,0:T(8,128)}, f32[64,256]{1,0:T(8,128)}, f32[64,256]{1,0:T(8,128)}) custom-call(f32[1,8192,256]{2,1,0:T(8,128)S(1)} %get-tuple-element.16.err, bf16[64,2,2,64,128]{4,3,2,1,0:T(8,128)(2,1)S(1)} %bitcast.2, ...), custom_call_target="tpu_custom_call" | custom-call | tf_op jit(solution)/shard_map/finish/pallas_call | solution.py:587
Async XLA Ops:
  0.6 43.5 %copy-start.2 = (f32[64,256]{1,0:T(8,128)S(1)}, f32[64,256]{1,0:T(8,128)}, u32[]{:S(2)}) copy-start(f32[64,256]{1,0:T(8,128)} %second.1) | copy-start | bytes 196612
  0.6 43.5 %copy-start.1 = (f32[64,256]{1,0:T(8,128)S(1)}, f32[64,256]{1,0:T(8,128)}, u32[]{:S(2)}) copy-start(f32[64,256]{1,0:T(8,128)} %first.1) | copy-start | bytes 196612
  0.7 43.5 %copy-start = (f32[64,256]{1,0:T(8,128)S(1)}, f32[64,256]{1,0:T(8,128)}, u32[]{:S(2)}) copy-start(f32[64,256]{1,0:T(8,128)} %master.1) | copy-start | bytes 196612

commit v9 on v8

--- a/solution.py
+++ b/solution.py
@@ -134,11 +134,8 @@
 
     lax.fori_loop(0, chunks, load, 0)
 
+    own_rows = pl.ds(pl.multiple_of(c * 64, 64), 64)
     pltpu.make_async_copy(raw, raw, raw_sem).wait()
-    for h in range(2):
-        new_master, _, _ = adamw(raw[h, 0], raw[h, 1], raw[h, 2], 0.0)
-        weights[x, z, y, c, h] = new_master.astype(BF16)
-    own_rows = pl.ds(pl.multiple_of(c * 64, 64), 64)
     raw_b[...] = raw[:, 1:].astype(BF16)
     mine_at = [at[order[0]] for order in STATE_ORDERS]
     master0[mine_at[0], own_rows, :] = raw[c, 0]
@@ -170,10 +167,13 @@
         ((pl.ds(0, 2),), pl.ds(48, 16)),
     )
     pieces = (
-        (((0,), pl.ds(0, 16)), ((0,), pl.ds(16, 32))),
-        (((1,), pl.ds(0, 16)), ((1,), pl.ds(16, 32))),
+        (((0,), pl.ds(0, 16)), ((0,), pl.ds(16, 16)), ((0,), pl.ds(32, 16))),
+        (((1,), pl.ds(0, 16)), ((1,), pl.ds(16, 16)), ((1,), pl.ds(32, 16))),
         (((0,), pl.ds(48, 16)), ((1,), pl.ds(48, 16))),
     )
+
+    def streams(stage):
+        return range(2 if stage == 4 else 3)
 
     def region(s, stage, place):
         cols, span = parts[s] if stage < 2 else pieces[s][stage - 2]
@@ -183,34 +183,32 @@
 
     def triple(s, stage, sends, recvs):
         axis = ORDERS[s][min(stage, 2)]
-        n = s * 4 + stage
+        n = s * 5 + stage
         block = region(s, stage, {**at, axis: pl.ds(0, 3)})
         return bytes_of(block, sends.at[n], recvs.at[n])
 
     def spread(stage):
-        for s, order in enumerate(ORDERS):
+        for s in streams(stage):
+            order = ORDERS[s]
             block = region(s, stage, at)
-            n = s * 4 + stage
+            n = s * 5 + stage
             for k in (1, 2, 3):
                 copy(
                     block, block, w_send.at[n], w_recv.at[n],
                     along(order[min(stage, 2)], k),
                 ).start()
 
-    def arrive(stage, s):
-        triple(s, stage, w_send, w_recv).wait_recv()
-
-    def forward(stage, s):
-        axis = ORDERS[s][min(stage, 2)]
-        n = s * 4 + stage
-        for k in (1, 2, 3):
-            block = region(s, stage, {**at, axis: (at[axis] + k) % 4})
-            copy(block, block, f_send.at[n], f_recv.at[n], sibling).start()
-
-    spread(0)
-    mine = weights.at[x, z, y, c]
-    own_forward = copy(mine, mine, f_send.at[12], f_recv.at[12], sibling)
-    own_forward.start()
+    def arrive(stage):
+        for s in streams(stage):
+            triple(s, stage, w_send, w_recv).wait_recv()
+
+    def forward(stage):
+        for s in streams(stage):
+            axis = ORDERS[s][min(stage, 2)]
+            n = s * 5 + stage
+            for k in (1, 2, 3):
+                block = region(s, stage, {**at, axis: (at[axis] + k) % 4})
+                copy(block, block, f_send.at[n], f_recv.at[n], sibling).start()
 
     list_load.wait()
 
@@ -233,6 +231,17 @@
     starts[...] = start.astype(jnp.int32)
     rooted[...] = jnp.where(root > 0.5, rank, -1.0)
 
+    chip_ranks = rooted[pl.ds(chip, 1), :]
+    column[...] = jnp.transpose(jnp.broadcast_to(chip_ranks, (GROUP, GROUP)))
+    half = column[own_rows, :]
+    for h in range(2):
+        new_master, _, _ = adamw(raw[h, 0], raw[h, 1], raw[h, 2], 0.0)
+        weights[x, z, y, c, h] = jnp.where(half < 0.0, new_master, 0.0).astype(BF16)
+    spread(0)
+    mine = weights.at[x, z, y, c]
+    own_forward = copy(mine, mine, f_send.at[15], f_recv.at[15], sibling)
+    own_forward.start()
+
     for go in raw_swaps:
         go.wait_recv()
     for a, order in enumerate(STATE_ORDERS):
@@ -247,8 +256,6 @@
     for r in range(1, levels - 1):
         keep = keep * member(r)
     kept[...] = jnp.where(keep * root > 0.5, rank, -1.0)
-
-    chip_ranks = rooted[pl.ds(chip, 1), :]
 
     acc[...] = jnp.zeros_like(acc)
     diagonal = iota((GROUP, GROUP), 0) == iota((GROUP, GROUP), 1)
@@ -352,53 +359,62 @@
 
     lax.fori_loop(chunks // 4, chunks // 2, pack, 0)
 
-    for s in range(3):
-        arrive(0, s)
+    arrive(0)
     spread(1)
-    for s in range(3):
-        forward(0, s)
+    forward(0)
+
+    lax.fori_loop(chunks // 2, chunks, pack, 0)
+
+    half_chips = chips // 2
+    swaps = []
+    for p in range(2):
+        ranks = slice(p * keep_n // 2, (p + 1) * keep_n // 2)
+        span = pl.ds(p * half_chips, half_chips)
+        for h in range(2):
+            packed[h, span] = (
+                acc[ranks, h * 128 : (h + 1) * 128]
+                .astype(BF16)
+                .reshape(half_chips, UNIT, 128)
+            )
+        swap = copy(
+            packed.at[1 - c, span], from_core.at[span],
+            core_send.at[p], core_recv.at[p], sibling,
+        )
+        swap.start()
+        swaps.append(swap)
 
     for a in range(3):
         place(a)
     state_phase(1, state1, sgot2)
-
-    lax.fori_loop(chunks // 2, chunks, pack, 0)
-
-    for h in range(2):
-        packed[h] = (
-            acc[:, h * 128 : (h + 1) * 128].astype(BF16).reshape(packed.shape[1:])
-        )
-    swap = copy(packed.at[1 - c], from_core, core_send, core_recv, sibling)
-    swap.start()
-
     pl.semaphore_wait(round_x, 3)
 
-    swap.wait_recv()
-    part[...] = (packed[c].astype(F32) + from_core[...].astype(F32)).astype(BF16)
 
     def scatter(k):
         other, peer = far(k)
         return copy(part.at[other], got.at[k - 1], rs_send, rs_recv, peer)
 
+    for p in range(2):
+        swaps[p].wait_recv()
+        span = pl.ds(p * half_chips, half_chips)
+        part[span] = (packed[c, span].astype(F32) + from_core[span].astype(F32)).astype(
+            BF16
+        )
+
     each(lambda k: scatter(k).start())
     own = packed[c, chip].astype(F32) + from_core[chip].astype(F32)
 
     state_sum(1, state1, sgot2, state2)
     state_phase(2, state2, sgot3)
 
-    for s in range(3):
-        arrive(1, s)
+    arrive(1)
     spread(2)
-    for s in range(3):
-        forward(1, s)
-
-    column[...] = jnp.transpose(jnp.broadcast_to(chip_ranks, (GROUP, GROUP)))
-    half = column[own_rows, :]
+    spread(3)
+    forward(1)
+
     for k in range(keep_n // GROUP):
         lanes = (iota((64, GROUP), 1) + k * GROUP).astype(F32)
         expand[:, k * GROUP : (k + 1) * GROUP] = onehot(half == lanes)
 
-    lax.fori_loop(0, chunks // 2, settle, 0)
     state_sum(2, state2, sgot3, state3)
     scattered = bytes_of(got, rs_send, rs_recv)
     scattered.wait_recv()
@@ -418,11 +434,11 @@
         return copy(block, block, half_send, half_recv, sibling)
 
     each(lambda k: gather(k).start())
-    spread(3)
-    for s in range(3):
-        arrive(2, s)
-        forward(2, s)
-    lax.fori_loop(chunks // 2, chunks, settle, 0)
+    spread(4)
+    for stage in (2, 3):
+        arrive(stage)
+        forward(stage)
+    lax.fori_loop(0, chunks, settle, 0)
 
     for k in (3, 2, 1):
         q = (x + k) % 4
@@ -432,22 +448,22 @@
     bytes_of(result.at[c, pl.ds(0, plane - 1)], ag_send, ag_recv.at[x]).wait_recv()
     pass_on(x).start()
 
-    for s in range(3):
-        arrive(3, s)
-        forward(3, s)
+    arrive(4)
+    forward(4)
 
     scattered.wait_send()
     bytes_of(result.at[c, pl.ds(0, chips - 1)], ag_send, ag_recv.at[x]).wait_send()
     for go in raw_swaps:
         go.wait_send()
-    swap.wait_send()
+    for go in swaps:
+        go.wait_send()
     own_forward.wait()
     for a in range(3):
         bytes_of(state[a].at[pl.ds(0, 3)], s_send.at[a], s_recv.at[a]).wait_send()
         state_bytes(1, sgot2, a).wait_send()
         state_bytes(2, sgot3, a).wait_send()
-    for stage in range(4):
-        for s in range(3):
+    for stage in range(5):
+        for s in streams(stage):
             triple(s, stage, w_send, w_recv).wait_send()
             triple(s, stage, f_send, f_recv).wait()
     bytes_of(result.at[c], half_send, half_recv).wait()
@@ -470,20 +486,6 @@
         go.start()
         copies.append(go)
 
-    total = jnp.concatenate(
-        [
-            jnp.dot(
-                expand[...], result[h, :, 0].reshape(-1, 128),
-                preferred_element_type=F32,
-            )
-            for h in range(2)
-        ],
-        axis=1,
-    )
-    new_master[...], new_first[...], new_second[...] = adamw(
-        master[...], first[...], second[...], total
-    )
-
     to_smem.wait()
     units = result.shape[1]
     window = GROUP // UNIT + 1
@@ -499,28 +501,40 @@
             unit = jnp.minimum(starts[g, 0] // UNIT, units - window)
             near = rooted[pl.ds(g, 1), :] - (unit * UNIT).astype(F32)
             hits = onehot(iota((window * UNIT, GROUP), 0).astype(F32) == near)
-            held = [
-                result[h, pl.ds(unit, window), 1].reshape(window * UNIT, 128)
-                for h in range(2)
-            ]
-            held = jnp.concatenate([*held, jnp.ones_like(held[0])], axis=1)
+            held = jnp.concatenate(
+                [
+                    result[h, pl.ds(unit, window), 1].reshape(window * UNIT, 128)
+                    for h in range(2)
+                ],
+                axis=1,
+            )
             moved = lax.dot_general(
                 hits, held, (((0,), (0,)), ((), ())), preferred_element_type=F32
-            )
+            ).astype(BF16)
             for c in range(2):
                 span = slice(c * 64, c * 64 + 64)
-                reached = moved[span, 256:] > 0.5
                 for h in range(2):
                     lanes = slice(h * 128, h * 128 + 128)
-                    before = weights[g, c, h].astype(F32)
-                    out[g, span, lanes] = jnp.where(
-                        reached, moved[span, lanes], before
-                    ).astype(BF16)
+                    out[g, span, lanes] = weights[g, c, h] + moved[span, lanes]
         store(i).start()
         return 0
 
     steps = out_sem.shape[0]
     lax.fori_loop(0, steps, fill, 0)
+    total = jnp.concatenate(
+        [
+            jnp.dot(
+                expand[...], result[h, :, 0].reshape(-1, 128),
+                preferred_element_type=F32,
+            )
+            for h in range(2)
+        ],
+        axis=1,
+    )
+    new_master[...], new_first[...], new_second[...] = adamw(
+        master[...], first[...], second[...], total
+    )
+
     for go in copies:
         go.wait()
     lax.fori_loop(0, steps, lambda i, _: (store(i).wait(), 0)[1], 0)
@@ -571,11 +585,11 @@
                 )
             ),
             dma((chunks,)), dma((chunks,)), dma, dma,
-            dma, dma, dma, dma, dma((2,)), dma((2,)),
+            dma((2,)), dma((2,)), dma, dma, dma((2,)), dma((2,)),
             dma, dma, dma, dma((4,)), dma, dma,
             dma((9,)), dma((9,)),
-            dma((12,)), dma((12,)),
-            dma((13,)), dma((13,)),
+            dma((15,)), dma((15,)),
+            dma((16,)), dma((16,)),
             pltpu.SemaphoreType.REGULAR, pltpu.SemaphoreType.REGULAR,
         ],
         compiler_params=pltpu.CompilerParams(

time: 51 us -> 47.7 us (0.935)
  Pallas kernels: 50.2 us -> 46.9 us
    pallas_call x1, Pallas kernels: 43.4 us -> 41.2 us  [body(): pl.pallas_call(merge_kernel, out_shape=(pltpu.VMEM((1, rows, width), F32)...]
    pallas_call x1, Pallas kernels: 6.8 us -> 5.73 us  [body(): pl.pallas_call(finish_kernel, out_shape=(jax.ShapeDtypeStruct((1, rows, w...]
where the time goes in v9:
time: 47.7 us; the launch traced here: 47.6 us
  Pallas kernels  46.9 us (98%)
  between operations  0.69 us (1%)
    pallas_call x1, Pallas kernels, body(): pl.pallas_call(merge_kernel, out_shape=(pltpu.VMEM((1, rows, width), F32)...  41.2 us
    pallas_call x1, Pallas kernels, body(): pl.pallas_call(finish_kernel, out_shape=(jax.ShapeDtypeStruct((1, rows, w...  5.73 us

profile of v9, /device:TPU:1, one launch (start us, length us, event | category | flops | bytes accessed | tf_op | source)
XLA Modules:
  0.0 47.6 jit_solution(8697979704036594235)
XLA Ops:
  0.6 0.0 copy-start.2
  0.6 0.0 copy-start.1
  0.7 0.0 copy-start
  0.7 41.2 %merge.1 = (f32[1,8192,256]{2,1,0:T(8,128)S(1)}, bf16[4,4,4,2,2,64,128]{6,5,4,3,2,1,0:T(8,128)(2,1)S(1)}, bf16[2,64,2,16,128]{4,3,2,1,0:T(8,128)(2,1)S(1)}, bf16...) custom-call(bf16[1,8192,256]{2,1,0:T(8,128)(2,1)} %grad_hbm.1, f32[1,8192,256]{2,1,0:T(8,128)} %err_hbm.1, ...), custom_call_target="tpu_custom_call" | custom-call | tf_op jit(solution)/shard_map/merge/pallas_call | solution.py:553
  41.8 0.0 copy-done.2
  41.9 0.0 copy-done.1
  41.9 0.0 copy-done
  41.9 5.7 %finish.1 = (f32[1,8192,256]{2,1,0:T(8,128)}, bf16[64,128,256]{2,1,0:T(8,128)(2,1)}, f32[64,256]{1,0:T(8,128)}, f32[64,256]{1,0:T(8,128)}, f32[64,256]{1,0:T(8,128)}) custom-call(f32[1,8192,256]{2,1,0:T(8,128)S(1)} %get-tuple-element.16.err, bf16[64,2,2,64,128]{4,3,2,1,0:T(8,128)(2,1)S(1)} %bitcast.2, ...), custom_call_target="tpu_custom_call" | custom-call | tf_op jit(solution)/shard_map/finish/pallas_call | solution.py:601
Async XLA Ops:
  0.6 41.2 %copy-start.2 = (f32[64,256]{1,0:T(8,128)S(1)}, f32[64,256]{1,0:T(8,128)}, u32[]{:S(2)}) copy-start(f32[64,256]{1,0:T(8,128)} %second.1) | copy-start | bytes 196612
  0.6 41.2 %copy-start.1 = (f32[64,256]{1,0:T(8,128)S(1)}, f32[64,256]{1,0:T(8,128)}, u32[]{:S(2)}) copy-start(f32[64,256]{1,0:T(8,128)} %first.1) | copy-start | bytes 196612
  0.7 41.2 %copy-start = (f32[64,256]{1,0:T(8,128)S(1)}, f32[64,256]{1,0:T(8,128)}, u32[]{:S(2)}) copy-start(f32[64,256]{1,0:T(8,128)} %master.1) | copy-start | bytes 196612

commit v10 on v9

--- a/solution.py
+++ b/solution.py
@@ -81,12 +81,12 @@
         )
 
     def each(act):
-        def nine(i, _):
-            for j in range(9):
-                act(i * 9 + j + 1)
+        def some(i, _):
+            for j in range(21):
+                act(i * 21 + j + 1)
             return 0
 
-        lax.fori_loop(0, (chips - 1) // 9, nine, 0)
+        lax.fori_loop(0, (chips - 1) // 21, some, 0)
 
     def bytes_of(ref, send, recv):
         return copy(ref, ref, send, recv, sibling)
@@ -212,12 +212,28 @@
 
     list_load.wait()
 
+    ids = lists[...]
+    high_ids = (ids >> 7).astype(F32)
+    low_ids = (ids & 127).astype(F32)
+
+    inner = iota((SPAN // 16, 16, GROUP), 0) * 16 + iota((SPAN // 16, 16, GROUP), 1)
+    inner = inner.astype(F32).astype(BF16)
+    one = jnp.ones((SPAN // 16, 16, GROUP), BF16)
+    zero = jnp.zeros((SPAN // 16, 16, GROUP), BF16)
+
+    def ladder(row, count):
+        tiles = count // 16
+        near = jnp.broadcast_to(row, (16, GROUP)).astype(BF16)
+        hit = jnp.where(inner[:tiles] == near[None], one[:tiles], zero[:tiles])
+        return hit.reshape(count, GROUP)
+
     def member(r):
-        ids = lists[r : r + 1, :]
-        high = onehot(iota((groups, keep_n), 0) == ids // GROUP)
-        low = onehot(iota((GROUP, keep_n), 0) == ids % GROUP)
+        spans = [slice(j, j + GROUP) for j in range(0, keep_n, GROUP)]
+        high = [ladder(high_ids[r : r + 1, span], groups) for span in spans]
+        low = [ladder(low_ids[r : r + 1, span], GROUP) for span in spans]
         return lax.dot_general(
-            high, low, (((1,), (1,)), ((), ())), preferred_element_type=F32
+            jnp.concatenate(high, axis=1), jnp.concatenate(low, axis=1),
+            (((1,), (1,)), ((), ())), preferred_element_type=F32,
         )
 
     root = member(levels - 1)
@@ -259,10 +275,6 @@
 
     acc[...] = jnp.zeros_like(acc)
     diagonal = iota((GROUP, GROUP), 0) == iota((GROUP, GROUP), 1)
-    inner = iota((SPAN // 16, 16, GROUP), 0) * 16 + iota((SPAN // 16, 16, GROUP), 1)
-    inner = inner.astype(F32).astype(BF16)
-    one = jnp.ones((SPAN // 16, 16, GROUP), BF16)
-    zero = jnp.zeros((SPAN // 16, 16, GROUP), BF16)
 
     def pack(i, _):
         for go in loads(i):
@@ -277,10 +289,7 @@
         for q in range(keep_n // SPAN):
             hits = []
             for row in each_row:
-                near = jnp.clip(row - q * SPAN, -1.0, SPAN)
-                near = jnp.broadcast_to(near, (16, GROUP)).astype(BF16)
-                hit = jnp.where(inner == near[None], one, zero)
-                hits.append(hit.reshape(SPAN, GROUP))
+                hits.append(ladder(jnp.clip(row - q * SPAN, -1.0, SPAN), SPAN))
             acc[q * SPAN : (q + 1) * SPAN, :] += jnp.dot(
                 jnp.concatenate(hits, axis=1), value_b[...], preferred_element_type=F32
             )

time: 47.7 us -> 47.8 us (level)
  no operation moved by 1% of the time
where the time goes in v10:
time: 47.8 us; the launch traced here: 47.7 us
  Pallas kernels  47 us (98%)
  between operations  0.69 us (1%)
    pallas_call x1, Pallas kernels, body(): pl.pallas_call(merge_kernel, out_shape=(pltpu.VMEM((1, rows, width), F32)...  41.2 us
    pallas_call x1, Pallas kernels, body(): pl.pallas_call(finish_kernel, out_shape=(jax.ShapeDtypeStruct((1, rows, w...  5.72 us

profile of v10, /device:TPU:1, one launch (start us, length us, event | category | flops | bytes accessed | tf_op | source)
XLA Modules:
  0.0 47.7 jit_solution(11602186079165754154)
XLA Ops:
  0.6 0.0 copy-start.2
  0.6 0.0 copy-start.1
  0.7 0.0 copy-start
  0.7 41.2 %merge.1 = (f32[1,8192,256]{2,1,0:T(8,128)S(1)}, bf16[4,4,4,2,2,64,128]{6,5,4,3,2,1,0:T(8,128)(2,1)S(1)}, bf16[2,64,2,16,128]{4,3,2,1,0:T(8,128)(2,1)S(1)}, bf16...) custom-call(bf16[1,8192,256]{2,1,0:T(8,128)(2,1)} %grad_hbm.1, f32[1,8192,256]{2,1,0:T(8,128)} %err_hbm.1, ...), custom_call_target="tpu_custom_call" | custom-call | tf_op jit(solution)/shard_map/merge/pallas_call | solution.py:562
  41.9 0.0 copy-done.2
  41.9 0.0 copy-done.1
  41.9 0.0 copy-done
  41.9 5.7 %finish.1 = (f32[1,8192,256]{2,1,0:T(8,128)}, bf16[64,128,256]{2,1,0:T(8,128)(2,1)}, f32[64,256]{1,0:T(8,128)}, f32[64,256]{1,0:T(8,128)}, f32[64,256]{1,0:T(8,128)}) custom-call(f32[1,8192,256]{2,1,0:T(8,128)S(1)} %get-tuple-element.16.err, bf16[64,2,2,64,128]{4,3,2,1,0:T(8,128)(2,1)S(1)} %bitcast.2, ...), custom_call_target="tpu_custom_call" | custom-call | tf_op jit(solution)/shard_map/finish/pallas_call | solution.py:610
Async XLA Ops:
  0.6 41.3 %copy-start.2 = (f32[64,256]{1,0:T(8,128)S(1)}, f32[64,256]{1,0:T(8,128)}, u32[]{:S(2)}) copy-start(f32[64,256]{1,0:T(8,128)} %second.1) | copy-start | bytes 196612
  0.6 41.3 %copy-start.1 = (f32[64,256]{1,0:T(8,128)S(1)}, f32[64,256]{1,0:T(8,128)}, u32[]{:S(2)}) copy-start(f32[64,256]{1,0:T(8,128)} %first.1) | copy-start | bytes 196612
  0.7 41.3 %copy-start = (f32[64,256]{1,0:T(8,128)S(1)}, f32[64,256]{1,0:T(8,128)}, u32[]{:S(2)}) copy-start(f32[64,256]{1,0:T(8,128)} %master.1) | copy-start | bytes 196612

commit v11 on v10

--- a/solution.py
+++ b/solution.py
@@ -13,7 +13,7 @@
 MIB = 1 << 20
 
 GROUP = 128
-CHUNK = 1024
+CHUNK = 2048
 UNIT = 16
 SPAN = 256
 
@@ -134,33 +134,6 @@
 
     lax.fori_loop(0, chunks, load, 0)
 
-    own_rows = pl.ds(pl.multiple_of(c * 64, 64), 64)
-    pltpu.make_async_copy(raw, raw, raw_sem).wait()
-    raw_b[...] = raw[:, 1:].astype(BF16)
-    mine_at = [at[order[0]] for order in STATE_ORDERS]
-    master0[mine_at[0], own_rows, :] = raw[c, 0]
-    for a in (1, 2):
-        moment0[a - 1, mine_at[a], own_rows, :] = raw_b[c, a - 1]
-
-    pl.semaphore_wait(barrier, 10)
-    greet(round_z, line["z"])
-
-    raw_swaps = [
-        copy(
-            raw.at[1 - c, 0], state[0].at[mine_at[0], own_rows],
-            raw_send, raw_recv, sibling,
-        )
-    ]
-    for a in (1, 2):
-        raw_swaps.append(
-            copy(
-                raw_b.at[1 - c, a - 1], state[a].at[mine_at[a], own_rows],
-                rawb_send.at[a - 1], rawb_recv.at[a - 1], sibling,
-            )
-        )
-    for go in raw_swaps:
-        go.start()
-
     parts = (
         ((0,), pl.ds(0, 48)),
         ((1,), pl.ds(0, 48)),
@@ -181,34 +154,35 @@
         index = tuple(pl.ds(0, 4) if axis in taken else place[axis] for axis in "xzy")
         return weights.at[(*index, c, *cols, span)]
 
-    def triple(s, stage, sends, recvs):
-        axis = ORDERS[s][min(stage, 2)]
-        n = s * 5 + stage
-        block = region(s, stage, {**at, axis: pl.ds(0, 3)})
-        return bytes_of(block, sends.at[n], recvs.at[n])
+    def stage_bytes(stage, sends, recvs):
+        three_of = (
+            weights.at[0, 0, pl.ds(0, 3), c],
+            weights.at[0, pl.ds(0, 3), :, c],
+            weights.at[pl.ds(0, 3), :, :, c, 0, pl.ds(0, 48)],
+            weights.at[pl.ds(0, 3), :, :, c, 0, pl.ds(0, 48)],
+            weights.at[pl.ds(0, 3), :, :, c, 0, pl.ds(0, 32)],
+        )
+        return bytes_of(three_of[stage], sends.at[stage], recvs.at[stage])
 
     def spread(stage):
         for s in streams(stage):
             order = ORDERS[s]
             block = region(s, stage, at)
-            n = s * 5 + stage
             for k in (1, 2, 3):
                 copy(
-                    block, block, w_send.at[n], w_recv.at[n],
+                    block, block, w_send.at[stage], w_recv.at[stage],
                     along(order[min(stage, 2)], k),
                 ).start()
 
     def arrive(stage):
-        for s in streams(stage):
-            triple(s, stage, w_send, w_recv).wait_recv()
+        stage_bytes(stage, w_send, w_recv).wait_recv()
 
     def forward(stage):
         for s in streams(stage):
             axis = ORDERS[s][min(stage, 2)]
-            n = s * 5 + stage
             for k in (1, 2, 3):
                 block = region(s, stage, {**at, axis: (at[axis] + k) % 4})
-                copy(block, block, f_send.at[n], f_recv.at[n], sibling).start()
+                copy(block, block, f_send, f_recv, sibling).start()
 
     list_load.wait()
 
@@ -247,36 +221,30 @@
     starts[...] = start.astype(jnp.int32)
     rooted[...] = jnp.where(root > 0.5, rank, -1.0)
 
-    chip_ranks = rooted[pl.ds(chip, 1), :]
-    column[...] = jnp.transpose(jnp.broadcast_to(chip_ranks, (GROUP, GROUP)))
-    half = column[own_rows, :]
-    for h in range(2):
-        new_master, _, _ = adamw(raw[h, 0], raw[h, 1], raw[h, 2], 0.0)
-        weights[x, z, y, c, h] = jnp.where(half < 0.0, new_master, 0.0).astype(BF16)
-    spread(0)
-    mine = weights.at[x, z, y, c]
-    own_forward = copy(mine, mine, f_send.at[15], f_recv.at[15], sibling)
-    own_forward.start()
-
-    for go in raw_swaps:
-        go.wait_recv()
-    for a, order in enumerate(STATE_ORDERS):
-        block = state[a].at[mine_at[a]]
-        for k in (1, 2, 3):
-            copy(
-                block, block, s_send.at[a], s_recv.at[a], along(order[0], k)
-            ).start()
-
     keep = member(0)
     sent[...] = keep
     for r in range(1, levels - 1):
         keep = keep * member(r)
     kept[...] = jnp.where(keep * root > 0.5, rank, -1.0)
 
+    chip_ranks = rooted[pl.ds(chip, 1), :]
+    column[...] = jnp.transpose(jnp.broadcast_to(chip_ranks, (GROUP, GROUP)))
+    own_rows = pl.ds(pl.multiple_of(c * 64, 64), 64)
+    half = column[own_rows, :]
+    pltpu.make_async_copy(raw, raw, raw_sem).wait()
+    raw_b[...] = raw[:, 1:].astype(BF16)
+    mine_at = [at[order[0]] for order in STATE_ORDERS]
+    master0[mine_at[0], own_rows, :] = raw[c, 0]
+    for a in (1, 2):
+        moment0[a - 1, mine_at[a], own_rows, :] = raw_b[c, a - 1]
+
+    for h in range(2):
+        new_master, _, _ = adamw(raw[h, 0], raw[h, 1], raw[h, 2], 0.0)
+        weights[x, z, y, c, h] = jnp.where(half < 0.0, new_master, 0.0).astype(BF16)
     acc[...] = jnp.zeros_like(acc)
     diagonal = iota((GROUP, GROUP), 0) == iota((GROUP, GROUP), 1)
 
-    def pack(i, _):
+    def pack(i):
         for go in loads(i):
             go.wait()
         each_row = []
@@ -293,7 +261,6 @@
             acc[q * SPAN : (q + 1) * SPAN, :] += jnp.dot(
                 jnp.concatenate(hits, axis=1), value_b[...], preferred_element_type=F32
             )
-        return 0
 
     def settle(i, _):
         for j in range(CHUNK // GROUP):
@@ -308,10 +275,49 @@
             err[0, span, :] = (grad[span, :].astype(F32) + err[0, span, :]) * mask
         return 0
 
-    lax.fori_loop(0, chunks // 4, pack, 0)
+    pack(0)
+    pl.semaphore_wait(barrier, 10)
+    greet(round_z, line["z"])
+
+    raw_swaps = [
+        copy(
+            raw.at[1 - c, 0], state[0].at[mine_at[0], own_rows],
+            raw_send, raw_recv, sibling,
+        )
+    ]
+    for a in (1, 2):
+        raw_swaps.append(
+            copy(
+                raw_b.at[1 - c, a - 1], state[a].at[mine_at[a], own_rows],
+                rawb_send.at[a - 1], rawb_recv.at[a - 1], sibling,
+            )
+        )
+    for go in raw_swaps:
+        go.start()
+
+    spread(0)
+    mine = weights.at[x, z, y, c]
+    copy(mine, mine, f_send, f_recv, sibling).start()
+
+    pack(1)
+
+    for go in raw_swaps:
+        go.wait_recv()
+    for a, order in enumerate(STATE_ORDERS):
+        block = state[a].at[mine_at[a]]
+        for k in (1, 2, 3):
+            copy(
+                block, block, s_send.at[a], s_recv.at[a], along(order[0], k)
+            ).start()
 
     pl.semaphore_wait(round_z, 3)
     greet(round_x, line["x"])
+    pack(2)
+
+    arrive(0)
+    spread(1)
+    forward(0)
+    pack(3)
 
     def place(a):
         order = STATE_ORDERS[a]
@@ -366,14 +372,6 @@
                 value = value + target[a][k].astype(F32)
             total[a][...] = value.astype(total[a].dtype)
 
-    lax.fori_loop(chunks // 4, chunks // 2, pack, 0)
-
-    arrive(0)
-    spread(1)
-    forward(0)
-
-    lax.fori_loop(chunks // 2, chunks, pack, 0)
-
     half_chips = chips // 2
     swaps = []
     for p in range(2):
@@ -466,15 +464,13 @@
         go.wait_send()
     for go in swaps:
         go.wait_send()
-    own_forward.wait()
     for a in range(3):
         bytes_of(state[a].at[pl.ds(0, 3)], s_send.at[a], s_recv.at[a]).wait_send()
         state_bytes(1, sgot2, a).wait_send()
         state_bytes(2, sgot3, a).wait_send()
     for stage in range(5):
-        for s in streams(stage):
-            triple(s, stage, w_send, w_recv).wait_send()
-            triple(s, stage, f_send, f_recv).wait()
+        stage_bytes(stage, w_send, w_recv).wait_send()
+    bytes_of(weights.at[:, :, :, c], f_send, f_recv).wait()
     bytes_of(result.at[c], half_send, half_recv).wait()
 
 
@@ -597,8 +593,7 @@
             dma((2,)), dma((2,)), dma, dma, dma((2,)), dma((2,)),
             dma, dma, dma, dma((4,)), dma, dma,
             dma((9,)), dma((9,)),
-            dma((15,)), dma((15,)),
-            dma((16,)), dma((16,)),
+            dma((5,)), dma((5,)), dma, dma,
             pltpu.SemaphoreType.REGULAR, pltpu.SemaphoreType.REGULAR,
         ],
         compiler_params=pltpu.CompilerParams(

time: 47.8 us -> 45.9 us (0.960)
  Pallas kernels: 47 us -> 45.1 us
    pallas_call x1, Pallas kernels: 41.2 us -> 39.3 us  [body(): pl.pallas_call(merge_kernel, out_shape=(pltpu.VMEM((1, rows, width), F32)...]
where the time goes in v11:
time: 45.9 us; the launch traced here: 45.8 us
  Pallas kernels  45.1 us (98%)
  between operations  0.69 us (2%)
    pallas_call x1, Pallas kernels, body(): pl.pallas_call(merge_kernel, out_shape=(pltpu.VMEM((1, rows, width), F32)...  39.3 us
    pallas_call x1, Pallas kernels, body(): pl.pallas_call(finish_kernel, out_shape=(jax.ShapeDtypeStruct((1, rows, w...  5.73 us

profile of v11, /device:TPU:1, one launch (start us, length us, event | category | flops | bytes accessed | tf_op | source)
XLA Modules:
  0.0 45.8 jit_solution(2850964946088401415)
XLA Ops:
  0.6 0.0 copy-start.2
  0.6 0.0 copy-start.1
  0.7 0.0 copy-start
  0.7 39.3 %merge.1 = (f32[1,8192,256]{2,1,0:T(8,128)S(1)}, bf16[4,4,4,2,2,64,128]{6,5,4,3,2,1,0:T(8,128)(2,1)S(1)}, bf16[2,64,2,16,128]{4,3,2,1,0:T(8,128)(2,1)S(1)}, bf16...) custom-call(bf16[1,8192,256]{2,1,0:T(8,128)(2,1)} %grad_hbm.1, f32[1,8192,256]{2,1,0:T(8,128)} %err_hbm.1, ...), custom_call_target="tpu_custom_call" | custom-call | tf_op jit(solution)/shard_map/merge/pallas_call | solution.py:558
  40.0 0.0 copy-done.2
  40.0 0.0 copy-done.1
  40.0 0.0 copy-done
  40.0 5.7 %finish.1 = (f32[1,8192,256]{2,1,0:T(8,128)}, bf16[64,128,256]{2,1,0:T(8,128)(2,1)}, f32[64,256]{1,0:T(8,128)}, f32[64,256]{1,0:T(8,128)}, f32[64,256]{1,0:T(8,128)}) custom-call(f32[1,8192,256]{2,1,0:T(8,128)S(1)} %get-tuple-element.16.err, bf16[64,2,2,64,128]{4,3,2,1,0:T(8,128)(2,1)S(1)} %bitcast.2, ...), custom_call_target="tpu_custom_call" | custom-call | tf_op jit(solution)/shard_map/finish/pallas_call | solution.py:605
Async XLA Ops:
  0.6 39.4 %copy-start.2 = (f32[64,256]{1,0:T(8,128)S(1)}, f32[64,256]{1,0:T(8,128)}, u32[]{:S(2)}) copy-start(f32[64,256]{1,0:T(8,128)} %second.1) | copy-start | bytes 196612
  0.6 39.4 %copy-start.1 = (f32[64,256]{1,0:T(8,128)S(1)}, f32[64,256]{1,0:T(8,128)}, u32[]{:S(2)}) copy-start(f32[64,256]{1,0:T(8,128)} %first.1) | copy-start | bytes 196612
  0.7 39.4 %copy-start = (f32[64,256]{1,0:T(8,128)S(1)}, f32[64,256]{1,0:T(8,128)}, u32[]{:S(2)}) copy-start(f32[64,256]{1,0:T(8,128)} %master.1) | copy-start | bytes 196612

commit v12 on v11

--- a/solution.py
+++ b/solution.py
@@ -139,48 +139,44 @@
         ((1,), pl.ds(0, 48)),
         ((pl.ds(0, 2),), pl.ds(48, 16)),
     )
-    pieces = (
-        (((0,), pl.ds(0, 16)), ((0,), pl.ds(16, 16)), ((0,), pl.ds(32, 16))),
-        (((1,), pl.ds(0, 16)), ((1,), pl.ds(16, 16)), ((1,), pl.ds(32, 16))),
-        (((0,), pl.ds(48, 16)), ((1,), pl.ds(48, 16))),
-    )
-
-    def streams(stage):
-        return range(2 if stage == 4 else 3)
-
-    def region(s, stage, place):
-        cols, span = parts[s] if stage < 2 else pieces[s][stage - 2]
+
+    def region(s, stage, place, half=None):
+        cols, span = parts[s]
         taken = ORDERS[s][: min(stage, 2)]
-        index = tuple(pl.ds(0, 4) if axis in taken else place[axis] for axis in "xzy")
+        index = [pl.ds(0, 4) if axis in taken else place[axis] for axis in "xzy"]
+        if half is not None:
+            index["xzy".index(taken[0])] = pl.ds(2 * half, 2)
         return weights.at[(*index, c, *cols, span)]
 
     def stage_bytes(stage, sends, recvs):
-        three_of = (
+        same = (
             weights.at[0, 0, pl.ds(0, 3), c],
             weights.at[0, pl.ds(0, 3), :, c],
-            weights.at[pl.ds(0, 3), :, :, c, 0, pl.ds(0, 48)],
-            weights.at[pl.ds(0, 3), :, :, c, 0, pl.ds(0, 48)],
-            weights.at[pl.ds(0, 3), :, :, c, 0, pl.ds(0, 32)],
-        )
-        return bytes_of(three_of[stage], sends.at[stage], recvs.at[stage])
+            weights.at[pl.ds(0, 2), :, :, c],
+            weights.at[0, :, :, c],
+        )
+        return bytes_of(same[stage], sends.at[stage], recvs.at[stage])
 
     def spread(stage):
-        for s in streams(stage):
-            order = ORDERS[s]
-            block = region(s, stage, at)
-            for k in (1, 2, 3):
+        for s, order in enumerate(ORDERS):
+            axis = order[min(stage, 2)]
+            for k in (1, 2, 3) if stage < 2 else (1, 3):
+                if stage < 3:
+                    block = region(s, stage, at)
+                else:
+                    origin = {**at, axis: (at[axis] + 4 - k) % 4}
+                    block = region(s, stage, origin, k // 2)
                 copy(
-                    block, block, w_send.at[stage], w_recv.at[stage],
-                    along(order[min(stage, 2)], k),
+                    block, block, w_send.at[stage], w_recv.at[stage], along(axis, k)
                 ).start()
 
     def arrive(stage):
         stage_bytes(stage, w_send, w_recv).wait_recv()
 
     def forward(stage):
-        for s in streams(stage):
-            axis = ORDERS[s][min(stage, 2)]
-            for k in (1, 2, 3):
+        for s, order in enumerate(ORDERS):
+            axis = order[min(stage, 2)]
+            for k in ((1, 2, 3), (1, 2, 3), (1, 3), (2,))[stage]:
                 block = region(s, stage, {**at, axis: (at[axis] + k) % 4})
                 copy(block, block, f_send, f_recv, sibling).start()
 
@@ -322,18 +318,17 @@
     def place(a):
         order = STATE_ORDERS[a]
         bytes_of(state[a].at[pl.ds(0, 3)], s_send.at[a], s_recv.at[a]).wait_recv()
+        shifts = {"x": 8, "z": 6, "y": 4}
         units = {"x": 16, "z": 4, "y": 1}
-        spot = iota((16 * UNIT, GROUP), 0)
-        target = (
-            (spot // 64) * (units[order[1]] * UNIT)
-            + (spot // 16) % 4 * (units[order[2]] * UNIT)
-            + spot % 16
-            + at[order[0]] * (units[order[0]] * UNIT)
-        ).astype(F32)
         hits = []
         for k in range(4):
             source = chip + (k - at[order[0]]) * units[order[0]]
-            hits.append(onehot(rooted[pl.ds(source, 1), :] == target))
+            ranks = rooted[pl.ds(source, 1), :].astype(jnp.int32)
+            first, second, third = ((ranks >> shifts[axis]) & 3 for axis in order)
+            here = (ranks >= 0) & (first == at[order[0]])
+            spot = second * (4 * UNIT) + third * UNIT + (ranks & (UNIT - 1))
+            row = jnp.where(here, spot, -1).astype(F32)
+            hits.append(ladder(row, 16 * UNIT))
         hits = jnp.concatenate(hits, axis=1)
         whole = state[a][...].reshape(4 * GROUP, 128)
         if a:
@@ -415,7 +410,6 @@
 
     arrive(1)
     spread(2)
-    spread(3)
     forward(1)
 
     for k in range(keep_n // GROUP):
@@ -441,10 +435,9 @@
         return copy(block, block, half_send, half_recv, sibling)
 
     each(lambda k: gather(k).start())
-    spread(4)
-    for stage in (2, 3):
-        arrive(stage)
-        forward(stage)
+    arrive(2)
+    spread(3)
+    forward(2)
     lax.fori_loop(0, chunks, settle, 0)
 
     for k in (3, 2, 1):
@@ -455,8 +448,8 @@
     bytes_of(result.at[c, pl.ds(0, plane - 1)], ag_send, ag_recv.at[x]).wait_recv()
     pass_on(x).start()
 
-    arrive(4)
-    forward(4)
+    arrive(3)
+    forward(3)
 
     scattered.wait_send()
     bytes_of(result.at[c, pl.ds(0, chips - 1)], ag_send, ag_recv.at[x]).wait_send()
@@ -468,7 +461,7 @@
         bytes_of(state[a].at[pl.ds(0, 3)], s_send.at[a], s_recv.at[a]).wait_send()
         state_bytes(1, sgot2, a).wait_send()
         state_bytes(2, sgot3, a).wait_send()
-    for stage in range(5):
+    for stage in range(4):
         stage_bytes(stage, w_send, w_recv).wait_send()
     bytes_of(weights.at[:, :, :, c], f_send, f_recv).wait()
     bytes_of(result.at[c], half_send, half_recv).wait()
@@ -593,7 +586,7 @@
             dma((2,)), dma((2,)), dma, dma, dma((2,)), dma((2,)),
             dma, dma, dma, dma((4,)), dma, dma,
             dma((9,)), dma((9,)),
-            dma((5,)), dma((5,)), dma, dma,
+            dma((4,)), dma((4,)), dma, dma,
             pltpu.SemaphoreType.REGULAR, pltpu.SemaphoreType.REGULAR,
         ],
         compiler_params=pltpu.CompilerParams(

time: 45.9 us -> 45.6 us (level)
  no operation moved by 1% of the time
where the time goes in v12:
time: 45.6 us; the launch traced here: 45.5 us
  Pallas kernels  44.8 us (98%)
  between operations  0.69 us (2%)
    pallas_call x1, Pallas kernels, body(): pl.pallas_call(merge_kernel, out_shape=(pltpu.VMEM((1, rows, width), F32)...  39.1 us
    pallas_call x1, Pallas kernels, body(): pl.pallas_call(finish_kernel, out_shape=(jax.ShapeDtypeStruct((1, rows, w...  5.74 us

profile of v12, /device:TPU:1, one launch (start us, length us, event | category | flops | bytes accessed | tf_op | source)
XLA Modules:
  0.0 45.5 jit_solution(2879169427853520132)
XLA Ops:
  0.6 0.0 copy-start.2
  0.6 0.0 copy-start.1
  0.7 0.0 copy-start
  0.7 39.1 %merge.1 = (f32[1,8192,256]{2,1,0:T(8,128)S(1)}, bf16[4,4,4,2,2,64,128]{6,5,4,3,2,1,0:T(8,128)(2,1)S(1)}, bf16[2,64,2,16,128]{4,3,2,1,0:T(8,128)(2,1)S(1)}, bf16...) custom-call(bf16[1,8192,256]{2,1,0:T(8,128)(2,1)} %grad_hbm.1, f32[1,8192,256]{2,1,0:T(8,128)} %err_hbm.1, ...), custom_call_target="tpu_custom_call" | custom-call | tf_op jit(solution)/shard_map/merge/pallas_call | solution.py:551
  39.7 0.0 copy-done.2
  39.8 0.0 copy-done.1
  39.8 0.0 copy-done
  39.8 5.7 %finish.1 = (f32[1,8192,256]{2,1,0:T(8,128)}, bf16[64,128,256]{2,1,0:T(8,128)(2,1)}, f32[64,256]{1,0:T(8,128)}, f32[64,256]{1,0:T(8,128)}, f32[64,256]{1,0:T(8,128)}) custom-call(f32[1,8192,256]{2,1,0:T(8,128)S(1)} %get-tuple-element.16.err, bf16[64,2,2,64,128]{4,3,2,1,0:T(8,128)(2,1)S(1)} %bitcast.2, ...), custom_call_target="tpu_custom_call" | custom-call | tf_op jit(solution)/shard_map/finish/pallas_call | solution.py:598
Async XLA Ops:
  0.6 39.1 %copy-start.2 = (f32[64,256]{1,0:T(8,128)S(1)}, f32[64,256]{1,0:T(8,128)}, u32[]{:S(2)}) copy-start(f32[64,256]{1,0:T(8,128)} %second.1) | copy-start | bytes 196612
  0.6 39.1 %copy-start.1 = (f32[64,256]{1,0:T(8,128)S(1)}, f32[64,256]{1,0:T(8,128)}, u32[]{:S(2)}) copy-start(f32[64,256]{1,0:T(8,128)} %first.1) | copy-start | bytes 196612
  0.7 39.1 %copy-start = (f32[64,256]{1,0:T(8,128)S(1)}, f32[64,256]{1,0:T(8,128)}, u32[]{:S(2)}) copy-start(f32[64,256]{1,0:T(8,128)} %master.1) | copy-start | bytes 196612

commit v13 on v12

--- a/solution.py
+++ b/solution.py
@@ -18,7 +18,7 @@
 SPAN = 256
 
 ORDERS = ("xzy", "zyx", "yxz")
-STATE_ORDERS = ("zyx", "xzy", "yxz")
+STATE_ORDERS = ("zyx", "xzy")
 
 
 def iota(shape, dim):
@@ -91,15 +91,12 @@
     def bytes_of(ref, send, recv):
         return copy(ref, ref, send, recv, sibling)
 
-    def three(master_ref, moments_ref):
-        return master_ref, moments_ref.at[0], moments_ref.at[1]
-
-    state = three(master0, moment0)
-    state1 = three(master1, moment1)
-    state2 = three(master2, moment2)
-    state3 = three(master3, moment3)
-    sgot2 = three(mgot2, vgot2)
-    sgot3 = three(mgot3, vgot3)
+    state = master0, moment0
+    state1 = master1, moment1
+    state2 = master2, moment2
+    state3 = master3, moment3
+    sgot2 = mgot2, vgot2
+    sgot3 = mgot3, vgot3
 
     def greet(semaphore, peers):
         for peer in peers:
@@ -228,11 +225,11 @@
     own_rows = pl.ds(pl.multiple_of(c * 64, 64), 64)
     half = column[own_rows, :]
     pltpu.make_async_copy(raw, raw, raw_sem).wait()
-    raw_b[...] = raw[:, 1:].astype(BF16)
+    for a in range(2):
+        raw_b[:, :, a * 128 : (a + 1) * 128] = raw[:, 1 + a].astype(BF16)
     mine_at = [at[order[0]] for order in STATE_ORDERS]
     master0[mine_at[0], own_rows, :] = raw[c, 0]
-    for a in (1, 2):
-        moment0[a - 1, mine_at[a], own_rows, :] = raw_b[c, a - 1]
+    moment0[mine_at[1], own_rows, :] = raw_b[c]
 
     for h in range(2):
         new_master, _, _ = adamw(raw[h, 0], raw[h, 1], raw[h, 2], 0.0)
@@ -271,7 +268,6 @@
             err[0, span, :] = (grad[span, :].astype(F32) + err[0, span, :]) * mask
         return 0
 
-    pack(0)
     pl.semaphore_wait(barrier, 10)
     greet(round_z, line["z"])
 
@@ -279,23 +275,16 @@
         copy(
             raw.at[1 - c, 0], state[0].at[mine_at[0], own_rows],
             raw_send, raw_recv, sibling,
-        )
+        ),
+        copy(
+            raw_b.at[1 - c], state[1].at[mine_at[1], own_rows],
+            rawb_send, rawb_recv, sibling,
+        ),
     ]
-    for a in (1, 2):
-        raw_swaps.append(
-            copy(
-                raw_b.at[1 - c, a - 1], state[a].at[mine_at[a], own_rows],
-                rawb_send.at[a - 1], rawb_recv.at[a - 1], sibling,
-            )
-        )
     for go in raw_swaps:
         go.start()
 
-    spread(0)
-    mine = weights.at[x, z, y, c]
-    copy(mine, mine, f_send, f_recv, sibling).start()
-
-    pack(1)
+    pack(0)
 
     for go in raw_swaps:
         go.wait_recv()
@@ -308,11 +297,12 @@
 
     pl.semaphore_wait(round_z, 3)
     greet(round_x, line["x"])
+    spread(0)
+    mine = weights.at[x, z, y, c]
+    copy(mine, mine, f_send, f_recv, sibling).start()
+
+    pack(1)
     pack(2)
-
-    arrive(0)
-    spread(1)
-    forward(0)
     pack(3)
 
     def place(a):
@@ -330,7 +320,7 @@
             row = jnp.where(here, spot, -1).astype(F32)
             hits.append(ladder(row, 16 * UNIT))
         hits = jnp.concatenate(hits, axis=1)
-        whole = state[a][...].reshape(4 * GROUP, 128)
+        whole = state[a][...].reshape(4 * GROUP, -1)
         if a:
             split = whole
         else:
@@ -347,7 +337,7 @@
     def state_phase(phase, source, target):
         for a, order in enumerate(STATE_ORDERS):
             axis = order[phase]
-            n = phase * 3 + a
+            n = phase * 2 + a
             for k in (1, 2, 3):
                 copy(
                     source[a].at[(at[axis] + k) % 4], target[a].at[k - 1],
@@ -355,11 +345,11 @@
                 ).start()
 
     def state_bytes(phase, target, a):
-        n = phase * 3 + a
+        n = phase * 2 + a
         return bytes_of(target[a], s_send.at[n], s_recv.at[n])
 
     def state_sum(phase, source, target, total):
-        for a in range(3):
+        for a in range(2):
             state_bytes(phase, target, a).wait_recv()
         for a, order in enumerate(STATE_ORDERS):
             value = source[a][at[order[phase]]].astype(F32)
@@ -385,7 +375,9 @@
         swap.start()
         swaps.append(swap)
 
-    for a in range(3):
+    arrive(0)
+    spread(1)
+    for a in range(2):
         place(a)
     state_phase(1, state1, sgot2)
     pl.semaphore_wait(round_x, 3)
@@ -404,6 +396,7 @@
 
     each(lambda k: scatter(k).start())
     own = packed[c, chip].astype(F32) + from_core[chip].astype(F32)
+    forward(0)
 
     state_sum(1, state1, sgot2, state2)
     state_phase(2, state2, sgot3)
@@ -420,7 +413,10 @@
     scattered = bytes_of(got, rs_send, rs_recv)
     scattered.wait_recv()
     summed = (own + jnp.sum(got[...].astype(F32), axis=0)).astype(BF16)
-    new_master, _, _ = adamw(*(ref[...].astype(F32) for ref in state3), summed.astype(F32))
+    new_master, _, _ = adamw(
+        master3[...], moment3[:, :128].astype(F32), moment3[:, 128:].astype(F32),
+        summed.astype(F32),
+    )
     result[c, chip, 0] = summed
     result[c, chip, 1] = new_master.astype(BF16)
 
@@ -457,7 +453,7 @@
         go.wait_send()
     for go in swaps:
         go.wait_send()
-    for a in range(3):
+    for a in range(2):
         bytes_of(state[a].at[pl.ds(0, 3)], s_send.at[a], s_recv.at[a]).wait_send()
         state_bytes(1, sgot2, a).wait_send()
         state_bytes(2, sgot3, a).wait_send()
@@ -564,7 +560,7 @@
             pltpu.VMEM((rows, width), BF16),
             pltpu.VMEM((levels, keep_n), jnp.int32),
             pltpu.VMEM((2, 3, owned, 128), F32),
-            pltpu.VMEM((2, 2, owned, 128), BF16),
+            pltpu.VMEM((2, owned, 256), BF16),
             pltpu.VMEM((keep_n, width), F32),
             pltpu.VMEM((groups, GROUP), F32),
             pltpu.VMEM((groups, GROUP), F32),
@@ -575,17 +571,17 @@
             pltpu.VMEM((groups, UNIT, 128), BF16),
             pltpu.VMEM((groups - 1, UNIT, 128), BF16),
             *(
-                pltpu.VMEM((*lead, *shape, 128), kind)
-                for lead, kind in (((), F32), ((2,), BF16))
+                pltpu.VMEM((*shape, lanes), kind)
+                for lanes, kind in ((128, F32), (256, BF16))
                 for shape in (
                     (4, GROUP), (4, 4, UNIT), (4, UNIT), (UNIT,),
                     (3, 4, UNIT), (3, UNIT),
                 )
             ),
             dma((chunks,)), dma((chunks,)), dma, dma,
-            dma((2,)), dma((2,)), dma, dma, dma((2,)), dma((2,)),
+            dma((2,)), dma((2,)), dma, dma, dma, dma,
             dma, dma, dma, dma((4,)), dma, dma,
-            dma((9,)), dma((9,)),
+            dma((6,)), dma((6,)),
             dma((4,)), dma((4,)), dma, dma,
             pltpu.SemaphoreType.REGULAR, pltpu.SemaphoreType.REGULAR,
         ],

time: 45.6 us -> 48.3 us (1.059)
  Pallas kernels: 44.8 us -> 47.5 us
    pallas_call x1, Pallas kernels: 39.1 us -> 41.7 us  [body(): pl.pallas_call(merge_kernel, out_shape=(pltpu.VMEM((1, rows, width), F32)...]
where the time goes in v13:
time: 48.3 us; the launch traced here: 48.2 us
  Pallas kernels  47.5 us (98%)
  between operations  0.69 us (1%)
    pallas_call x1, Pallas kernels, body(): pl.pallas_call(merge_kernel, out_shape=(pltpu.VMEM((1, rows, width), F32)...  41.7 us
    pallas_call x1, Pallas kernels, body(): pl.pallas_call(finish_kernel, out_shape=(jax.ShapeDtypeStruct((1, rows, w...  5.72 us

profile of v13, /device:TPU:1, one launch (start us, length us, event | category | flops | bytes accessed | tf_op | source)
XLA Modules:
  0.0 48.2 jit_solution(2554634375608244581)
XLA Ops:
  0.6 0.0 copy-start.2
  0.6 0.0 copy-start.1
  0.7 0.0 copy-start
  0.7 41.7 %merge.1 = (f32[1,8192,256]{2,1,0:T(8,128)S(1)}, bf16[4,4,4,2,2,64,128]{6,5,4,3,2,1,0:T(8,128)(2,1)S(1)}, bf16[2,64,2,16,128]{4,3,2,1,0:T(8,128)(2,1)S(1)}, bf16...) custom-call(bf16[1,8192,256]{2,1,0:T(8,128)(2,1)} %grad_hbm.1, f32[1,8192,256]{2,1,0:T(8,128)} %err_hbm.1, ...), custom_call_target="tpu_custom_call" | custom-call | tf_op jit(solution)/shard_map/merge/pallas_call | solution.py:547
  42.4 0.0 copy-done.2
  42.4 0.0 copy-done.1
  42.4 0.0 copy-done
  42.4 5.7 %finish.1 = (f32[1,8192,256]{2,1,0:T(8,128)}, bf16[64,128,256]{2,1,0:T(8,128)(2,1)}, f32[64,256]{1,0:T(8,128)}, f32[64,256]{1,0:T(8,128)}, f32[64,256]{1,0:T(8,128)}) custom-call(f32[1,8192,256]{2,1,0:T(8,128)S(1)} %get-tuple-element.16.err, bf16[64,2,2,64,128]{4,3,2,1,0:T(8,128)(2,1)S(1)} %bitcast.2, ...), custom_call_target="tpu_custom_call" | custom-call | tf_op jit(solution)/shard_map/finish/pallas_call | solution.py:594
Async XLA Ops:
  0.6 41.8 %copy-start.2 = (f32[64,256]{1,0:T(8,128)S(1)}, f32[64,256]{1,0:T(8,128)}, u32[]{:S(2)}) copy-start(f32[64,256]{1,0:T(8,128)} %second.1) | copy-start | bytes 196612
  0.6 41.8 %copy-start.1 = (f32[64,256]{1,0:T(8,128)S(1)}, f32[64,256]{1,0:T(8,128)}, u32[]{:S(2)}) copy-start(f32[64,256]{1,0:T(8,128)} %first.1) | copy-start | bytes 196612
  0.7 41.8 %copy-start = (f32[64,256]{1,0:T(8,128)S(1)}, f32[64,256]{1,0:T(8,128)}, u32[]{:S(2)}) copy-start(f32[64,256]{1,0:T(8,128)} %master.1) | copy-start | bytes 196612

commit v14 on v13

--- a/solution.py
+++ b/solution.py
@@ -284,6 +284,10 @@
     for go in raw_swaps:
         go.start()
 
+    spread(0)
+    mine = weights.at[x, z, y, c]
+    copy(mine, mine, f_send, f_recv, sibling).start()
+
     pack(0)
 
     for go in raw_swaps:
@@ -297,12 +301,11 @@
 
     pl.semaphore_wait(round_z, 3)
     greet(round_x, line["x"])
-    spread(0)
-    mine = weights.at[x, z, y, c]
-    copy(mine, mine, f_send, f_recv, sibling).start()
-
     pack(1)
     pack(2)
+
+    arrive(0)
+    spread(1)
     pack(3)
 
     def place(a):
@@ -375,8 +378,6 @@
         swap.start()
         swaps.append(swap)
 
-    arrive(0)
-    spread(1)
     for a in range(2):
         place(a)
     state_phase(1, state1, sgot2)

time: 48.3 us -> 45.1 us (0.934)
  Pallas kernels: 47.5 us -> 44.3 us
    pallas_call x1, Pallas kernels: 41.7 us -> 38.5 us  [body(): pl.pallas_call(merge_kernel, out_shape=(pltpu.VMEM((1, rows, width), F32)...]
where the time goes in v14:
time: 45.1 us; the launch traced here: 45 us
  Pallas kernels  44.3 us (98%)
  between operations  0.69 us (2%)
    pallas_call x1, Pallas kernels, body(): pl.pallas_call(merge_kernel, out_shape=(pltpu.VMEM((1, rows, width), F32)...  38.5 us
    pallas_call x1, Pallas kernels, body(): pl.pallas_call(finish_kernel, out_shape=(jax.ShapeDtypeStruct((1, rows, w...  5.74 us

profile of v14, /device:TPU:1, one launch (start us, length us, event | category | flops | bytes accessed | tf_op | source)
XLA Modules:
  0.0 45.0 jit_solution(9779866512143177612)
XLA Ops:
  0.6 0.0 copy-start.2
  0.6 0.0 copy-start.1
  0.7 0.0 copy-start
  0.7 38.5 %merge.1 = (f32[1,8192,256]{2,1,0:T(8,128)S(1)}, bf16[4,4,4,2,2,64,128]{6,5,4,3,2,1,0:T(8,128)(2,1)S(1)}, bf16[2,64,2,16,128]{4,3,2,1,0:T(8,128)(2,1)S(1)}, bf16...) custom-call(bf16[1,8192,256]{2,1,0:T(8,128)(2,1)} %grad_hbm.1, f32[1,8192,256]{2,1,0:T(8,128)} %err_hbm.1, ...), custom_call_target="tpu_custom_call" | custom-call | tf_op jit(solution)/shard_map/merge/pallas_call | solution.py:548
  39.2 0.0 copy-done.2
  39.2 0.0 copy-done.1
  39.2 0.0 copy-done
  39.2 5.7 %finish.1 = (f32[1,8192,256]{2,1,0:T(8,128)}, bf16[64,128,256]{2,1,0:T(8,128)(2,1)}, f32[64,256]{1,0:T(8,128)}, f32[64,256]{1,0:T(8,128)}, f32[64,256]{1,0:T(8,128)}) custom-call(f32[1,8192,256]{2,1,0:T(8,128)S(1)} %get-tuple-element.16.err, bf16[64,2,2,64,128]{4,3,2,1,0:T(8,128)(2,1)S(1)} %bitcast.2, ...), custom_call_target="tpu_custom_call" | custom-call | tf_op jit(solution)/shard_map/finish/pallas_call | solution.py:595
Async XLA Ops:
  0.6 38.6 %copy-start.2 = (f32[64,256]{1,0:T(8,128)S(1)}, f32[64,256]{1,0:T(8,128)}, u32[]{:S(2)}) copy-start(f32[64,256]{1,0:T(8,128)} %second.1) | copy-start | bytes 196612
  0.6 38.6 %copy-start.1 = (f32[64,256]{1,0:T(8,128)S(1)}, f32[64,256]{1,0:T(8,128)}, u32[]{:S(2)}) copy-start(f32[64,256]{1,0:T(8,128)} %first.1) | copy-start | bytes 196612
  0.7 38.6 %copy-start = (f32[64,256]{1,0:T(8,128)S(1)}, f32[64,256]{1,0:T(8,128)}, u32[]{:S(2)}) copy-start(f32[64,256]{1,0:T(8,128)} %master.1) | copy-start | bytes 196612

commit v15 on v14

--- a/solution.py
+++ b/solution.py
@@ -68,8 +68,11 @@
     strides = {"x": 32, "z": 8, "y": 2}
 
     def far(k):
-        other = (chip + k) % chips
+        other = (x + k // 16) % 4 * 16 + (z + k // 4 % 4) % 4 * 4 + (y + k % 4) % 4
         return other, 2 * other + c
+
+    away = (2, 1, 3, 0)
+    offsets = [16 * i + 4 * j + k for i in away for j in away for k in away][:-1]
 
     def along(axis, k):
         return me + ((at[axis] + k) % 4 - at[axis]) * strides[axis]
@@ -81,12 +84,8 @@
         )
 
     def each(act):
-        def some(i, _):
-            for j in range(21):
-                act(i * 21 + j + 1)
-            return 0
-
-        lax.fori_loop(0, (chips - 1) // 21, some, 0)
+        for k in offsets:
+            act(k)
 
     def bytes_of(ref, send, recv):
         return copy(ref, ref, send, recv, sibling)
@@ -432,10 +431,11 @@
         return copy(block, block, half_send, half_recv, sibling)
 
     each(lambda k: gather(k).start())
+    lax.fori_loop(0, chunks // 2, settle, 0)
     arrive(2)
     spread(3)
     forward(2)
-    lax.fori_loop(0, chunks, settle, 0)
+    lax.fori_loop(chunks // 2, chunks, settle, 0)
 
     for k in (3, 2, 1):
         q = (x + k) % 4

time: 45.1 us -> 45 us (level)
  no operation moved by 1% of the time
where the time goes in v15:
time: 45 us; the launch traced here: 44.9 us
  Pallas kernels  44.2 us (98%)
  between operations  0.69 us (2%)
    pallas_call x1, Pallas kernels, body(): pl.pallas_call(merge_kernel, out_shape=(pltpu.VMEM((1, rows, width), F32)...  38.5 us
    pallas_call x1, Pallas kernels, body(): pl.pallas_call(finish_kernel, out_shape=(jax.ShapeDtypeStruct((1, rows, w...  5.73 us

profile of v15, /device:TPU:1, one launch (start us, length us, event | category | flops | bytes accessed | tf_op | source)
XLA Modules:
  0.0 44.9 jit_solution(345115778739786837)
XLA Ops:
  0.6 0.0 copy-start.2
  0.6 0.0 copy-start.1
  0.7 0.0 copy-start
  0.7 38.5 %merge.1 = (f32[1,8192,256]{2,1,0:T(8,128)S(1)}, bf16[4,4,4,2,2,64,128]{6,5,4,3,2,1,0:T(8,128)(2,1)S(1)}, bf16[2,64,2,16,128]{4,3,2,1,0:T(8,128)(2,1)S(1)}, bf16...) custom-call(bf16[1,8192,256]{2,1,0:T(8,128)(2,1)} %grad_hbm.1, f32[1,8192,256]{2,1,0:T(8,128)} %err_hbm.1, ...), custom_call_target="tpu_custom_call" | custom-call | tf_op jit(solution)/shard_map/merge/pallas_call | solution.py:548
  39.2 0.0 copy-done.2
  39.2 0.0 copy-done.1
  39.2 0.0 copy-done
  39.2 5.7 %finish.1 = (f32[1,8192,256]{2,1,0:T(8,128)}, bf16[64,128,256]{2,1,0:T(8,128)(2,1)}, f32[64,256]{1,0:T(8,128)}, f32[64,256]{1,0:T(8,128)}, f32[64,256]{1,0:T(8,128)}) custom-call(f32[1,8192,256]{2,1,0:T(8,128)S(1)} %get-tuple-element.16.err, bf16[64,2,2,64,128]{4,3,2,1,0:T(8,128)(2,1)S(1)} %bitcast.2, ...), custom_call_target="tpu_custom_call" | custom-call | tf_op jit(solution)/shard_map/finish/pallas_call | solution.py:595
Async XLA Ops:
  0.6 38.5 %copy-start.2 = (f32[64,256]{1,0:T(8,128)S(1)}, f32[64,256]{1,0:T(8,128)}, u32[]{:S(2)}) copy-start(f32[64,256]{1,0:T(8,128)} %second.1) | copy-start | bytes 196612
  0.6 38.5 %copy-start.1 = (f32[64,256]{1,0:T(8,128)S(1)}, f32[64,256]{1,0:T(8,128)}, u32[]{:S(2)}) copy-start(f32[64,256]{1,0:T(8,128)} %first.1) | copy-start | bytes 196612
  0.7 38.5 %copy-start = (f32[64,256]{1,0:T(8,128)S(1)}, f32[64,256]{1,0:T(8,128)}, u32[]{:S(2)}) copy-start(f32[64,256]{1,0:T(8,128)} %master.1) | copy-start | bytes 196612

commit v16 on v15

--- a/solution.py
+++ b/solution.py
@@ -437,7 +437,7 @@
     forward(2)
     lax.fori_loop(chunks // 2, chunks, settle, 0)
 
-    for k in (3, 2, 1):
+    for k in (2, 3, 1):
         q = (x + k) % 4
         block = result.at[c, pl.ds(q * plane, plane)]
         bytes_of(block, ag_send, ag_recv.at[q]).wait_recv()

time: 45 us -> 45.1 us (level)
  no operation moved by 1% of the time
where the time goes in v16:
time: 45.1 us; the launch traced here: 44.9 us
  Pallas kernels  44.2 us (98%)
  between operations  0.69 us (2%)
    pallas_call x1, Pallas kernels, body(): pl.pallas_call(merge_kernel, out_shape=(pltpu.VMEM((1, rows, width), F32)...  38.5 us
    pallas_call x1, Pallas kernels, body(): pl.pallas_call(finish_kernel, out_shape=(jax.ShapeDtypeStruct((1, rows, w...  5.74 us

profile of v16, /device:TPU:1, one launch (start us, length us, event | category | flops | bytes accessed | tf_op | source)
XLA Modules:
  0.0 44.9 jit_solution(6681226137413826428)
XLA Ops:
  0.6 0.0 copy-start.2
  0.6 0.0 copy-start.1
  0.7 0.0 copy-start
  0.7 38.5 %merge.1 = (f32[1,8192,256]{2,1,0:T(8,128)S(1)}, bf16[4,4,4,2,2,64,128]{6,5,4,3,2,1,0:T(8,128)(2,1)S(1)}, bf16[2,64,2,16,128]{4,3,2,1,0:T(8,128)(2,1)S(1)}, bf16...) custom-call(bf16[1,8192,256]{2,1,0:T(8,128)(2,1)} %grad_hbm.1, f32[1,8192,256]{2,1,0:T(8,128)} %err_hbm.1, ...), custom_call_target="tpu_custom_call" | custom-call | tf_op jit(solution)/shard_map/merge/pallas_call | solution.py:548
  39.2 0.0 copy-done.2
  39.2 0.0 copy-done.1
  39.2 0.0 copy-done
  39.2 5.7 %finish.1 = (f32[1,8192,256]{2,1,0:T(8,128)}, bf16[64,128,256]{2,1,0:T(8,128)(2,1)}, f32[64,256]{1,0:T(8,128)}, f32[64,256]{1,0:T(8,128)}, f32[64,256]{1,0:T(8,128)}) custom-call(f32[1,8192,256]{2,1,0:T(8,128)S(1)} %get-tuple-element.16.err, bf16[64,2,2,64,128]{4,3,2,1,0:T(8,128)(2,1)S(1)} %bitcast.2, ...), custom_call_target="tpu_custom_call" | custom-call | tf_op jit(solution)/shard_map/finish/pallas_call | solution.py:595
Async XLA Ops:
  0.6 38.5 %copy-start.2 = (f32[64,256]{1,0:T(8,128)S(1)}, f32[64,256]{1,0:T(8,128)}, u32[]{:S(2)}) copy-start(f32[64,256]{1,0:T(8,128)} %second.1) | copy-start | bytes 196612
  0.6 38.5 %copy-start.1 = (f32[64,256]{1,0:T(8,128)S(1)}, f32[64,256]{1,0:T(8,128)}, u32[]{:S(2)}) copy-start(f32[64,256]{1,0:T(8,128)} %first.1) | copy-start | bytes 196612
  0.7 38.5 %copy-start = (f32[64,256]{1,0:T(8,128)S(1)}, f32[64,256]{1,0:T(8,128)}, u32[]{:S(2)}) copy-start(f32[64,256]{1,0:T(8,128)} %master.1) | copy-start | bytes 196612

commit v17 on v16

--- a/solution.py
+++ b/solution.py
@@ -405,10 +405,6 @@
     spread(2)
     forward(1)
 
-    for k in range(keep_n // GROUP):
-        lanes = (iota((64, GROUP), 1) + k * GROUP).astype(F32)
-        expand[:, k * GROUP : (k + 1) * GROUP] = onehot(half == lanes)
-
     state_sum(2, state2, sgot3, state3)
     scattered = bytes_of(got, rs_send, rs_recv)
     scattered.wait_recv()
@@ -431,6 +427,10 @@
         return copy(block, block, half_send, half_recv, sibling)
 
     each(lambda k: gather(k).start())
+    for k in range(keep_n // GROUP):
+        lanes = (iota((64, GROUP), 1) + k * GROUP).astype(F32)
+        expand[:, k * GROUP : (k + 1) * GROUP] = onehot(half == lanes)
+
     lax.fori_loop(0, chunks // 2, settle, 0)
     arrive(2)
     spread(3)

time: 45.1 us -> 45 us (level)
  no operation moved by 1% of the time
where the time goes in v17:
time: 45 us; the launch traced here: 44.9 us
  Pallas kernels  44.2 us (98%)
  between operations  0.69 us (2%)
    pallas_call x1, Pallas kernels, body(): pl.pallas_call(merge_kernel, out_shape=(pltpu.VMEM((1, rows, width), F32)...  38.5 us
    pallas_call x1, Pallas kernels, body(): pl.pallas_call(finish_kernel, out_shape=(jax.ShapeDtypeStruct((1, rows, w...  5.73 us

profile of v17, /device:TPU:1, one launch (start us, length us, event | category | flops | bytes accessed | tf_op | source)
XLA Modules:
  0.0 44.9 jit_solution(14208476424024050446)
XLA Ops:
  0.6 0.0 copy-start.2
  0.6 0.0 copy-start.1
  0.7 0.0 copy-start
  0.7 38.5 %merge.1 = (f32[1,8192,256]{2,1,0:T(8,128)S(1)}, bf16[4,4,4,2,2,64,128]{6,5,4,3,2,1,0:T(8,128)(2,1)S(1)}, bf16[2,64,2,16,128]{4,3,2,1,0:T(8,128)(2,1)S(1)}, bf16...) custom-call(bf16[1,8192,256]{2,1,0:T(8,128)(2,1)} %grad_hbm.1, f32[1,8192,256]{2,1,0:T(8,128)} %err_hbm.1, ...), custom_call_target="tpu_custom_call" | custom-call | tf_op jit(solution)/shard_map/merge/pallas_call | solution.py:548
  39.2 0.0 copy-done.2
  39.2 0.0 copy-done.1
  39.2 0.0 copy-done
  39.2 5.7 %finish.1 = (f32[1,8192,256]{2,1,0:T(8,128)}, bf16[64,128,256]{2,1,0:T(8,128)(2,1)}, f32[64,256]{1,0:T(8,128)}, f32[64,256]{1,0:T(8,128)}, f32[64,256]{1,0:T(8,128)}) custom-call(f32[1,8192,256]{2,1,0:T(8,128)S(1)} %get-tuple-element.16.err, bf16[64,2,2,64,128]{4,3,2,1,0:T(8,128)(2,1)S(1)} %bitcast.2, ...), custom_call_target="tpu_custom_call" | custom-call | tf_op jit(solution)/shard_map/finish/pallas_call | solution.py:595
Async XLA Ops:
  0.6 38.5 %copy-start.2 = (f32[64,256]{1,0:T(8,128)S(1)}, f32[64,256]{1,0:T(8,128)}, u32[]{:S(2)}) copy-start(f32[64,256]{1,0:T(8,128)} %second.1) | copy-start | bytes 196612
  0.6 38.5 %copy-start.1 = (f32[64,256]{1,0:T(8,128)S(1)}, f32[64,256]{1,0:T(8,128)}, u32[]{:S(2)}) copy-start(f32[64,256]{1,0:T(8,128)} %first.1) | copy-start | bytes 196612
  0.7 38.5 %copy-start = (f32[64,256]{1,0:T(8,128)S(1)}, f32[64,256]{1,0:T(8,128)}, u32[]{:S(2)}) copy-start(f32[64,256]{1,0:T(8,128)} %master.1) | copy-start | bytes 196612
